TPU v7x, 128 devices: a whole 4x4x4 slice. The times are simulated.
128 devices in a mesh: seq: 8 (over x_lo, y), fsdp: 16 (over z, x_hi, core).
Axes of the slice: x: 4 (x_hi: 2, x_lo: 2; x = x_hi * 2 + x_lo), y: 4, z: 4, core: 2. Of those that a mesh axis runs over, the one named last changes fastest.
Arguments:
- tokens: bfloat16 [16, 2048, 1024], P('fsdp', 'seq'), may hold values from -6 to 6
- attn_gain: bfloat16 [1024], P(('seq', 'fsdp')), may hold values from 0.25 to 1.75
- qkv_weight: bfloat16 [1024, 2048], P(('seq', 'fsdp')), may hold values from -0.1875 to 0.1875
- qk_gain: bfloat16 [128], P(('seq', 'fsdp')), may hold values from 0.25 to 1.75
- out_weight: bfloat16 [1024, 1024], P(('seq', 'fsdp')), may hold values from -6 to 6
- ffn_gain: bfloat16 [1024], P(('seq', 'fsdp')), may hold values from 0.25 to 1.75
- router_weight: bfloat16 [1024, 32], P(('seq', 'fsdp')), may hold values from -0.09375 to 0.09375
- gate_up_weight: bfloat16 [32, 1024, 1024], P('fsdp'), may hold values from -0.1875 to 0.1875
- down_weight: bfloat16 [32, 1024, 512], P('fsdp'), may hold values from -1.5 to 1.5
- routes: int32 [16, 2048, 8], P('fsdp', 'seq'), may hold values from 0 to 31, all different within a row; in each aligned block of 256 rows (0 to 255, 256 to 511, ..., all dimensions but the last counted through in order) at most 88 rows name the same one
- cotangent: bfloat16 [16, 2048, 1024], P('fsdp', 'seq'), may hold values from -6 to 6
Outputs:
- layer_out: bfloat16 [16, 2048, 1024], P('fsdp', 'seq')
- token_grad: float32 [16, 2048, 1024], P('fsdp', 'seq')
- attn_gain_grad: float32 [1024], P(('seq', 'fsdp'))
- qkv_weight_grad: float32 [1024, 2048], P(('seq', 'fsdp'))
- qk_gain_grad: float32 [128], P(('seq', 'fsdp'))
- out_weight_grad: float32 [1024, 1024], P(('seq', 'fsdp'))
- ffn_gain_grad: float32 [1024], P(('seq', 'fsdp'))
- router_grad: float32 [1024, 32], P(('seq', 'fsdp'))
- gate_up_grad: float32 [32, 1024, 1024], P('fsdp', 'seq')
- down_grad: float32 [32, 1024, 512], P('fsdp', 'seq')
Inputs may be any that keep to these rules, and one draw needn't show every extreme that they name: `routes`: each row names 8 different experts; among the rows of one device no expert is named by more than 88 rows, a bound that some block reaches.
All inputs are finite; a program needn't handle non-finite values.
Results may differ from a plain program's by a relative error of at most 0.035.
Values may be sent and summed in bfloat16 or wider, within the bound.
A program may use at most 192 MiB of HBM per device.

v0:
```python
import math

import jax
import jax.numpy as jnp
from jax import lax
from jax.sharding import PartitionSpec as P

D = 1024
QUERY_HEADS = 16
KEY_VALUE_HEADS = 8
HEAD_SIZE = 64
F = 512
TOPK = 8


epsilon = 1e-06
rope_base = 10000.0


def rms_forward(values, weights):
    scaling = lax.rsqrt(jnp.mean(values * values, axis=-1, keepdims=True) + epsilon)
    return (values * scaling * weights, scaling)


def rms_backward(values, scaling, weights, incoming):
    weighted = incoming * weights
    scaling_cube = scaling * scaling * scaling
    result = scaling * weighted - values * scaling_cube * jnp.mean(
        weighted * values, axis=-1, keepdims=True
    )
    return (result, incoming * values * scaling)


def silu_slope(values):
    sigmoid = jax.nn.sigmoid(values)
    return sigmoid * (1.0 + values * (1.0 - sigmoid))


def rotary_tables(positions, head_dim):
    half_dim = head_dim // 2
    freq_index = jnp.arange(half_dim, dtype=jnp.float32)
    inverse = jnp.exp(-(2.0 * freq_index / head_dim) * math.log(rope_base))
    angles = positions.astype(jnp.float32)[:, None] * inverse[None, :]
    return (jnp.cos(angles)[:, None, :], jnp.sin(angles)[:, None, :])


def rotate(values, cosine_values, sine_values):
    half_dim = values.shape[-1] // 2
    first_half = values[..., :half_dim]
    second_half = values[..., half_dim:]
    return jnp.concatenate(
        [
            first_half * cosine_values - second_half * sine_values,
            second_half * cosine_values + first_half * sine_values,
        ],
        axis=-1,
    )


def attend_block(query_block, key_heads, value_heads, head_scale):
    scores = (
        jnp.einsum("bkgd,lkd->kgbl", query_block, key_heads, preferred_element_type=jnp.float32)
        * head_scale
    )
    row_peak = jnp.max(scores, axis=-1, keepdims=True)
    exp_scores = jnp.exp(scores - row_peak)
    row_total = jnp.sum(exp_scores, axis=-1, keepdims=True)
    attn_probs = (exp_scores / row_total).astype(jnp.bfloat16)
    attention_output = jnp.einsum(
        "kgbl,lkd->bkgd", attn_probs, value_heads, preferred_element_type=jnp.float32
    )
    return (attention_output, (row_peak + jnp.log(row_total))[..., 0])


def on_device(
    tokens,
    attn_gain,
    qkv_weight,
    qk_gain,
    out_weight,
    ffn_gain,
    router_weight,
    gate_up_weight,
    down_weight,
    routes,
    cotangent,
):
    device_tokens = tokens.shape[1]
    layer_inputs = tokens.reshape(device_tokens, D).astype(jnp.float32)
    query_total_width = QUERY_HEADS * HEAD_SIZE
    key_total_width = KEY_VALUE_HEADS * HEAD_SIZE
    head_scale = 1.0 / math.sqrt(HEAD_SIZE)
    seq_place = lax.axis_index("seq")
    gathered = (
        lax.all_gather(attn_gain, ("seq", "fsdp"), axis=0, tiled=True),
        lax.all_gather(qkv_weight, ("seq", "fsdp"), axis=0, tiled=True),
        lax.all_gather(qk_gain, ("seq", "fsdp"), axis=0, tiled=True),
        lax.all_gather(out_weight, ("seq", "fsdp"), axis=0, tiled=True),
        lax.all_gather(ffn_gain, ("seq", "fsdp"), axis=0, tiled=True),
        lax.all_gather(router_weight, ("seq", "fsdp"), axis=0, tiled=True),
    )
    full_attn_gain, full_qkv, full_qk_gain, full_out, full_ffn_gain, full_router = gathered
    experts_all = full_router.shape[1]
    cap_rows = device_tokens * TOPK * 11 // (8 * experts_all)
    attn_norm = full_attn_gain.astype(jnp.float32)
    normed_attn, attn_scaling = rms_forward(layer_inputs, attn_norm)
    normed_attn = normed_attn.astype(jnp.bfloat16)
    projected_rows = jnp.dot(normed_attn, full_qkv, preferred_element_type=jnp.float32)
    query_raw = projected_rows[:, :query_total_width].reshape(device_tokens, QUERY_HEADS, HEAD_SIZE)
    unnormed_key = projected_rows[
        :, query_total_width : query_total_width + key_total_width
    ].reshape(device_tokens, KEY_VALUE_HEADS, HEAD_SIZE)
    value_low = projected_rows[:, query_total_width + key_total_width :].astype(jnp.bfloat16)
    qk_norm = full_qk_gain.astype(jnp.float32)
    query_normed, query_scaling = rms_forward(query_raw, qk_norm[:HEAD_SIZE])
    key_normed, key_scaling = rms_forward(unnormed_key, qk_norm[HEAD_SIZE:])
    positions = seq_place * device_tokens + jnp.arange(device_tokens, dtype=jnp.int32)
    cosine_values, sine_values = rotary_tables(positions, HEAD_SIZE)
    query_low = (
        rotate(query_normed, cosine_values, sine_values)
        .reshape(device_tokens, query_total_width)
        .astype(jnp.bfloat16)
    )
    key_low = (
        rotate(key_normed, cosine_values, sine_values)
        .reshape(device_tokens, key_total_width)
        .astype(jnp.bfloat16)
    )
    head_query, head_key, head_value = (
        lax.all_to_all(query_low, "seq", split_axis=1, concat_axis=0, tiled=True),
        lax.all_to_all(key_low, "seq", split_axis=1, concat_axis=0, tiled=True),
        lax.all_to_all(value_low, "seq", split_axis=1, concat_axis=0, tiled=True),
    )
    sequence_length = head_key.shape[0]
    kv_local = head_key.shape[1] // HEAD_SIZE
    group_count = QUERY_HEADS // KEY_VALUE_HEADS
    block_rows = min(512, sequence_length)
    blocks = sequence_length // block_rows
    query_heads = head_query.reshape(blocks, block_rows, kv_local, group_count, HEAD_SIZE)
    key_heads = head_key.reshape(sequence_length, kv_local, HEAD_SIZE)
    value_heads = head_value.reshape(sequence_length, kv_local, HEAD_SIZE)

    def forward_block(query_block):
        return attend_block(query_block, key_heads, value_heads, head_scale)

    attention_output, log_totals = lax.map(forward_block, query_heads)
    attended_low = attention_output.astype(jnp.bfloat16).reshape(
        sequence_length, kv_local * group_count * HEAD_SIZE
    )
    attended_tokens = lax.all_to_all(attended_low, "seq", split_axis=0, concat_axis=1, tiled=True)
    after_attention = layer_inputs + jnp.dot(
        attended_tokens, full_out, preferred_element_type=jnp.float32
    )
    ffn_norm = full_ffn_gain.astype(jnp.float32)
    normed_ffn, ffn_scaling = rms_forward(after_attention, ffn_norm)
    normed_ffn = normed_ffn.astype(jnp.bfloat16)
    logits = jnp.dot(normed_ffn, full_router, preferred_element_type=jnp.float32)
    route_ids = routes.reshape(device_tokens, TOPK)
    expert_ids = jnp.arange(experts_all, dtype=jnp.int32)
    route_hot = (route_ids[:, :, None] == expert_ids).astype(jnp.float32)
    chosen = jnp.sum(route_hot * logits[:, None, :], axis=2)
    chosen_peak = jnp.max(chosen, axis=1, keepdims=True)
    chosen_exp = jnp.exp(chosen - chosen_peak)
    gate_probs = chosen_exp / jnp.sum(chosen_exp, axis=1, keepdims=True)
    pair_count = device_tokens * TOPK
    flat_ids = route_ids.reshape(pair_count)
    pair_hot = (flat_ids[:, None] == expert_ids).astype(jnp.int32)
    running = jnp.cumsum(pair_hot, axis=0)
    slot_index = jnp.sum(pair_hot * (running - 1), axis=1)
    position = flat_ids * cap_rows + slot_index
    slot_table = (
        jnp.full((experts_all * cap_rows,), pair_count, jnp.int32)
        .at[position]
        .set(jnp.arange(pair_count, dtype=jnp.int32))
    )
    token_table = jnp.where(slot_table < pair_count, slot_table // TOPK, device_tokens)
    padded_rows = jnp.concatenate([normed_ffn, jnp.zeros((1, D), jnp.bfloat16)], axis=0)
    send_rows = padded_rows[token_table].reshape(experts_all, cap_rows, D)
    expert_rows = lax.all_to_all(send_rows, "fsdp", split_axis=0, concat_axis=1, tiled=True)
    gate_up_out = jnp.einsum(
        "erd,edf->erf", expert_rows, gate_up_weight, preferred_element_type=jnp.float32
    )
    gate_part = gate_up_out[..., :F]
    up_part = gate_up_out[..., F:]
    silu_gate = jax.nn.silu(gate_part)
    hidden = (silu_gate * up_part).astype(jnp.bfloat16)
    expert_out = jnp.einsum(
        "erf,edf->erd", hidden, down_weight, preferred_element_type=jnp.float32
    ).astype(jnp.bfloat16)
    returned = lax.all_to_all(expert_out, "fsdp", split_axis=1, concat_axis=0, tiled=True)
    pair_out = returned.reshape(experts_all * cap_rows, D)[position].reshape(device_tokens, TOPK, D)
    expert_sum = jnp.sum(gate_probs[:, :, None] * pair_out, axis=1)
    layer_out = (after_attention + expert_sum).astype(jnp.bfloat16).reshape(1, device_tokens, D)
    back_attn_gain, back_qkv, back_qk_gain, back_out, back_ffn_gain, back_router = (
        lax.all_gather(attn_gain, ("seq", "fsdp"), axis=0, tiled=True),
        lax.all_gather(qkv_weight, ("seq", "fsdp"), axis=0, tiled=True),
        lax.all_gather(qk_gain, ("seq", "fsdp"), axis=0, tiled=True),
        lax.all_gather(out_weight, ("seq", "fsdp"), axis=0, tiled=True),
        lax.all_gather(ffn_gain, ("seq", "fsdp"), axis=0, tiled=True),
        lax.all_gather(router_weight, ("seq", "fsdp"), axis=0, tiled=True),
    )
    incoming = cotangent.reshape(device_tokens, D).astype(jnp.float32)
    gate_grad = jnp.sum(pair_out * incoming[:, None, :], axis=2)
    pair_grad = (
        (gate_probs[:, :, None] * incoming[:, None, :]).astype(jnp.bfloat16).reshape(pair_count, D)
    )
    padded_grad = jnp.concatenate([pair_grad, jnp.zeros((1, D), jnp.bfloat16)], axis=0)
    send_grad = padded_grad[slot_table].reshape(experts_all, cap_rows, D)
    expert_grad = lax.all_to_all(send_grad, "fsdp", split_axis=0, concat_axis=1, tiled=True)
    hidden_grad = jnp.einsum(
        "erd,edf->erf", expert_grad, down_weight, preferred_element_type=jnp.float32
    )
    down_grad = jnp.einsum("erd,erf->edf", expert_grad, hidden, preferred_element_type=jnp.float32)
    gate_up_out_grad = jnp.concatenate(
        [hidden_grad * up_part * silu_slope(gate_part), hidden_grad * silu_gate], axis=-1
    ).astype(jnp.bfloat16)
    gate_up_grad = jnp.einsum(
        "erd,erf->edf", expert_rows, gate_up_out_grad, preferred_element_type=jnp.float32
    )
    row_grad = jnp.einsum(
        "erf,edf->erd", gate_up_out_grad, gate_up_weight, preferred_element_type=jnp.float32
    ).astype(jnp.bfloat16)
    row_back = lax.all_to_all(row_grad, "fsdp", split_axis=1, concat_axis=0, tiled=True)
    pair_rows = row_back.reshape(experts_all * cap_rows, D)[position].reshape(
        device_tokens, TOPK, D
    )
    normed_ffn_grad = jnp.sum(pair_rows, axis=1, dtype=jnp.float32)
    chosen_grad = gate_probs * (gate_grad - jnp.sum(gate_probs * gate_grad, axis=1, keepdims=True))
    logits_grad = jnp.sum(route_hot * chosen_grad[:, :, None], axis=1).astype(jnp.bfloat16)
    router_grad = jnp.einsum(
        "td,te->de", normed_ffn, logits_grad, preferred_element_type=jnp.float32
    )
    normed_ffn_grad = normed_ffn_grad + jnp.einsum(
        "te,de->td", logits_grad, back_router, preferred_element_type=jnp.float32
    )
    after_extra, ffn_terms = rms_backward(
        after_attention, ffn_scaling, back_ffn_gain.astype(jnp.float32), normed_ffn_grad
    )
    after_grad = incoming + after_extra
    ffn_gain_grad = jnp.sum(ffn_terms, axis=0)
    after_low = after_grad.astype(jnp.bfloat16)
    out_weight_grad = jnp.einsum(
        "tq,td->qd", attended_tokens, after_low, preferred_element_type=jnp.float32
    )
    attended_grad = jnp.einsum(
        "td,qd->tq", after_low, back_out, preferred_element_type=jnp.float32
    ).astype(jnp.bfloat16)
    grad_heads = lax.all_to_all(attended_grad, "seq", split_axis=1, concat_axis=0, tiled=True)
    grad_blocks = grad_heads.reshape(blocks, block_rows, kv_local, group_count, HEAD_SIZE)

    def backward_block(totals_pair, pieces):
        key_total, value_total = totals_pair
        query_block, grad_block, lse_block = pieces
        scores = (
            jnp.einsum("bkgd,lkd->kgbl", query_block, key_heads, preferred_element_type=jnp.float32)
            * head_scale
        )
        attn_probs = jnp.exp(scores - lse_block[..., None])
        value_total = value_total + jnp.einsum(
            "kgbl,bkgd->lkd",
            attn_probs.astype(jnp.bfloat16),
            grad_block,
            preferred_element_type=jnp.float32,
        )
        prob_grad = jnp.einsum(
            "bkgd,lkd->kgbl", grad_block, value_heads, preferred_element_type=jnp.float32
        )
        score_grad = (
            attn_probs * (prob_grad - jnp.sum(attn_probs * prob_grad, axis=-1, keepdims=True))
        ).astype(jnp.bfloat16)
        query_grad = (
            jnp.einsum("kgbl,lkd->bkgd", score_grad, key_heads, preferred_element_type=jnp.float32)
            * head_scale
        )
        key_total = (
            key_total
            + jnp.einsum(
                "kgbl,bkgd->lkd", score_grad, query_block, preferred_element_type=jnp.float32
            )
            * head_scale
        )
        return ((key_total, value_total), query_grad.astype(jnp.bfloat16))

    zero_heads = jnp.zeros((sequence_length, kv_local, HEAD_SIZE), jnp.float32)
    (key_total, value_total), query_grads = lax.scan(
        backward_block, (zero_heads, zero_heads), (query_heads, grad_blocks, log_totals)
    )
    query_grad_low = query_grads.reshape(sequence_length, kv_local * group_count * HEAD_SIZE)
    key_grad_low = key_total.astype(jnp.bfloat16).reshape(sequence_length, kv_local * HEAD_SIZE)
    value_grad_low = value_total.astype(jnp.bfloat16).reshape(sequence_length, kv_local * HEAD_SIZE)
    token_query_grad, key_token_gradient, token_value_grad = (
        lax.all_to_all(query_grad_low, "seq", split_axis=0, concat_axis=1, tiled=True),
        lax.all_to_all(key_grad_low, "seq", split_axis=0, concat_axis=1, tiled=True),
        lax.all_to_all(value_grad_low, "seq", split_axis=0, concat_axis=1, tiled=True),
    )
    back_qk_norm = back_qk_gain.astype(jnp.float32)
    query_normed_grad = rotate(
        token_query_grad.reshape(device_tokens, QUERY_HEADS, HEAD_SIZE).astype(jnp.float32),
        cosine_values,
        -sine_values,
    )
    key_normed_grad = rotate(
        key_token_gradient.reshape(device_tokens, KEY_VALUE_HEADS, HEAD_SIZE).astype(jnp.float32),
        cosine_values,
        -sine_values,
    )
    query_raw_grad, query_terms = rms_backward(
        query_raw, query_scaling, back_qk_norm[:HEAD_SIZE], query_normed_grad
    )
    key_raw_grad, key_terms = rms_backward(
        unnormed_key, key_scaling, back_qk_norm[HEAD_SIZE:], key_normed_grad
    )
    qk_gain_grad = jnp.concatenate(
        [jnp.sum(query_terms, axis=(0, 1)), jnp.sum(key_terms, axis=(0, 1))], axis=0
    )
    projected_grad = jnp.concatenate(
        [
            query_raw_grad.reshape(device_tokens, query_total_width).astype(jnp.bfloat16),
            key_raw_grad.reshape(device_tokens, key_total_width).astype(jnp.bfloat16),
            token_value_grad,
        ],
        axis=1,
    )
    qkv_weight_grad = jnp.einsum(
        "td,tc->dc", normed_attn, projected_grad, preferred_element_type=jnp.float32
    )
    normed_attn_grad = jnp.einsum(
        "tc,dc->td", projected_grad, back_qkv, preferred_element_type=jnp.float32
    )
    input_extra, attn_terms = rms_backward(
        layer_inputs, attn_scaling, back_attn_gain.astype(jnp.float32), normed_attn_grad
    )
    token_grad = (after_grad + input_extra).reshape(1, device_tokens, D)
    attn_gain_grad = jnp.sum(attn_terms, axis=0)
    attn_part, qkv_part, qk_part, out_part, ffn_part, router_part = (
        lax.psum_scatter(attn_gain_grad, ("seq", "fsdp"), scatter_dimension=0, tiled=True),
        lax.psum_scatter(qkv_weight_grad, ("seq", "fsdp"), scatter_dimension=0, tiled=True),
        lax.psum_scatter(qk_gain_grad, ("seq", "fsdp"), scatter_dimension=0, tiled=True),
        lax.psum_scatter(out_weight_grad, ("seq", "fsdp"), scatter_dimension=0, tiled=True),
        lax.psum_scatter(ffn_gain_grad, ("seq", "fsdp"), scatter_dimension=0, tiled=True),
        lax.psum_scatter(router_grad, ("seq", "fsdp"), scatter_dimension=0, tiled=True),
    )
    gate_up_part, down_part = (
        lax.psum_scatter(
            gate_up_grad.astype(jnp.bfloat16), "seq", scatter_dimension=1, tiled=True
        ).astype(jnp.float32),
        lax.psum_scatter(
            down_grad.astype(jnp.bfloat16), "seq", scatter_dimension=1, tiled=True
        ).astype(jnp.float32),
    )
    return (
        layer_out,
        token_grad,
        attn_part,
        qkv_part,
        qk_part,
        out_part,
        ffn_part,
        router_part,
        gate_up_part,
        down_part,
    )


def solution(mesh):
    return jax.shard_map(
        on_device,
        mesh=mesh,
        in_specs=(
            P("fsdp", "seq", None),
            P(("seq", "fsdp")),
            P(("seq", "fsdp"), None),
            P(("seq", "fsdp")),
            P(("seq", "fsdp"), None),
            P(("seq", "fsdp")),
            P(("seq", "fsdp"), None),
            P("fsdp", None, None),
            P("fsdp", None, None),
            P("fsdp", "seq", None),
            P("fsdp", "seq", None),
        ),
        out_specs=(
            P("fsdp", "seq", None),
            P("fsdp", "seq", None),
            P(("seq", "fsdp")),
            P(("seq", "fsdp"), None),
            P(("seq", "fsdp")),
            P(("seq", "fsdp"), None),
            P(("seq", "fsdp")),
            P(("seq", "fsdp"), None),
            P("fsdp", "seq", None),
            P("fsdp", "seq", None),
        ),
        check_vma=False,
    )
```

profile of v0, /device:TPU:1, one launch (start us, length us, event | category | flops | bytes accessed | tf_op | source)
XLA Modules:
  0.0 2376.0 jit_solution(12739824652027636703)
XLA Ops:
  12.9 68.9 %all-reduce.10 = (bf16[128]{0:T(256)(128)(2,1)S(1)}, bf16[1024]{0:T(1024)(128)(2,1)S(1)}, bf16[1024]{0:T(1024)(128)(2,1)S(1)}) all-reduce(bf16[128]{0:T(256)(128)(2,1)S(1)} %dynamic-update-slice.1, bf16[1024]{0:T(1024)(128)(2,1)S(1)} %dynamic-update-slice, ...), channel_id=1, replica_groups=mesh['seq'=8,'fsdp'=16] {'seq','fsdp'}, use_global_device_ids=true, to_apply=%add.3 | all-reduce | flops 2176 | bytes 8704
  83.7 9.1 reduce-window.6
  94.3 116.5 %all-gather.3.cloned.1.call-done = bf16[1024,2048]{1,0:T(8,128)(2,1)} async-done(((bf16[8,2048]{1,0:T(8,128)(2,1)}), bf16[1024,2048]{1,0:T(8,128)(2,1)}) %all-gather.3.cloned.1.call-update) | async-done | bytes 4194320 | tf_op jit(solution)/shard_map/all_gather | solution.py:96
  210.8 3.7 fusion.82
  219.2 4.1 all-to-all-start.1
  229.5 4.3 all-to-all-start.2
  236.0 4.0 all-to-all-done.2
  239.9 4.1 all-to-all-start
  244.5 8.3 scatter_custom_fusion
  258.9 26.0 %while.27 = (s32[]{:T(128)}, bf16[4,512,1,2,64]{1,4,3,2,0:T(8,128)(2,1)}, f32[4,1,2,512]{3,2,1,0:T(2,128)}, bf16[4,512,1,2,64]{1,4,3,2,0:T(8,128)(2,1)S(1)}, bf1...) while((s32[]{:T(128)}, bf16[4,512,1,2,64]{1,4,3,2,0:T(8,128)(2,1)}, ...), condition=%wide.region_6.7_spmd, body=%wide.region_3.6_spmd.sunk | while | flops 555744256 | bytes 26117200 | solution.py:146
  291.5 5.0 all-to-all-start.3
  296.5 179.9 %all_gather.29 = bf16[1024,32]{1,0:T(8,128)(2,1)S(1)} all-gather(bf16[8,32]{1,0:T(8,128)(2,1)S(1)} %copy-done.61), channel_id=1, replica_groups=mesh['seq'=8,'fsdp'=16] {'seq','fsdp'}, dimensions={0}, use_global_device_ids=true | all-gather | bytes 66048 | tf_op jit(solution)/shard_map/all_gather | solution.py:100
  489.7 15.9 gather_fusion.2
  505.6 4.7 all-to-all-start.6
  510.3 9.7 gather_fusion
  520.0 58.3 %all-to-all-done.6 = bf16[32,88,1024]{2,1,0:T(8,128)(2,1)} async-done(((bf16[32,88,1024]{2,1,0:T(8,128)(2,1)}), bf16[32,88,1024]{2,1,0:T(8,128)(2,1)}, u32[]{:S(2)}, u32[]{:S(2)}) %all-to-all-start.6) | async-done | bytes 5767200 | tf_op jit(solution)/shard_map/all_to_all | solution.py:209
  578.3 5.8 all-to-all-start.4
  584.1 5.9 copy.252
  590.1 61.9 %all-to-all-done.4 = bf16[32,88,1024]{2,1,0:T(8,128)(2,1)} async-done(((bf16[32,88,1024]{2,1,0:T(8,128)(2,1)}), bf16[32,88,1024]{2,1,0:T(8,128)(2,1)}, u32[]{:S(2)}, u32[]{:S(2)}) %all-to-all-start.4) | async-done | bytes 5767200 | tf_op jit(solution)/shard_map/all_to_all | solution.py:179
  652.0 3.6 copy.246
  655.9 9.5 fusion.101
  665.3 11.8 multiply_convert_fusion.1
  677.2 4.3 convolution_convert_fusion
  681.4 20.2 copy.249
  701.7 5.5 all-to-all-start.5
  707.2 9.1 convolution_convert_fusion.2
  716.4 78.3 %all-to-all-done.5 = bf16[2,1408,1024]{2,0,1:T(2,128)(2,1)} async-done(((bf16[2,1408,1024]{2,0,1:T(2,128)(2,1)}), bf16[2,1408,1024]{2,0,1:T(2,128)(2,1)}, u32[]{:S(2)}, u32[]{:S(2)}) %all-to-all-start.5) | async-done | bytes 5767200 | tf_op jit(solution)/shard_map/all_to_all | solution.py:190
  794.7 7.1 copy.250
  801.8 14.5 gather_fusion.1
  816.3 6.1 fusion.57
  824.0 12.6 fusion.61
  836.7 11.4 convolution_convert_fusion.1
  848.1 12.3 copy.255
  860.5 71.6 %all_to_all.188 = bf16[2,1408,1024]{2,0,1:T(2,128)(2,1)S(1)} all-to-all(bf16[2,1408,1024]{2,0,1:T(2,128)(2,1)S(1)} %copy.255), channel_id=1, replica_groups=mesh['seq'=8,'fsdp'=16] {'fsdp'}, dimensions={1} | all-to-all | bytes 11534336 | tf_op jit(solution)/shard_map/all_to_all | solution.py:223
  932.1 4.4 copy.256
  936.5 14.4 gather_fusion.3
  950.9 5.6 convert_reduce_fusion
  960.2 4.2 all-to-all-start.8
  964.6 3.8 fusion.77
  968.5 3.5 all-to-all-done.8
  978.3 76.7 %while.28 = (s32[]{:T(128)}, f32[2048,1,64]{0,2,1:T(8,128)S(1)}, f32[2048,1,64]{0,2,1:T(8,128)S(1)}, bf16[4,512,1,2,64]{1,4,3,2,0:T(8,128)(2,1)}, bf16[4,512,1,2...) while((s32[]{:T(128)}, f32[2048,1,64]{0,2,1:T(8,128)S(1)}, ...), condition=%wide.region_23.24_spmd.clone, body=%wide.region_21.23_spmd.clone.sunk | while | flops 1368128512 | bytes 133592760 | solution.py:285
  983.5 3.4 fusion.159
  986.9 3.2 fusion.160
  990.1 4.6 fusion.162
  1002.6 3.4 fusion.159
  1006.0 3.3 fusion.160
  1009.3 4.7 fusion.162
  1018.5 3.2 fusion.158
  1021.8 3.4 fusion.159
  1025.2 3.2 fusion.160
  1028.4 4.6 fusion.162
  1037.7 3.2 fusion.158
  1040.9 3.4 fusion.159
  1044.3 3.3 fusion.160
  1047.6 4.8 fusion.162
  1055.9 5.2 all-to-all-start.10
  1075.8 5.1 all-to-all-start.11
  1081.2 5.8 all-to-all-done.11
  1087.0 4.1 all-to-all-start.9
  1108.1 5.8 fusion.73
  1117.3 5.0 fusion.71
  1122.3 66.2 %all-reduce.9 = (f32[1024]{0:T(1024)S(1)}, f32[128]{0:T(128)S(1)}, f32[1024]{0:T(1024)S(1)}) all-reduce(f32[1024]{0:T(1024)S(1)} %get-tuple-element.206, f32[128]{0:T(128)S(1)} %pad_maximum_fusion.12, f32[1024]{0:T(1024)S(1)} %get-tuple-element.204), channel_id=2, replica_groups=mesh['seq'=8,'fsdp'=16] {'seq','fsdp'}, use_global_device_ids=true, to_apply=%region_28.29.clone | all-reduce | flops 2176 | bytes 17408
  1195.0 525.5 %reduce-scatter.7.cloned.1.call-done = f32[8,1024]{1,0:T(8,128)} async-done(((f32[1024,1024]{1,0:T(8,128)}), f32[8,1024]{1,0:T(8,128)}) %reduce-scatter.7.cloned.1.call-update) | async-done | bytes 32784 | tf_op jit(solution)/shard_map/reduce_scatter | solution.py:339
  1720.5 648.4 %reduce-scatter.5.cloned.1.call-done = f32[8,2048]{1,0:T(8,128)} async-done(((f32[1024,2048]{1,0:T(8,128)}), f32[8,2048]{1,0:T(8,128)}) %reduce-scatter.5.cloned.1.call-update) | async-done | bytes 65552 | tf_op jit(solution)/shard_map/reduce_scatter | solution.py:337
  (333 shorter events, 152.8 us)
Async XLA Ops:
  7.2 658.2 %copy-start = (bf16[2,1024,512]{2,1,0:T(8,128)(2,1)S(1)}, bf16[2,1024,512]{2,1,0:T(8,128)(2,1)}, u32[]{:S(2)}) copy-start(bf16[2,1024,512]{2,1,0:T(8,128)(2,1)} %param.23) | copy-start | bytes 6291460
  7.2 203.6 %all-gather.3.cloned.1.call-start = ((), (), s32[]{:S(2)}) async-start(), calls=%async_computation.16 | async-start | bytes 4227072 | tf_op jit(solution)/shard_map/all_gather | solution.py:96
  7.9 471.4 %all-gather.5.cloned.1.call-start = ((), (), s32[]{:S(2)}) async-start(), calls=%async_computation.17 | async-start | bytes 2113536 | tf_op jit(solution)/shard_map/all_gather | solution.py:98
  81.8 129.0 %copy-start.32 = (f32[1024]{0:T(1024)}, f32[1024]{0:T(1024)S(1)}, u32[]{:S(2)}) copy-start(f32[1024]{0:T(1024)S(1)} %convert_element_type.163) | copy-start | bytes 12292
  83.5 132.1 %copy-start.53 = (f32[256]{0:T(256)}, f32[256]{0:T(256)S(1)}, u32[]{:S(2)}) copy-start(f32[256]{0:T(256)S(1)} %get-tuple-element.279) | copy-start | bytes 3076
  83.6 134.2 %copy-start.55 = (f32[64]{0:T(128)}, f32[64]{0:T(128)S(1)}, u32[]{:S(2)}) copy-start(f32[64]{0:T(128)S(1)} %get-tuple-element.282) | copy-start | bytes 772
  83.6 143.9 %copy-start.57 = (f32[64]{0:T(128)}, f32[64]{0:T(128)S(1)}, u32[]{:S(2)}) copy-start(f32[64]{0:T(128)S(1)} %get-tuple-element.283) | copy-start | bytes 772
  94.3 139.5 %copy-start.29 = (f32[256,32]{0,1:T(8,128)}, f32[256,32]{0,1:T(8,128)S(1)}, u32[]{:S(2)}) copy-start(f32[256,32]{0,1:T(8,128)S(1)} %get-tuple-element.277) | copy-start | bytes 98308
  219.2 10.2 all-to-all-start.1
  224.9 27.9 %copy-start.8 = (f32[256,1024]{0,1:T(8,128)}, f32[256,1024]{0,1:T(8,128)S(1)}, u32[]{:S(2)}) copy-start(f32[256,1024]{0,1:T(8,128)S(1)} %copy.231) | copy-start | bytes 3145732
  225.8 32.0 %copy-start.34 = (f32[256,16]{0,1:T(8,128)}, f32[256,16]{0,1:T(8,128)S(1)}, u32[]{:S(2)}) copy-start(f32[256,16]{0,1:T(8,128)S(1)} %get-tuple-element.270) | copy-start | bytes 49156
  229.5 10.5 all-to-all-start.2
  239.9 15.3 all-to-all-start
  244.5 14.4 copy-start.45
  258.9 37.6 %copy-start.61 = (bf16[8,32]{1,0:T(8,128)(2,1)S(1)}, bf16[8,32]{1,0:T(8,128)(2,1)}, u32[]{:S(2)}) copy-start(bf16[8,32]{1,0:T(8,128)(2,1)} %param.21) | copy-start | bytes 1540
  284.9 198.4 %copy-start.4 = (bf16[2048,1,64]{0,2,1:T(8,128)(2,1)}, bf16[2048,1,64]{0,2,1:T(8,128)(2,1)S(1)}, u32[]{:S(2)}) copy-start(bf16[2048,1,64]{0,2,1:T(8,128)(2,1)S(1)} %get-tuple-element.451) | copy-start | bytes 786436
  284.9 198.4 %copy-start.10 = (bf16[4,512,1,2,64]{1,4,3,2,0:T(8,128)(2,1)}, bf16[4,512,1,2,64]{1,4,3,2,0:T(8,128)(2,1)S(1)}, u32[]{:S(2)}) copy-start(bf16[4,512,1,2,64]{1,4,3,2,0:T(8,128)(2,1)S(1)} %get-tuple-element.462) | copy-start | bytes 1572868
  284.9 198.4 %copy-start.13 = (bf16[2048,1,64]{0,2,1:T(8,128)(2,1)}, bf16[2048,1,64]{0,2,1:T(8,128)(2,1)S(1)}, u32[]{:S(2)}) copy-start(bf16[2048,1,64]{0,2,1:T(8,128)(2,1)S(1)} %get-tuple-element.463) | copy-start | bytes 786436
  287.5 196.6 %copy-start.36 = (s32[1,256,8]{1,2,0:T(8,128)S(1)}, s32[1,256,8]{1,2,0:T(8,128)}, u32[]{:S(2)}) copy-start(s32[1,256,8]{1,2,0:T(8,128)} %param.24) | copy-start | bytes 24580
  291.5 187.8 %all-to-all-start.3 = ((bf16[8,256,128]{1,2,0:T(8,128)(2,1)}), bf16[8,256,128]{1,2,0:T(8,128)(2,1)}, u32[]{:S(2)}, u32[]{:S(2)}) async-start(bf16[8,256,128]{1,2,0:T(8,128)(2,1)} %copy.239), calls=%async_computation.3 | async-start | bytes 1048576 | tf_op jit(solution)/shard_map/all_to_all | solution.py:150
  296.5 186.0 %copy-start.39 = (f32[1024]{0:T(1024)}, f32[1024]{0:T(1024)S(1)}, u32[]{:S(2)}) copy-start(f32[1024]{0:T(1024)S(1)} %convert_element_type.169) | copy-start | bytes 12292
  476.5 10.8 copy-start.24
  505.6 72.7 %all-to-all-start.6 = ((bf16[32,88,1024]{2,1,0:T(8,128)(2,1)}), bf16[32,88,1024]{2,1,0:T(8,128)(2,1)}, u32[]{:S(2)}, u32[]{:S(2)}) async-start(bf16[32,88,1024]{2,1,0:T(8,128)(2,1)} %bitcast.369), calls=%async_computation.6 | async-start | bytes 11534336 | tf_op jit(solution)/shard_map/all_to_all | solution.py:209
  578.3 73.7 %all-to-all-start.4 = ((bf16[32,88,1024]{2,1,0:T(8,128)(2,1)}), bf16[32,88,1024]{2,1,0:T(8,128)(2,1)}, u32[]{:S(2)}, u32[]{:S(2)}) async-start(bf16[32,88,1024]{2,1,0:T(8,128)(2,1)} %bitcast.368), calls=%async_computation.4 | async-start | bytes 11534336 | tf_op jit(solution)/shard_map/all_to_all | solution.py:179
  655.6 9.7 copy-start.21
  701.7 93.1 %all-to-all-start.5 = ((bf16[2,1408,1024]{2,0,1:T(2,128)(2,1)}), bf16[2,1408,1024]{2,0,1:T(2,128)(2,1)}, u32[]{:S(2)}, u32[]{:S(2)}) async-start(bf16[2,1408,1024]{2,0,1:T(2,128)(2,1)} %copy.249), calls=%async_computation.5 | async-start | bytes 11534336 | tf_op jit(solution)/shard_map/all_to_all | solution.py:190
  707.1 9.3 copy-start.46
  707.1 406.8 %reduce-scatter.11.cloned.1.call-start = ((), (), s32[]{:S(2)}) async-start(), calls=%async_computation.21 | async-start | bytes 2359296 | tf_op jit(solution)/shard_map/reduce_scatter | solution.py:347
  716.3 399.4 %all-reduce.13.cloned.1.call-start = ((), (), s32[]{:S(2)}) async-start(), calls=%async_computation.22 | async-start | bytes 1048576
  801.8 14.5 copy-start.12
  823.8 369.1 %reduce-scatter.9.cloned.1.call-start = ((), (), s32[]{:S(2)}) async-start(), calls=%async_computation.20 | async-start | bytes 4718592 | tf_op jit(solution)/shard_map/reduce_scatter | solution.py:344
  936.5 20.1 copy-start.25
  936.5 20.1 copy-start.40
  936.5 20.1 copy-start.52
  950.9 6.3 copy-start.60
  950.9 7.5 copy-start.15
  960.2 11.8 all-to-all-start.8
  964.4 756.2 %reduce-scatter.7.cloned.1.call-start = ((), (), s32[]{:S(2)}) async-start(), calls=%async_computation.19 | async-start | bytes 4227072 | tf_op jit(solution)/shard_map/reduce_scatter | solution.py:339
  964.6 13.6 copy-start.5
  964.6 13.6 copy-start.11
  964.6 13.6 copy-start.14
  978.2 82.8 %copy-start.58 = (f32[64]{0:T(128)S(1)}, f32[64]{0:T(128)}, u32[]{:S(2)}) copy-start(f32[64]{0:T(128)} %copy-done.57) | copy-start | bytes 772
  978.2 82.9 %copy-start.56 = (f32[64]{0:T(128)S(1)}, f32[64]{0:T(128)}, u32[]{:S(2)}) copy-start(f32[64]{0:T(128)} %copy-done.55) | copy-start | bytes 772
  978.3 83.0 %copy-start.35 = (f32[256,16]{0,1:T(8,128)S(1)}, f32[256,16]{0,1:T(8,128)}, u32[]{:S(2)}) copy-start(f32[256,16]{0,1:T(8,128)} %copy-done.34) | copy-start | bytes 49156
  978.3 86.6 %copy-start.41 = (f32[256,16]{0,1:T(8,128)S(1)}, f32[256,16]{0,1:T(8,128)}, u32[]{:S(2)}) copy-start(f32[256,16]{0,1:T(8,128)} %get-tuple-element.269) | copy-start | bytes 49156
  986.9 7.9 copy-start.3
  1006.0 7.9 copy-start.3
  1025.2 7.9 copy-start.3
  1044.3 8.1 copy-start.3
  1055.0 13.5 copy-start.38
  1055.0 14.5 copy-start.44
  1055.9 19.9 all-to-all-start.10
  1065.9 15.0 copy-start.30
  1065.9 15.1 copy-start.31
  1068.5 12.5 copy-start.18
  1075.8 11.2 all-to-all-start.11
  1081.2 18.4 copy-start.9
  1087.0 11.3 all-to-all-start.9
  1091.1 1277.8 %reduce-scatter.5.cloned.1.call-start = ((), (), s32[]{:S(2)}) async-start(), calls=%async_computation.18 | async-start | bytes 8454144 | tf_op jit(solution)/shard_map/reduce_scatter | solution.py:337
  1099.9 8.1 copy-start.16
  1099.9 8.1 copy-start.33
  1099.9 8.1 copy-start.54
  1113.9 76.4 %copy-start.59 = (f32[256]{0:T(256)S(1)}, f32[256]{0:T(256)}, u32[]{:S(2)}) copy-start(f32[256]{0:T(256)} %get-tuple-element.278) | copy-start | bytes 3076
  1117.2 1251.7 %copy-start.1 = (bf16[2,1024,512]{2,1,0:T(8,128)(2,1)S(1)}, bf16[2,1024,512]{2,1,0:T(8,128)(2,1)}, u32[]{:S(2)}) copy-start(bf16[2,1024,512]{2,1,0:T(8,128)(2,1)} %param.23) | copy-start | bytes 6291460
  (24 other events, 87.9 us)
Sparse Core Ops, SparseCore 0:
  9.8 200.9 all-gather.2
  212.5 196.1 all-gather.4
  716.5 51.8 reduce-scatter.10
  823.9 200.0 all-reduce.12
  1026.4 54.4 reduce-scatter.8
  1083.8 636.6 reduce-scatter.6
  1723.4 645.4 reduce-scatter.4
where the time goes:
time: 2390 us; the launch traced here: 2380 us
  waiting for transfers between devices  1510 us (63%)
  blocking collectives  387 us (16%)
  local copies, waits for them, and re-layouts  180 us (8%)
  matrix products  160 us (7%)
  other arithmetic  73.9 us (3%)
  starting transfers between devices  53 us (2%)
    reduce_scatter x1, waiting for transfers between devices, on_device(): lax.psum_scatter(qkv_weight_grad, ('seq', 'fsdp'), scatter_dimension=0, t...  648 us
    reduce_scatter x1, waiting for transfers between devices, on_device(): lax.psum_scatter(out_weight_grad, ('seq', 'fsdp'), scatter_dimension=0, t...  525 us
    all_gather x1, blocking collectives, on_device(): lax.all_gather(router_weight, ('seq', 'fsdp'), axis=0, tiled=True)  180 us
    unnamed x2, blocking collectives  135 us
    all_gather x1, waiting for transfers between devices, on_device(): lax.all_gather(qkv_weight, ('seq', 'fsdp'), axis=0, tiled=True)  116 us
    all_to_all x1, waiting for transfers between devices, on_device(): lax.all_to_all(expert_out, 'fsdp', split_axis=1, concat_axis=0, tiled=True)  78.3 us
    all_to_all x1, blocking collectives, on_device(): lax.all_to_all(row_grad, 'fsdp', split_axis=1, concat_axis=0, tiled=True)  71.6 us
    all_to_all x1, waiting for transfers between devices, on_device(): lax.all_to_all(send_rows, 'fsdp', split_axis=0, concat_axis=1, tiled=True)  61.9 us
  transfers between devices with their start and end apart: 18, of which 11 were waited for; matrix products, arithmetic and copies ran while one was open for 14% of the time, Pallas kernels for 0%

commit v1 on v0

v1 whole, which is shorter than its diff:
```python
import functools
import math

import jax
import jax.numpy as jnp
from jax import lax
from jax.experimental import pallas as pl
from jax.experimental.pallas import tpu as pltpu
from jax.sharding import PartitionSpec as P

D = 1024
QUERY_HEADS = 16
KEY_VALUE_HEADS = 8
HEAD_SIZE = 64
F = 512
TOPK = 8
EXPERTS = 32
CAP = 88
TOKENS = 256
SEQ = 8
FSDP = 16
LENGTH = SEQ * TOKENS
QKW = 2048
ROWS = FSDP * CAP
GROUP = 4
STEPS = FSDP // GROUP
STEP_ROWS = GROUP * CAP
VMEM = 60 * 1024 * 1024

epsilon = 1e-06
rope_base = 10000.0
f32 = jnp.float32
bf16 = jnp.bfloat16


def rms_forward(values, weights):
    scaling = lax.rsqrt(jnp.mean(values * values, axis=-1, keepdims=True) + epsilon)
    return (values * scaling * weights, scaling)


def rms_backward(values, scaling, weights, incoming):
    weighted = incoming * weights
    scaling_cube = scaling * scaling * scaling
    result = scaling * weighted - values * scaling_cube * jnp.mean(
        weighted * values, axis=-1, keepdims=True
    )
    return (result, incoming * values * scaling)


def rotary_tables(positions, head_dim):
    half_dim = head_dim // 2
    freq_index = jnp.arange(half_dim, dtype=f32)
    inverse = jnp.exp(-(2.0 * freq_index / head_dim) * math.log(rope_base))
    angles = positions.astype(f32)[:, None] * inverse[None, :]
    return (jnp.cos(angles)[:, None, :], jnp.sin(angles)[:, None, :])


def rotate(values, cosine_values, sine_values):
    half_dim = values.shape[-1] // 2
    first_half = values[..., :half_dim]
    second_half = values[..., half_dim:]
    return jnp.concatenate(
        [
            first_half * cosine_values - second_half * sine_values,
            second_half * cosine_values + first_half * sine_values,
        ],
        axis=-1,
    )


def dot(a, b):
    return lax.dot_general(a, b, (((1,), (0,)), ((), ())), preferred_element_type=f32)


def dot_t(a, b):
    return lax.dot_general(a, b, (((1,), (1,)), ((), ())), preferred_element_type=f32)


def t_dot(a, b):
    return lax.dot_general(a, b, (((0,), (0,)), ((), ())), preferred_element_type=f32)


def attend_kernel(heads_ref, out_ref, full_ref, logs_ref, key0, key1, value):
    step = pl.program_id(0)
    lanes = lax.broadcasted_iota(jnp.int32, (1, 128), 1)
    low_half = lanes < HEAD_SIZE

    @pl.when(step == 0)
    def _():
        pair = heads_ref[:, 128:256].astype(f32)
        key0[...] = jnp.where(low_half, pair, 0.0).astype(bf16)
        key1[...] = jnp.where(low_half, 0.0, pltpu.roll(pair, 64, 1)).astype(bf16)
        value[...] = jnp.where(low_half, jnp.where(lanes == 0, 1.0, 0.0), pair).astype(bf16)

    rows = pl.multiple_of(step * TOKENS, TOKENS)
    query = (heads_ref[pl.ds(rows, TOKENS), 0:128].astype(f32) * (1.0 / 8.0)).astype(bf16)
    results = []
    for key in (key0, key1):
        total = jnp.zeros((TOKENS, 128), f32)
        for c in range(4):
            part = pl.ds(c * 512, 512)
            weights = jnp.exp(dot_t(query, key[part, :]))
            total = total + dot(weights.astype(bf16), value[part, :])
        results.append(total)
    sum0, sum1 = results[0][:, 0:1], results[1][:, 0:1]
    full = jnp.where(low_half, pltpu.roll(results[0] / sum0, 64, 1), results[1] / sum1)
    full_ref[...] = full
    out_ref[...] = full.astype(bf16)
    logs_ref[...] = jnp.where(low_half, jnp.log(sum0), jnp.log(sum1))


def attend(heads):
    return pl.pallas_call(
        attend_kernel,
        grid=(LENGTH // TOKENS,),
        in_specs=[pl.BlockSpec((LENGTH, 256), lambda i: (0, 0))],
        out_specs=[pl.BlockSpec((TOKENS, 128), lambda i: (i, 0))] * 3,
        out_shape=[
            jax.ShapeDtypeStruct((LENGTH, 128), bf16),
            jax.ShapeDtypeStruct((LENGTH, 128), f32),
            jax.ShapeDtypeStruct((LENGTH, 128), f32),
        ],
        scratch_shapes=[pltpu.VMEM((LENGTH, 128), bf16)] * 3,
        compiler_params=pltpu.CompilerParams(vmem_limit_bytes=VMEM),
        cost_estimate=pl.CostEstimate(
            flops=4 * LENGTH * LENGTH * 128, bytes_accessed=4 << 20, transcendentals=2 * LENGTH * LENGTH
        ),
        name="attend",
    )(heads)


def split3(values):
    high = values.astype(bf16).astype(f32)
    rest = values - high
    middle = rest.astype(bf16).astype(f32)
    return high, middle, rest - middle


def with_terms(base, lanes, start, parts):
    high, middle, low = parts
    tail = jnp.where(
        lanes == start,
        high,
        jnp.where(lanes == start + 1, middle, jnp.where(lanes == start + 2, low, 0.0)),
    )
    return tail


def attend_back_kernel(
    heads_ref, full_ref, logs_ref, grad_ref, dq_ref, dkv_ref,
    key0, key1, value0, value1, key_t, dk_total, dv_total,
):
    step = pl.program_id(0)
    lanes = lax.broadcasted_iota(jnp.int32, (1, 128), 1)
    low_half = lanes < HEAD_SIZE

    @pl.when(step == 0)
    def _():
        pair = heads_ref[:, 128:256].astype(f32)
        swapped = pltpu.roll(pair, 64, 1)
        ones_high = jnp.where((lanes >= 64) & (lanes < 67), 1.0, 0.0)
        ones_low = jnp.where(lanes < 3, 1.0, 0.0)
        key0[...] = jnp.where(low_half, pair, ones_high).astype(bf16)
        key1[...] = jnp.where(low_half, ones_low, swapped).astype(bf16)
        value0[...] = jnp.where(low_half, swapped, ones_high).astype(bf16)
        value1[...] = jnp.where(low_half, ones_low, pair).astype(bf16)
        key_t[...] = jnp.transpose(pair)[0:64, :].astype(bf16)
        dk_total[...] = jnp.zeros_like(dk_total)
        dv_total[...] = jnp.zeros_like(dv_total)

    rows = pl.multiple_of(step * TOKENS, TOKENS)
    query = heads_ref[pl.ds(rows, TOKENS), 0:128].astype(f32) * (1.0 / 8.0)
    grad = grad_ref[...].astype(f32)
    logs = logs_ref[...]
    product = grad * full_ref[...]
    delta0 = jnp.sum(jnp.where(low_half, product, 0.0), axis=1, keepdims=True)
    delta1 = jnp.sum(jnp.where(low_half, 0.0, product), axis=1, keepdims=True)
    query0 = jnp.where(low_half, query, with_terms(query, lanes, 64, split3(-logs[:, 0:1]))).astype(bf16)
    query1 = jnp.where(low_half, with_terms(query, lanes, 0, split3(-logs[:, 64:65])), query).astype(bf16)
    grad0 = jnp.where(low_half, grad, with_terms(grad, lanes, 64, split3(-delta0))).astype(bf16)
    grad1 = jnp.where(low_half, with_terms(grad, lanes, 0, split3(-delta1)), grad).astype(bf16)
    only_query = (jnp.where(low_half, query, 0.0).astype(bf16), jnp.where(low_half, 0.0, query).astype(bf16))
    only_grad = (jnp.where(low_half, grad, 0.0).astype(bf16), jnp.where(low_half, 0.0, grad).astype(bf16))
    dq = [jnp.zeros((64, TOKENS), f32), jnp.zeros((64, TOKENS), f32)]
    for c in range(4):
        part = pl.ds(c * 512, 512)
        dv = dv_total[part, :]
        dk = dk_total[part, :]
        for h, (key, value, query_h, grad_h) in enumerate(
            ((key0, value0, query0, grad0), (key1, value1, query1, grad1))
        ):
            probs = jnp.exp(dot_t(key[part, :], query_h))
            inner = dot_t(value[part, :], grad_h)
            dv = dv + dot(probs.astype(bf16), only_grad[h])
            scores = (probs * inner).astype(bf16)
            dk = dk + dot(scores, only_query[h])
            dq[h] = dq[h] + dot(key_t[:, c * 512 : (c + 1) * 512], scores)
        dv_total[part, :] = dv
        dk_total[part, :] = dk
    both = jnp.concatenate(dq, axis=0) * (1.0 / 8.0)
    dq_ref[...] = jnp.transpose(both).astype(bf16)

    @pl.when(step == pl.num_programs(0) - 1)
    def _():
        dk = dk_total[...]
        dv = dv_total[...]
        dk = dk + pltpu.roll(dk, 64, 1)
        dv = dv + pltpu.roll(dv, 64, 1)
        dkv_ref[...] = jnp.where(low_half, dk, dv).astype(bf16)


def attend_back(heads, full, logs, grad):
    return pl.pallas_call(
        attend_back_kernel,
        grid=(LENGTH // TOKENS,),
        in_specs=[
            pl.BlockSpec((LENGTH, 256), lambda i: (0, 0)),
            pl.BlockSpec((TOKENS, 128), lambda i: (i, 0)),
            pl.BlockSpec((TOKENS, 128), lambda i: (i, 0)),
            pl.BlockSpec((TOKENS, 128), lambda i: (i, 0)),
        ],
        out_specs=[
            pl.BlockSpec((TOKENS, 128), lambda i: (i, 0)),
            pl.BlockSpec((LENGTH, 128), lambda i: (0, 0)),
        ],
        out_shape=[
            jax.ShapeDtypeStruct((LENGTH, 128), bf16),
            jax.ShapeDtypeStruct((LENGTH, 128), bf16),
        ],
        scratch_shapes=[pltpu.VMEM((LENGTH, 128), bf16)] * 4
        + [pltpu.VMEM((64, LENGTH), bf16)]
        + [pltpu.VMEM((LENGTH, 128), f32)] * 2,
        compiler_params=pltpu.CompilerParams(vmem_limit_bytes=VMEM),
        cost_estimate=pl.CostEstimate(
            flops=10 * LENGTH * LENGTH * 128, bytes_accessed=5 << 20, transcendentals=2 * LENGTH * LENGTH
        ),
        name="attend_back",
    )(heads, full, logs, grad)


def expert_kernel(
    x_ref, g_ref, gates_ref, up_ref, down_ref,
    y_ref, r_ref, gg_ref, dup_ref, ddown_ref,
    rows_x, rows_p, rows_h, rows_u, stage_x, stage_g, stage_gate, places,
):
    step = pl.program_id(0)

    @pl.when(step < STEPS)
    def _():
        gates = gates_ref[0]
        chosen = gates > 0.0
        before = (
            lax.broadcasted_iota(jnp.int32, (TOKENS, TOKENS), 0)
            < lax.broadcasted_iota(jnp.int32, (TOKENS, TOKENS), 1)
        ).astype(f32).astype(bf16)
        rank = dot(chosen.astype(f32).astype(bf16), before)
        rank = jnp.where(chosen, rank, -1000.0)
        slot = lax.broadcasted_iota(jnp.int32, (2 * CAP, TOKENS), 0)
        slot_place = slot.astype(f32)
        first = slot < CAP
        for s in range(GROUP):
            wanted = jnp.where(first, rank[2 * s : 2 * s + 1, :], rank[2 * s + 1 : 2 * s + 2, :] + CAP)
            wanted = jnp.where(
                (wanted < CAP) & jnp.logical_not(first), -1.0, wanted
            )
            hot = jnp.where(slot_place == wanted, 1.0, 0.0)
            gate = jnp.where(first, gates[2 * s : 2 * s + 1, :], gates[2 * s + 1 : 2 * s + 2, :])
            slot_gate = jnp.sum(hot * gate, axis=1, keepdims=True)
            hot = hot.astype(bf16)
            places[s] = hot
            picked = dot(hot, x_ref[TOKENS * s : TOKENS * (s + 1), :])
            for e in range(2):
                stage_x[e, CAP * s : CAP * (s + 1), :] = picked[CAP * e : CAP * (e + 1), :]
                stage_gate[e, CAP * s : CAP * (s + 1), :] = jnp.broadcast_to(
                    slot_gate[CAP * e : CAP * (e + 1), :], (CAP, 128)
                )
            picked = dot(hot, g_ref[TOKENS * s : TOKENS * (s + 1), :])
            for e in range(2):
                stage_g[e, CAP * s : CAP * (s + 1), :] = picked[CAP * e : CAP * (e + 1), :]
        here = pl.ds(pl.multiple_of(step * STEP_ROWS, 16), STEP_ROWS)
        for e in range(2):
            x_rows = stage_x[e].astype(bf16)
            rows_x[e, here, :] = x_rows
            gate = stage_gate[e][:, 0:1]
            grads = stage_g[e]
            pair = (grads * gate).astype(bf16)
            rows_p[e, here, :] = pair
            gate_part = dot(x_rows, up_ref[e, :, 0:F])
            up_part = dot(x_rows, up_ref[e, :, F : 2 * F])
            sigmoid = 1.0 / (1.0 + jnp.exp(-gate_part))
            silu = gate_part * sigmoid
            hidden = (silu * up_part).astype(bf16)
            rows_h[e, here, :] = hidden
            hidden_grad = dot(pair, down_ref[e])
            slope = sigmoid * (1.0 + gate_part * (1.0 - sigmoid))
            rows_u[e, here, 0:F] = (hidden_grad * up_part * slope).astype(bf16)
            rows_u[e, here, F : 2 * F] = (hidden_grad * silu).astype(bf16)
            out = dot_t(hidden, down_ref[e]).astype(bf16).astype(f32)
            gate_grad = jnp.sum(out * grads, axis=1, keepdims=True)
            for s in range(GROUP):
                hot = places[s, CAP * e : CAP * (e + 1), :].astype(f32)
                gg_ref[0, 2 * s + e : 2 * s + e + 1, :] = jnp.sum(
                    hot * gate_grad[CAP * s : CAP * (s + 1), :], axis=0, keepdims=True
                )
            stage_x[e] = out * gate
            stage_g[e] = dot_t(rows_u[e, here, :], up_ref[e])
        for s in range(GROUP):
            part = slice(CAP * s, CAP * (s + 1))
            both = jnp.concatenate([stage_x[0, part, :], stage_x[1, part, :]], axis=0).astype(bf16)
            y_ref[TOKENS * s : TOKENS * (s + 1), :] = t_dot(places[s], both).astype(bf16)
            both = jnp.concatenate([stage_g[0, part, :], stage_g[1, part, :]], axis=0).astype(bf16)
            r_ref[TOKENS * s : TOKENS * (s + 1), :] = t_dot(places[s], both).astype(bf16)

    @pl.when(step >= STEPS)
    def _():
        turn = step - STEPS
        e = turn // 4
        columns = pl.ds(pl.multiple_of((turn % 4) * 256, 256), 256)
        dup_ref[0] = t_dot(rows_x[e, :, columns], rows_u[e]).astype(bf16)
        ddown_ref[0] = t_dot(rows_p[e, :, columns], rows_h[e]).astype(bf16)


def experts(x_all, g_all, gates, up, down):
    last = STEPS - 1
    return pl.pallas_call(
        expert_kernel,
        grid=(STEPS + 8,),
        in_specs=[
            pl.BlockSpec((GROUP * TOKENS, D), lambda i: (jnp.minimum(i, last), 0)),
            pl.BlockSpec((GROUP * TOKENS, D), lambda i: (jnp.minimum(i, last), 0)),
            pl.BlockSpec((1, 2 * GROUP, TOKENS), lambda i: (jnp.minimum(i, last), 0, 0)),
            pl.BlockSpec((2, D, 2 * F), lambda i: (0, 0, 0), pipeline_mode=pl.Buffered(1)),
            pl.BlockSpec((2, D, F), lambda i: (0, 0, 0), pipeline_mode=pl.Buffered(1)),
        ],
        out_specs=[
            pl.BlockSpec((GROUP * TOKENS, D), lambda i: (jnp.minimum(i, last), 0)),
            pl.BlockSpec((GROUP * TOKENS, D), lambda i: (jnp.minimum(i, last), 0)),
            pl.BlockSpec((1, 2 * GROUP, TOKENS), lambda i: (jnp.minimum(i, last), 0, 0)),
            pl.BlockSpec((1, 256, 2 * F), lambda i: (jnp.maximum(i - STEPS, 0) // 4, jnp.maximum(i - STEPS, 0) % 4, 0)),
            pl.BlockSpec((1, 256, F), lambda i: (jnp.maximum(i - STEPS, 0) // 4, jnp.maximum(i - STEPS, 0) % 4, 0)),
        ],
        out_shape=[
            jax.ShapeDtypeStruct((FSDP * TOKENS, D), bf16),
            jax.ShapeDtypeStruct((FSDP * TOKENS, D), bf16),
            jax.ShapeDtypeStruct((STEPS, 2 * GROUP, TOKENS), f32),
            jax.ShapeDtypeStruct((2, D, 2 * F), bf16),
            jax.ShapeDtypeStruct((2, D, F), bf16),
        ],
        scratch_shapes=[
            pltpu.VMEM((2, ROWS, D), bf16),
            pltpu.VMEM((2, ROWS, D), bf16),
            pltpu.VMEM((2, ROWS, F), bf16),
            pltpu.VMEM((2, ROWS, 2 * F), bf16),
            pltpu.VMEM((2, STEP_ROWS, D), f32),
            pltpu.VMEM((2, STEP_ROWS, D), f32),
            pltpu.VMEM((2, STEP_ROWS, 128), f32),
            pltpu.VMEM((GROUP, 2 * CAP, TOKENS), bf16),
        ],
        compiler_params=pltpu.CompilerParams(vmem_limit_bytes=VMEM),
        cost_estimate=pl.CostEstimate(flops=30 * 10**9, bytes_accessed=40 << 20, transcendentals=1 << 21),
        name="experts",
    )(x_all, g_all, gates, up, down)


def on_device(
    tokens, attn_gain, qkv_weight, qk_gain, out_weight, ffn_gain, router_weight,
    gate_up_weight, down_weight, routes, cotangent,
):
    layer_inputs = tokens.reshape(TOKENS, D).astype(f32)
    query_total_width = QUERY_HEADS * HEAD_SIZE
    key_total_width = KEY_VALUE_HEADS * HEAD_SIZE
    seq_place = lax.axis_index("seq")

    small = jnp.concatenate(
        [router_weight.reshape(256), attn_gain, ffn_gain, qk_gain, jnp.zeros((2048 - 273,), bf16)]
    ).reshape(16, 128)
    packed = jnp.concatenate([qkv_weight.reshape(16, 1024), out_weight.reshape(16, 512), small], axis=1)
    packed = lax.all_gather(packed, "fsdp", axis=0, tiled=True)
    packed = lax.all_gather(packed, "seq", axis=0, tiled=True).reshape(128, 16, 1664)
    full_qkv = packed[:, :, :1024].reshape(D, QKW)
    full_out = packed[:, :, 1024:1536].reshape(D, D)
    small = packed[:, :, 1536:].reshape(128, 2048)
    full_router = small[:, :256].reshape(D, EXPERTS)
    attn_norm = small[:, 256:264].reshape(D).astype(f32)
    ffn_norm = small[:, 264:272].reshape(D).astype(f32)
    qk_norm = small[:, 272].astype(f32)

    cot = cotangent.reshape(TOKENS, D)
    g_all = lax.all_gather(cot, "fsdp", axis=0, tiled=True)

    normed_attn, attn_scaling = rms_forward(layer_inputs, attn_norm)
    normed_attn = normed_attn.astype(bf16)
    projected_rows = jnp.dot(normed_attn, full_qkv, preferred_element_type=f32)
    query_raw = projected_rows[:, :query_total_width].reshape(TOKENS, QUERY_HEADS, HEAD_SIZE)
    key_raw = projected_rows[:, query_total_width : query_total_width + key_total_width].reshape(
        TOKENS, KEY_VALUE_HEADS, HEAD_SIZE
    )
    value_low = projected_rows[:, query_total_width + key_total_width :].astype(bf16)
    query_normed, query_scaling = rms_forward(query_raw, qk_norm[:HEAD_SIZE])
    key_normed, key_scaling = rms_forward(key_raw, qk_norm[HEAD_SIZE:])
    positions = seq_place * TOKENS + jnp.arange(TOKENS, dtype=jnp.int32)
    cosine_values, sine_values = rotary_tables(positions, HEAD_SIZE)
    query_low = rotate(query_normed, cosine_values, sine_values).astype(bf16)
    key_low = rotate(key_normed, cosine_values, sine_values).astype(bf16)
    send = jnp.concatenate(
        [
            query_low.reshape(TOKENS, 8, 128),
            key_low.reshape(TOKENS, 8, 64),
            value_low.reshape(TOKENS, 8, 64),
        ],
        axis=2,
    ).transpose(1, 0, 2)
    heads = lax.all_to_all(send, "seq", split_axis=0, concat_axis=0, tiled=True).reshape(LENGTH, 256)
    attended_low, attended_full, logs = attend(heads)
    attended_tokens = (
        lax.all_to_all(attended_low.reshape(8, TOKENS, 128), "seq", split_axis=0, concat_axis=0, tiled=True)
        .transpose(1, 0, 2)
        .reshape(TOKENS, D)
    )
    after_attention = layer_inputs + jnp.dot(attended_tokens, full_out, preferred_element_type=f32)
    normed_ffn, ffn_scaling = rms_forward(after_attention, ffn_norm)
    normed_ffn = normed_ffn.astype(bf16)
    logits = lax.dot_general(full_router, normed_ffn, (((0,), (1,)), ((), ())), preferred_element_type=f32)
    route_ids = routes.reshape(TOKENS, TOPK)
    expert_ids = jnp.arange(EXPERTS, dtype=jnp.int32)
    named = jnp.any(route_ids[None, :, :] == expert_ids[:, None, None], axis=2)
    peak = jnp.max(jnp.where(named, logits, -jnp.inf), axis=0, keepdims=True)
    chosen_exp = jnp.where(named, jnp.exp(logits - peak), 0.0)
    gates = chosen_exp / jnp.sum(chosen_exp, axis=0, keepdims=True)

    x_all = lax.all_gather(normed_ffn, "fsdp", axis=0, tiled=True)
    my_gates = lax.all_to_all(gates.reshape(FSDP, 2, TOKENS), "fsdp", split_axis=0, concat_axis=0, tiled=True)
    y_all, r_all, gate_grads, dup, ddown = experts(
        x_all, g_all, my_gates.reshape(STEPS, 2 * GROUP, TOKENS), gate_up_weight, down_weight
    )
    gate_grad = lax.all_to_all(
        gate_grads.reshape(FSDP, 2, TOKENS), "fsdp", split_axis=0, concat_axis=0, tiled=True
    ).reshape(EXPERTS, TOKENS)
    row_sum = lax.psum_scatter(r_all, "fsdp", scatter_dimension=0, tiled=True)
    expert_sum = lax.psum_scatter(y_all, "fsdp", scatter_dimension=0, tiled=True)
    layer_out = (after_attention + expert_sum.astype(f32)).astype(bf16).reshape(1, TOKENS, D)

    incoming = cot.astype(f32)
    chosen_grad = gates * (gate_grad - jnp.sum(gates * gate_grad, axis=0, keepdims=True))
    logits_grad = chosen_grad.astype(bf16)
    router_grad = lax.dot_general(normed_ffn, logits_grad, (((0,), (1,)), ((), ())), preferred_element_type=f32)
    normed_ffn_grad = row_sum.astype(f32) + lax.dot_general(
        logits_grad, full_router, (((0,), (1,)), ((), ())), preferred_element_type=f32
    )
    after_extra, ffn_terms = rms_backward(after_attention, ffn_scaling, ffn_norm, normed_ffn_grad)
    after_grad = incoming + after_extra
    ffn_gain_grad = jnp.sum(ffn_terms, axis=0)
    after_low = after_grad.astype(bf16)
    out_weight_grad = t_dot(attended_tokens, after_low)
    attended_grad = dot_t(after_low, full_out).astype(bf16)
    grad_heads = lax.all_to_all(
        attended_grad.reshape(TOKENS, 8, 128).transpose(1, 0, 2), "seq", split_axis=0, concat_axis=0, tiled=True
    ).reshape(LENGTH, 128)
    dq, dkv = attend_back(heads, attended_full, logs, grad_heads)
    back = jnp.concatenate([dq, dkv], axis=1).reshape(8, TOKENS, 256)
    back = lax.all_to_all(back, "seq", split_axis=0, concat_axis=0, tiled=True)
    token_query_grad = back[:, :, :128].transpose(1, 0, 2).reshape(TOKENS, QUERY_HEADS, HEAD_SIZE)
    token_key_grad = back[:, :, 128:192].transpose(1, 0, 2)
    token_value_grad = back[:, :, 192:].transpose(1, 0, 2).reshape(TOKENS, key_total_width)
    query_normed_grad = rotate(token_query_grad.astype(f32), cosine_values, -sine_values)
    key_normed_grad = rotate(token_key_grad.astype(f32), cosine_values, -sine_values)
    query_raw_grad, query_terms = rms_backward(query_raw, query_scaling, qk_norm[:HEAD_SIZE], query_normed_grad)
    key_raw_grad, key_terms = rms_backward(key_raw, key_scaling, qk_norm[HEAD_SIZE:], key_normed_grad)
    qk_gain_grad = jnp.concatenate(
        [jnp.sum(query_terms, axis=(0, 1)), jnp.sum(key_terms, axis=(0, 1))], axis=0
    )
    projected_grad = jnp.concatenate(
        [
            query_raw_grad.reshape(TOKENS, query_total_width).astype(bf16),
            key_raw_grad.reshape(TOKENS, key_total_width).astype(bf16),
            token_value_grad,
        ],
        axis=1,
    )
    qkv_weight_grad = t_dot(normed_attn, projected_grad)
    normed_attn_grad = dot_t(projected_grad, full_qkv)
    input_extra, attn_terms = rms_backward(layer_inputs, attn_scaling, attn_norm, normed_attn_grad)
    token_grad = (after_grad + input_extra).reshape(1, TOKENS, D)
    attn_gain_grad = jnp.sum(attn_terms, axis=0)

    axes = ("seq", "fsdp")
    early = lax.all_to_all(
        out_weight_grad.astype(bf16).reshape(128, 16, 512), axes, split_axis=0, concat_axis=0, tiled=True
    )
    out_part = jnp.sum(early.astype(f32), axis=0).reshape(8, 1024)
    late = lax.all_to_all(
        qkv_weight_grad.astype(bf16).reshape(128, 16, 1024), axes, split_axis=0, concat_axis=0, tiled=True
    )
    qkv_part = jnp.sum(late.astype(f32), axis=0).reshape(8, 2048)
    small = jnp.concatenate(
        [
            router_grad.reshape(128, 256),
            attn_gain_grad.reshape(128, 8),
            ffn_gain_grad.reshape(128, 8),
            qk_gain_grad.reshape(128, 1),
            jnp.zeros((128, 111), f32),
        ],
        axis=1,
    )
    small = jnp.sum(lax.all_to_all(small, axes, split_axis=0, concat_axis=0, tiled=True), axis=0)
    router_part = small[:256].reshape(8, 32)
    attn_part = small[256:264]
    ffn_part = small[264:272]
    qk_part = small[272:273]
    gate_up_part = lax.psum_scatter(dup, "seq", scatter_dimension=1, tiled=True).astype(f32)
    down_part = lax.psum_scatter(ddown, "seq", scatter_dimension=1, tiled=True).astype(f32)
    return (
        layer_out, token_grad, attn_part, qkv_part, qk_part, out_part, ffn_part, router_part,
        gate_up_part, down_part,
    )


def solution(mesh):
    return jax.shard_map(
        on_device,
        mesh=mesh,
        in_specs=(
            P("fsdp", "seq", None),
            P(("seq", "fsdp")),
            P(("seq", "fsdp"), None),
            P(("seq", "fsdp")),
            P(("seq", "fsdp"), None),
            P(("seq", "fsdp")),
            P(("seq", "fsdp"), None),
            P("fsdp", None, None),
            P("fsdp", None, None),
            P("fsdp", "seq", None),
            P("fsdp", "seq", None),
        ),
        out_specs=(
            P("fsdp", "seq", None),
            P("fsdp", "seq", None),
            P(("seq", "fsdp")),
            P(("seq", "fsdp"), None),
            P(("seq", "fsdp")),
            P(("seq", "fsdp"), None),
            P(("seq", "fsdp")),
            P(("seq", "fsdp"), None),
            P("fsdp", "seq", None),
            P("fsdp", "seq", None),
        ),
        check_vma=False,
    )
```

time: 2390 us -> 752 us (0.31)
  waiting for transfers between devices: 1510 us -> 386 us
  blocking collectives: 387 us -> 91.4 us
  matrix products: 160 us -> 22.8 us
  local copies, waits for them, and re-layouts: 180 us -> 70.4 us
  Pallas kernels: 0 us -> 92.4 us
  other arithmetic: 73.9 us -> 29.6 us
    reduce_scatter x4, waiting for transfers between devices: 1170 us -> 188 us  [the longest x1 103 us: on_device(): lax.psum_scatter(y_all, 'fsdp', scatter_dimension=0, tiled=True)]
    all_gather x1, blocking collectives: 180 us -> 31.8 us  [on_device(): packed = lax.all_gather(packed, 'fsdp', axis=0, tiled=True)]
    all_to_all x11 -> x5, waiting for transfers between devices: 215 us -> 72.1 us  [the longest x1 43.8 us: on_device(): lax.all_to_all(qkv_weight_grad.astype(bf16).reshape(128, 16, 1024), axes,...]
    dot_general x43 -> x9, matrix products: 160 us -> 22.8 us  [the longest x2 6.48 us: t_dot(): lax.dot_general(a, b, (((0,), (0,)), ((), ())), preferred_element_type=f32)]
    unnamed x2 -> x0, blocking collectives: 135 us -> none
    pallas_call x0 -> x3, Pallas kernels: none -> 92.4 us  [the longest x1 47.6 us: experts(): pl.pallas_call(expert_kernel, grid=(STEPS + 8,), in_specs=[pl.BlockSpec((...]
    gather x4 -> x0, local copies, waits for them, and re-layouts: 54.5 us -> none  [the longest x1 15.9 us: on_device(): send_grad = padded_grad[slot_table].reshape(experts_all, cap_rows, D)]
    convert_element_type x3 -> x2, local copies, waits for them, and re-layouts: 35.2 us -> 0.18 us  [the longest x1 0.09 us: on_device(): ffn_norm = small[:, 264:272].reshape(D).astype(f32)]
  transfers between devices with their start and end apart: 18 -> 12, of which waited for: 11 -> 8; matrix products, arithmetic and copies ran while one was open for 14% -> 15% of each run, Pallas kernels for 0% -> 6%
where the time goes in v1:
time: 752 us; the launch traced here: 743 us
  waiting for transfers between devices  386 us (51%)
  Pallas kernels  92.4 us (12%)
  blocking collectives  91.4 us (12%)
  local copies, waits for them, and re-layouts  70.4 us (9%)
  starting transfers between devices  34.3 us (5%)
  other arithmetic  29.6 us (4%)
  matrix products  22.8 us (3%)
  between operations  15.9 us (2%)
    reduce_scatter x1, waiting for transfers between devices, on_device(): lax.psum_scatter(y_all, 'fsdp', scatter_dimension=0, tiled=True)  103 us
    reduce_scatter x1, waiting for transfers between devices, on_device(): row_sum = lax.psum_scatter(r_all, 'fsdp', scatter_dimension=0, tiled=True)  84.8 us
    all_gather x1, waiting for transfers between devices, on_device(): lax.all_gather(packed, 'seq', axis=0, tiled=True).reshape(128, 16, 1664)  71.5 us
    all_gather x1, waiting for transfers between devices, on_device(): x_all = lax.all_gather(normed_ffn, 'fsdp', axis=0, tiled=True)  53.2 us
    pallas_call x1, Pallas kernels, experts(): pl.pallas_call(expert_kernel, grid=(STEPS + 8,), in_specs=[pl.BlockSpec((...  47.6 us
    all_to_all x1, waiting for transfers between devices, on_device(): lax.all_to_all(qkv_weight_grad.astype(bf16).reshape(128, 16, 1024), axes,...  43.8 us
    all_gather x1, blocking collectives, on_device(): packed = lax.all_gather(packed, 'fsdp', axis=0, tiled=True)  31.8 us
    pallas_call x1, Pallas kernels, attend_back(): pl.pallas_call(attend_back_kernel, grid=(LENGTH // TOKENS,), in_specs=[pl...  27.6 us
  transfers between devices with their start and end apart: 12, of which 8 were waited for; matrix products, arithmetic and copies ran while one was open for 15% of the time, Pallas kernels for 6%

profile of v1, /device:TPU:1, one launch (start us, length us, event | category | flops | bytes accessed | tf_op | source)
XLA Modules:
  0.0 743.1 jit_solution(4193663665261880890)
XLA Ops:
  10.2 1.4 concatenate.38
  11.7 31.8 %all_gather.12 = bf16[256,1664]{1,0:T(8,128)(2,1)} all-gather(bf16[16,1664]{1,0:T(8,128)(2,1)S(1)} %pad_maximum_fusion.7), channel_id=1, replica_groups=mesh['seq'=8,'fsdp'=16] {'fsdp'}, dimensions={0}, use_global_device_ids=true | all-gather | bytes 905216 | tf_op jit(solution)/shard_map/all_gather | solution.py:378
  45.3 71.5 %all-gather.5.cloned.1.call-done = bf16[2048,1664]{1,0:T(8,128)(2,1)} async-done(((bf16[256,1664]{1,0:T(8,128)(2,1)}), bf16[2048,1664]{1,0:T(8,128)(2,1)}) %all-gather.5.cloned.1.call-update) | async-done | bytes 6815760 | tf_op jit(solution)/shard_map/all_gather | solution.py:379
  116.8 1.1 slice.127
  117.9 5.0 slice.129
  124.6 7.1 reshape.361
  131.8 3.5 fusion.20
  135.4 1.2 copy-done.6
  141.2 16.9 %all_to_all.49 = bf16[8,256,256]{1,2,0:T(8,128)(2,1)S(1)} all-to-all(bf16[8,256,256]{1,2,0:T(8,128)(2,1)S(1)} %maximum_bitcast_fusion), channel_id=1, replica_groups=mesh['seq'=8,'fsdp'=16] {'seq'}, dimensions={0} | all-to-all | bytes 2097152 | tf_op jit(solution)/shard_map/all_to_all | solution.py:413
  158.1 1.3 copy.106
  159.4 17.2 %attend.1 = (bf16[2048,128]{1,0:T(8,128)(2,1)}, f32[2048,128]{1,0:T(8,128)}, f32[2048,128]{1,0:T(8,128)}) custom-call(bf16[2048,256]{1,0:T(8,128)(2,1)} %bitcast.130), custom_call_target="tpu_custom_call" | custom-call | flops 2147483648 | bytes 4194304 | tf_op jit(solution)/shard_map/attend/pallas_call | solution.py:113
  176.7 2.0 copy.107
  178.7 3.5 all-to-all-start.1
  182.3 3.2 slice.140
  185.4 2.7 reshape.368
  188.3 1.0 all-to-all-done.1
  190.1 2.0 multiply_reduce_fusion.4
  192.8 1.0 multiply_convert_fusion
  193.9 1.5 slice.142
  195.4 1.0 reshape.370
  196.5 1.3 select_reduce_fusion
  198.5 19.5 %all_to_all.50 = f32[16,2,256]{2,1,0:T(2,128)S(1)} all-to-all(f32[16,2,256]{2,1,0:T(2,128)} %reshape.371), channel_id=1, replica_groups=mesh['seq'=8,'fsdp'=16] {'fsdp'}, dimensions={0} | all-to-all | bytes 65536 | tf_op jit(solution)/shard_map/all_to_all | solution.py:432
  218.6 53.2 %all-gather.7.cloned.1.call-done.x_ref = bf16[4096,1024]{1,0:T(8,128)(2,1)} async-done(((bf16[256,1024]{1,0:T(8,128)(2,1)}), bf16[4096,1024]{1,0:T(8,128)(2,1)}) %all-gather.7.cloned.1.call-update) | async-done | bytes 8388624 | tf_op jit(solution)/shard_map/all_gather | solution.py:431
  271.8 47.6 %experts.1 = (bf16[4096,1024]{1,0:T(8,128)(2,1)}, bf16[4096,1024]{1,0:T(8,128)(2,1)}, f32[4,8,256]{2,1,0:T(8,128)}, bf16[2,1024,1024]{2,1,0:T(8,128)(2,1)}, bf16[2,1024,512]{2,1,0:T(8,128)(2,1)}) custom-call(bf16[4096,1024]{1,0:T(8,128)(2,1)} %all-gather.7.cloned.1.call-done.x_ref, bf16[4096,1024]{1,0:T(8,128)(2,1)} %bitcast.141, ...), custom_call_target="tpu_custom_call" | custom-call | flops 30000001024 | bytes 41943040 | tf_op jit(solution)/shard_map/experts/pallas_call | solution.py:325
  321.4 10.7 %all_to_all.51 = f32[16,2,256]{2,1,0:T(2,128)} all-to-all(f32[16,2,256]{2,1,0:T(2,128)S(1)} %reshape.374), channel_id=1, replica_groups=mesh['seq'=8,'fsdp'=16] {'fsdp'}, dimensions={0} | all-to-all | bytes 65536 | tf_op jit(solution)/shard_map/all_to_all | solution.py:436
  333.5 84.8 %reduce-scatter.7.cloned.1.call-done = bf16[256,1024]{1,0:T(8,128)(2,1)} async-done(((bf16[4096,1024]{1,0:T(8,128)(2,1)}), bf16[256,1024]{1,0:T(8,128)(2,1)}) %reduce-scatter.7.cloned.1.call-update) | async-done | bytes 524304 | tf_op jit(solution)/shard_map/reduce_scatter | solution.py:439
  418.3 2.5 multiply_reduce_fusion.1
  420.8 102.8 %reduce-scatter.5.cloned.1.call-done = bf16[256,1024]{1,0:T(8,128)(2,1)} async-done(((bf16[4096,1024]{1,0:T(8,128)(2,1)}), bf16[256,1024]{1,0:T(8,128)(2,1)}) %reduce-scatter.5.cloned.1.call-update) | async-done | bytes 524304 | tf_op jit(solution)/shard_map/reduce_scatter | solution.py:440
  523.7 3.0 convert_add_fusion
  527.5 12.5 %all_to_all.52 = bf16[8,256,128]{2,1,0:T(8,128)(2,1)} all-to-all(bf16[8,256,128]{2,1,0:T(8,128)(2,1)S(1)} %bitcast.124), channel_id=1, replica_groups=mesh['seq'=8,'fsdp'=16] {'seq'}, dimensions={0} | all-to-all | bytes 1048576 | tf_op jit(solution)/shard_map/all_to_all | solution.py:456
  540.0 27.6 %attend_back.1 = (bf16[2048,128]{1,0:T(8,128)(2,1)}, bf16[2048,128]{1,0:T(8,128)(2,1)}) custom-call(bf16[2048,256]{1,0:T(8,128)(2,1)} %bitcast.131, f32[2048,128]{1,0:T(8,128)} %get-tuple-element.24.full_ref, f32[2048,128]{1,0:T(8,128)} %get-tuple-element.25.logs_ref, bf16[2048,128]{1,0:T(8,128)(2,1)} %bitcast.137), custom_call_target="tpu_custom_call" | custom-call | flops 5368709120 | bytes 5242880 | tf_op jit(solution)/shard_map/attend_back/pallas_call | solution.py:213
  567.6 1.3 pad_maximum_fusion
  568.9 1.3 copy.109
  570.2 5.0 all-to-all-start.5
  575.4 1.3 copy.111
  576.8 1.3 copy.112
  578.2 1.0 copy.115
  579.3 1.0 copy.116
  580.4 1.0 copy-done.5
  581.4 1.1 fusion.37
  582.5 2.0 reshape.381
  585.5 1.1 pad_maximum_fusion.1
  586.7 1.3 copy.113
  588.0 2.6 copy.110
  592.5 2.3 copy.117
  594.8 2.0 copy.114
  597.7 3.6 multiply_reduce_fusion
  601.4 2.5 multiply_reduce_fusion.6
  604.3 5.0 fusion.13
  609.6 0.9 copy.125
  610.5 11.9 %all-to-all-start.6 = ((f32[128,1,384]{2,1,0:T(1,128)}), f32[128,1,384]{2,1,0:T(1,128)S(1)}, u32[]{:S(2)}, u32[]{:S(2)}) async-start(f32[128,1,384]{2,1,0:T(1,128)} %copy.125), calls=%async_computation.8 | async-start | bytes 393216 | tf_op jit(solution)/shard_map/all_to_all | solution.py:505
  622.4 1.8 convolution_convert_fusion.1
  624.2 2.2 reshape.387
  626.4 8.8 %all-to-all-done.6 = f32[128,1,384]{2,1,0:T(1,128)S(1)} async-done(((f32[128,1,384]{2,1,0:T(1,128)}), f32[128,1,384]{2,1,0:T(1,128)S(1)}, u32[]{:S(2)}, u32[]{:S(2)}) %all-to-all-start.6) | async-done | bytes 196640 | tf_op jit(solution)/shard_map/all_to_all | solution.py:505
  635.2 8.6 %all-to-all-start.8 = ((bf16[128,16,512]{2,1,0:T(8,128)(2,1)}), bf16[128,16,512]{2,1,0:T(8,128)(2,1)S(1)}, u32[]{:S(2)}, u32[]{:S(2)}) async-start(bf16[128,16,512]{2,1,0:T(8,128)(2,1)} %reshape.387), calls=%async_computation.10 | async-start | bytes 4194304 | tf_op jit(solution)/shard_map/all_to_all | solution.py:487
  643.8 4.7 convolution_convert_fusion
  648.5 7.1 reshape.385
  655.6 18.6 %all-to-all-done.8 = bf16[128,16,512]{2,1,0:T(8,128)(2,1)S(1)} async-done(((bf16[128,16,512]{2,1,0:T(8,128)(2,1)}), bf16[128,16,512]{2,1,0:T(8,128)(2,1)S(1)}, u32[]{:S(2)}, u32[]{:S(2)}) %all-to-all-start.8) | async-done | bytes 2097184 | tf_op jit(solution)/shard_map/all_to_all | solution.py:487
  674.2 4.9 all-to-all-start.7
  679.2 1.8 convert_element_type.151
  681.0 2.2 convert_element_type.150
  683.2 2.3 fusion.10
  688.6 43.8 %all-to-all-done.7 = bf16[128,16,1024]{2,1,0:T(8,128)(2,1)} async-done(((bf16[128,16,1024]{2,1,0:T(8,128)(2,1)}), bf16[128,16,1024]{2,1,0:T(8,128)(2,1)}, u32[]{:S(2)}, u32[]{:S(2)}) %all-to-all-start.7) | async-done | bytes 4194336 | tf_op jit(solution)/shard_map/all_to_all | solution.py:491
  732.3 2.8 convert_reduce_fusion
  (171 shorter events, 26.2 us)
Async XLA Ops:
  7.2 37.1 %copy-start.9 = (bf16[1,256,1024]{2,1,0:T(8,128)(2,1)S(1)}, bf16[1,256,1024]{2,1,0:T(8,128)(2,1)}, u32[]{:S(2)}) copy-start(bf16[1,256,1024]{2,1,0:T(8,128)(2,1)} %param.11) | copy-start | bytes 1572868
  7.2 109.6 %all-gather.5.cloned.1.call-start = ((), (), s32[]{:S(2)}) async-start(), calls=%async_computation.13 | async-start | bytes 7667712 | tf_op jit(solution)/shard_map/all_gather | solution.py:379
  43.5 175.2 %all-gather.9.cloned.1.call-start = ((), (), s32[]{:S(2)}) async-start(), calls=%async_computation.19 | async-start | bytes 8912896 | tf_op jit(solution)/shard_map/all_gather | solution.py:389
  45.1 86.7 %copy-start.33 = (f32[256]{0:T(256)}, f32[256]{0:T(256)S(1)}, u32[]{:S(2)}) copy-start(f32[256]{0:T(256)S(1)} %get-tuple-element.68) | copy-start | bytes 3076
  123.0 0.8 copy-start.11
  124.6 7.2 copy-start.23
  135.3 1.3 copy-start.6
  136.7 1.0 slice-start
  137.7 2.3 copy-start
  137.9 3.0 copy-start.3
  139.0 1.2 copy-start.30
  139.1 1.9 copy-start.27
  140.9 17.2 %copy-start.17 = (f32[256,8]{0,1:T(8,128)}, f32[256,8]{0,1:T(8,128)S(1)}, u32[]{:S(2)}) copy-start(f32[256,8]{0,1:T(8,128)S(1)} %get-tuple-element.61) | copy-start | bytes 24580
  178.7 10.6 %all-to-all-start.1 = ((bf16[8,256,128]{1,2,0:T(8,128)(2,1)}), bf16[8,256,128]{1,2,0:T(8,128)(2,1)S(1)}, u32[]{:S(2)}, u32[]{:S(2)}) async-start(bf16[8,256,128]{1,2,0:T(8,128)(2,1)} %copy.107), calls=%async_computation.1 | async-start | bytes 1048576 | tf_op jit(solution)/shard_map/all_to_all | solution.py:416
  182.2 89.6 %all-gather.7.cloned.1.call-start = ((), (), s32[]{:S(2)}) async-start(), calls=%async_computation.14 | async-start | bytes 8912896 | tf_op jit(solution)/shard_map/all_gather | solution.py:431
  185.4 2.7 copy-start.14
  188.2 9.5 %copy-start.20 = (f32[1024]{0:T(1024)}, f32[1024]{0:T(1024)S(1)}, u32[]{:S(2)}) copy-start(f32[1024]{0:T(1024)S(1)} %reshape.392) | copy-start | bytes 12292
  189.3 0.8 copy-start.8
  192.1 226.1 %copy-start.2 = (f32[256,1024]{1,0:T(8,128)}, f32[256,1024]{1,0:T(8,128)S(1)}, u32[]{:S(2)}) copy-start(f32[256,1024]{1,0:T(8,128)S(1)} %get-tuple-element.72) | copy-start | bytes 3145732
  192.2 1.7 copy-start.29
  192.8 5.0 copy-start.25
  193.8 224.5 %reduce-scatter.7.cloned.1.call-start = ((), (), s32[]{:S(2)}) async-start(), calls=%async_computation.16 | async-start | bytes 8912896 | tf_op jit(solution)/shard_map/reduce_scatter | solution.py:439
  319.4 204.2 %reduce-scatter.5.cloned.1.call-start = ((), (), s32[]{:S(2)}) async-start(), calls=%async_computation.15 | async-start | bytes 8912896 | tf_op jit(solution)/shard_map/reduce_scatter | solution.py:440
  320.0 359.2 %reduce-scatter.11.cloned.1.call-start = ((), (), s32[]{:S(2)}) async-start(), calls=%async_computation.18 | async-start | bytes 2359296 | tf_op jit(solution)/shard_map/reduce_scatter | solution.py:511
  333.5 190.2 %copy-start.21 = (f32[1024]{0:T(1024)S(1)}, f32[1024]{0:T(1024)}, u32[]{:S(2)}) copy-start(f32[1024]{0:T(1024)} %copy-done.20) | copy-start | bytes 12292
  333.5 190.2 %copy-start.26 = (f32[256]{0:T(256)S(1)}, f32[256]{0:T(256)}, u32[]{:S(2)}) copy-start(f32[256]{0:T(256)} %copy-done.25) | copy-start | bytes 3076
  333.5 190.2 %copy-start.35 = (f32[256]{0:T(256)S(1)}, f32[256]{0:T(256)}, u32[]{:S(2)}) copy-start(f32[256]{0:T(256)} %get-tuple-element.69) | copy-start | bytes 3076
  570.2 15.0 %all-to-all-start.5 = ((bf16[8,256,256]{1,2,0:T(8,128)(2,1)}), bf16[8,256,256]{1,2,0:T(8,128)(2,1)S(1)}, u32[]{:S(2)}, u32[]{:S(2)}) async-start(bf16[8,256,256]{1,2,0:T(8,128)(2,1)} %copy.109), calls=%async_computation.7 | async-start | bytes 2097152 | tf_op jit(solution)/shard_map/all_to_all | solution.py:461
  575.2 1.5 copy-start.19
  575.2 105.8 %reduce-scatter.9.cloned.1.call-start = ((), (), s32[]{:S(2)}) async-start(), calls=%async_computation.17 | async-start | bytes 4718592 | tf_op jit(solution)/shard_map/reduce_scatter | solution.py:510
  576.7 1.4 copy-start.31
  576.7 1.5 copy-start.18
  576.8 2.4 copy-start.22
  578.1 2.2 copy-start.28
  580.3 1.0 copy-start.5
  580.4 1.0 copy-start.16
  582.5 2.9 copy-start.1
  588.0 2.8 copy-start.4
  591.6 6.1 copy-start.7
  601.3 2.9 copy-start.15
  601.3 2.9 copy-start.24
  601.4 2.9 copy-start.34
  604.3 5.2 copy-start.12
  604.3 5.2 copy-start.13
  610.5 24.7 %all-to-all-start.6 = ((f32[128,1,384]{2,1,0:T(1,128)}), f32[128,1,384]{2,1,0:T(1,128)S(1)}, u32[]{:S(2)}, u32[]{:S(2)}) async-start(f32[128,1,384]{2,1,0:T(1,128)} %copy.125), calls=%async_computation.8 | async-start | bytes 393216 | tf_op jit(solution)/shard_map/all_to_all | solution.py:505
  635.2 39.0 %all-to-all-start.8 = ((bf16[128,16,512]{2,1,0:T(8,128)(2,1)}), bf16[128,16,512]{2,1,0:T(8,128)(2,1)S(1)}, u32[]{:S(2)}, u32[]{:S(2)}) async-start(bf16[128,16,512]{2,1,0:T(8,128)(2,1)} %reshape.387), calls=%async_computation.10 | async-start | bytes 4194304 | tf_op jit(solution)/shard_map/all_to_all | solution.py:487
  674.2 58.1 %all-to-all-start.7 = ((bf16[128,16,1024]{2,1,0:T(8,128)(2,1)}), bf16[128,16,1024]{2,1,0:T(8,128)(2,1)}, u32[]{:S(2)}, u32[]{:S(2)}) async-start(bf16[128,16,1024]{2,1,0:T(8,128)(2,1)} %reshape.385), calls=%async_computation.9 | async-start | bytes 8388608 | tf_op jit(solution)/shard_map/all_to_all | solution.py:491
  679.2 4.1 copy-start.32
  681.0 2.2 copy-start.10
Sparse Core Ops, SparseCore 0:
  43.6 73.1 all-gather.4
  119.3 74.1 all-gather.8
  195.9 75.8 all-gather.6
  319.5 98.6 reduce-scatter.6
  422.4 101.2 reduce-scatter.4
  525.9 40.6 reduce-scatter.10
  580.5 58.6 reduce-scatter.8

commit v2 on v1

v2 whole, which is shorter than its diff:
```python
import functools
import math

import jax
import jax.numpy as jnp
from jax import lax
from jax.experimental import pallas as pl
from jax.experimental.pallas import tpu as pltpu
from jax.sharding import PartitionSpec as P

D = 1024
QUERY_HEADS = 16
KEY_VALUE_HEADS = 8
HEAD_SIZE = 64
F = 512
TOPK = 8
EXPERTS = 32
TOKENS = 256
SEQ = 8
FSDP = 16
LENGTH = SEQ * TOKENS
QKW = 2048
VMEM = 60 * 1024 * 1024

epsilon = 1e-06
rope_base = 10000.0
f32 = jnp.float32
bf16 = jnp.bfloat16


def rms_forward(values, weights):
    scaling = lax.rsqrt(jnp.mean(values * values, axis=-1, keepdims=True) + epsilon)
    return (values * scaling * weights, scaling)


def rms_backward(values, scaling, weights, incoming):
    weighted = incoming * weights
    scaling_cube = scaling * scaling * scaling
    result = scaling * weighted - values * scaling_cube * jnp.mean(
        weighted * values, axis=-1, keepdims=True
    )
    return (result, incoming * values * scaling)


def rotary_tables(positions, head_dim):
    half_dim = head_dim // 2
    freq_index = jnp.arange(half_dim, dtype=f32)
    inverse = jnp.exp(-(2.0 * freq_index / head_dim) * math.log(rope_base))
    angles = positions.astype(f32)[:, None] * inverse[None, :]
    return (jnp.cos(angles)[:, None, :], jnp.sin(angles)[:, None, :])


def rotate(values, cosine_values, sine_values):
    half_dim = values.shape[-1] // 2
    first_half = values[..., :half_dim]
    second_half = values[..., half_dim:]
    return jnp.concatenate(
        [
            first_half * cosine_values - second_half * sine_values,
            second_half * cosine_values + first_half * sine_values,
        ],
        axis=-1,
    )


def dot(a, b):
    return lax.dot_general(a, b, (((1,), (0,)), ((), ())), preferred_element_type=f32)


def dot_t(a, b):
    return lax.dot_general(a, b, (((1,), (1,)), ((), ())), preferred_element_type=f32)


def t_dot(a, b):
    return lax.dot_general(a, b, (((0,), (0,)), ((), ())), preferred_element_type=f32)


def attend_kernel(heads_ref, out_ref, full_ref, logs_ref, key0, key1, value):
    step = pl.program_id(0)
    lanes = lax.broadcasted_iota(jnp.int32, (1, 128), 1)
    low_half = lanes < HEAD_SIZE

    @pl.when(step == 0)
    def _():
        pair = heads_ref[:, 128:256].astype(f32)
        key0[...] = jnp.where(low_half, pair, 0.0).astype(bf16)
        key1[...] = jnp.where(low_half, 0.0, pltpu.roll(pair, 64, 1)).astype(bf16)
        value[...] = jnp.where(low_half, jnp.where(lanes == 0, 1.0, 0.0), pair).astype(bf16)

    rows = pl.multiple_of(step * TOKENS, TOKENS)
    query = (heads_ref[pl.ds(rows, TOKENS), 0:128].astype(f32) * (1.0 / 8.0)).astype(bf16)
    results = []
    for key in (key0, key1):
        total = jnp.zeros((TOKENS, 128), f32)
        for c in range(4):
            part = pl.ds(c * 512, 512)
            weights = jnp.exp(dot_t(query, key[part, :]))
            total = total + dot(weights.astype(bf16), value[part, :])
        results.append(total)
    sum0, sum1 = results[0][:, 0:1], results[1][:, 0:1]
    full = jnp.where(low_half, pltpu.roll(results[0] / sum0, 64, 1), results[1] / sum1)
    full_ref[...] = full
    out_ref[...] = full.astype(bf16)
    logs_ref[...] = jnp.where(low_half, jnp.log(sum0), jnp.log(sum1))


def attend(heads):
    return pl.pallas_call(
        attend_kernel,
        grid=(LENGTH // TOKENS,),
        in_specs=[pl.BlockSpec((LENGTH, 256), lambda i: (0, 0))],
        out_specs=[pl.BlockSpec((TOKENS, 128), lambda i: (i, 0))] * 3,
        out_shape=[
            jax.ShapeDtypeStruct((LENGTH, 128), bf16),
            jax.ShapeDtypeStruct((LENGTH, 128), f32),
            jax.ShapeDtypeStruct((LENGTH, 128), f32),
        ],
        scratch_shapes=[pltpu.VMEM((LENGTH, 128), bf16)] * 3,
        compiler_params=pltpu.CompilerParams(vmem_limit_bytes=VMEM),
        cost_estimate=pl.CostEstimate(
            flops=4 * LENGTH * LENGTH * 128, bytes_accessed=4 << 20, transcendentals=2 * LENGTH * LENGTH
        ),
        name="attend",
    )(heads)


def split3(values):
    high = values.astype(bf16).astype(f32)
    rest = values - high
    middle = rest.astype(bf16).astype(f32)
    return high, middle, rest - middle


def with_terms(lanes, start, parts):
    high, middle, low = parts
    tail = jnp.where(
        lanes == start,
        high,
        jnp.where(lanes == start + 1, middle, jnp.where(lanes == start + 2, low, 0.0)),
    )
    return tail


MESH = pl.DeviceIdType.MESH


class Place:
    def __init__(self):
        self.seq = lax.axis_index("seq")
        self.fsdp = lax.axis_index("fsdp")
        self.core = lax.rem(self.fsdp, 2)
        self.xh = lax.rem(self.fsdp // 2, 2)
        self.z = self.fsdp // 4
        self.y = lax.rem(self.seq, 4)
        self.xl = self.seq // 4

    def sibling(self):
        return {"fsdp": self.fsdp + 1 - 2 * self.core}

    def fsdp_at(self, ring, pair):
        z = lax.rem(self.z + ring + 4, 4)
        xh = 1 - self.xh if pair else self.xh
        return z * 4 + xh * 2 + self.core

    def seq_at(self, ring, pair):
        y = lax.rem(self.y + ring + 4, 4)
        xl = 1 - self.xl if pair else self.xl
        return xl * 4 + y

    def plane(self, axis):
        at = self.fsdp_at if axis == "fsdp" else self.seq_at
        return {
            "up": {axis: at(1, 0)},
            "down": {axis: at(-1, 0)},
            "across": {axis: at(0, 1)},
        }


def meet(targets):
    barrier = pltpu.get_barrier_semaphore()
    for target in targets:
        pl.semaphore_signal(barrier, inc=1, device_id=target, device_id_type=MESH)
    pl.semaphore_wait(barrier, len(targets))


class Copies:
    def __init__(self, send_sems, recv_sems):
        self.send_sems, self.recv_sems, self.count, self.all = send_sems, recv_sems, 0, []

    def start(self, src, dst, target):
        k = self.count
        self.count += 1
        copy = pltpu.make_async_remote_copy(
            src_ref=src, dst_ref=dst, send_sem=self.send_sems.at[k], recv_sem=self.recv_sems.at[k],
            device_id=target, device_id_type=MESH,
        )
        copy.start()
        self.all.append(copy)
        return copy

    def finish(self):
        for copy in self.all:
            copy.wait_send()


WCOLS = 1664

def attend_back_kernel(
    heads_ref, full_ref, logs_ref, grad_ref, y_ref, dq_ref, dkv_ref, sum_ref,
    key0, key1, value0, value1, key_t, dk_total, dv_total,
    slots, sib_in, hop_in, local_sems, send_sems, recv_sems,
):
    here = Place()
    sib = here.sibling()
    way = here.plane("fsdp")
    loads = [
        pltpu.make_async_copy(y_ref.at[2 * k], slots.at[k], local_sems.at[k]) for k in (6, 7, 5, 3, 4, 2, 1, 0)
    ]
    for copy in loads:
        copy.start()
    meet([sib, *way.values()])
    net = Copies(send_sems, recv_sems)
    joins = {k: net.start(y_ref.at[2 * k + 1], sib_in.at[k], sib) for k in (7, 6, 5, 3, 4, 2, 1, 0)}
    lanes = lax.broadcasted_iota(jnp.int32, (1, 128), 1)
    low_half = lanes < HEAD_SIZE
    pair = heads_ref[:, 128:256].astype(f32)
    swapped = pltpu.roll(pair, 64, 1)
    ones_high = jnp.where((lanes >= 64) & (lanes < 67), 1.0, 0.0)
    ones_low = jnp.where(lanes < 3, 1.0, 0.0)
    key0[...] = jnp.where(low_half, pair, ones_high).astype(bf16)
    key1[...] = jnp.where(low_half, ones_low, swapped).astype(bf16)
    value0[...] = jnp.where(low_half, swapped, ones_high).astype(bf16)
    value1[...] = jnp.where(low_half, ones_low, pair).astype(bf16)
    key_t[...] = jnp.transpose(pair)[0:64, :].astype(bf16)
    dk_total[...] = jnp.zeros_like(dk_total)
    dv_total[...] = jnp.zeros_like(dv_total)

    def one(step, carry):
        rows = pl.ds(pl.multiple_of(step * TOKENS, TOKENS), TOKENS)
        query = heads_ref[rows, 0:128].astype(f32) * (1.0 / 8.0)
        grad = grad_ref[rows, :].astype(f32)
        logs = logs_ref[rows, :]
        product = grad * full_ref[rows, :]
        delta0 = jnp.sum(jnp.where(low_half, product, 0.0), axis=1, keepdims=True)
        delta1 = jnp.sum(jnp.where(low_half, 0.0, product), axis=1, keepdims=True)
        query0 = jnp.where(low_half, query, with_terms(lanes, 64, split3(-logs[:, 0:1]))).astype(bf16)
        query1 = jnp.where(low_half, with_terms(lanes, 0, split3(-logs[:, 64:65])), query).astype(bf16)
        grad0 = jnp.where(low_half, grad, with_terms(lanes, 64, split3(-delta0))).astype(bf16)
        grad1 = jnp.where(low_half, with_terms(lanes, 0, split3(-delta1)), grad).astype(bf16)
        only_query = (
            jnp.where(low_half, query, 0.0).astype(bf16), jnp.where(low_half, 0.0, query).astype(bf16)
        )
        only_grad = (jnp.where(low_half, grad, 0.0).astype(bf16), jnp.where(low_half, 0.0, grad).astype(bf16))
        dq = [jnp.zeros((64, TOKENS), f32), jnp.zeros((64, TOKENS), f32)]
        for c in range(4):
            part = pl.ds(c * 512, 512)
            dv = dv_total[part, :]
            dk = dk_total[part, :]
            for h, (key, value, query_h, grad_h) in enumerate(
                ((key0, value0, query0, grad0), (key1, value1, query1, grad1))
            ):
                probs = jnp.exp(dot_t(key[part, :], query_h))
                inner = dot_t(value[part, :], grad_h)
                dv = dv + dot(probs.astype(bf16), only_grad[h])
                scores = (probs * inner).astype(bf16)
                dk = dk + dot(scores, only_query[h])
                dq[h] = dq[h] + dot(key_t[:, c * 512 : (c + 1) * 512], scores)
            dv_total[part, :] = dv
            dk_total[part, :] = dk
        both = jnp.concatenate(dq, axis=0) * (1.0 / 8.0)
        dq_ref[rows, :] = jnp.transpose(both).astype(bf16)
        return carry

    def run(first, last):
        lax.fori_loop(first, last, one, 0)

    def add_to(ref, *values):
        result = ref[...].astype(f32)
        for value in values:
            result = result + value[...].astype(f32)
        ref[...] = result.astype(bf16)

    def join(k):
        joins[k].wait_recv()
        add_to(slots.at[k], sib_in.at[k])

    def half(ref, which):
        return ref.at[pl.ds(128 * which, 128)]

    run(0, 1)
    for copy in loads:
        copy.wait()
    join(7)
    a = net.start(slots.at[7], hop_in.at[0], way["across"])
    join(3)
    xd = net.start(slots.at[3], hop_in.at[2], way["down"])
    join(5)
    xu = net.start(slots.at[5], hop_in.at[3], way["up"])
    join(6)
    run(1, 4)
    a.wait_recv()
    add_to(slots.at[6], hop_in.at[0])
    u = net.start(half(slots.at[6], 0), half(hop_in.at[1], 0), way["up"])
    d = net.start(half(slots.at[6], 1), half(hop_in.at[1], 1), way["down"])
    join(1)
    xd.wait_recv()
    xu.wait_recv()
    add_to(slots.at[1], hop_in.at[2], hop_in.at[3])
    rx = net.start(slots.at[1], hop_in.at[6], way["across"])
    join(2)
    join(4)
    join(0)
    run(4, 6)
    u.wait_recv()
    add_to(half(slots.at[4], 0), half(hop_in.at[1], 0))
    ru = net.start(slots.at[4], hop_in.at[4], way["up"])
    d.wait_recv()
    add_to(half(slots.at[2], 1), half(hop_in.at[1], 1))
    rd = net.start(slots.at[2], hop_in.at[5], way["down"])
    run(6, 8)
    dk = dk_total[...]
    dv = dv_total[...]
    dk = dk + pltpu.roll(dk, 64, 1)
    dv = dv + pltpu.roll(dv, 64, 1)
    dkv_ref[...] = jnp.where(low_half, dk, dv).astype(bf16)
    rx.wait_recv()
    ru.wait_recv()
    rd.wait_recv()
    sum_ref[...] = (
        slots[0].astype(f32) + hop_in[4].astype(f32) + hop_in[5].astype(f32) + hop_in[6].astype(f32)
    )
    net.finish()


def attend_back(heads, full, logs, grad, y_all):
    vmem = pl.BlockSpec(memory_space=pltpu.VMEM)
    return pl.pallas_call(
        attend_back_kernel,
        in_specs=[vmem] * 4 + [pl.BlockSpec(memory_space=pl.ANY)],
        out_specs=[vmem] * 3,
        out_shape=[
            jax.ShapeDtypeStruct((LENGTH, 128), bf16),
            jax.ShapeDtypeStruct((LENGTH, 128), bf16),
            jax.ShapeDtypeStruct((TOKENS, D), f32),
        ],
        scratch_shapes=[pltpu.VMEM((LENGTH, 128), bf16)] * 4
        + [pltpu.VMEM((64, LENGTH), bf16)]
        + [pltpu.VMEM((LENGTH, 128), f32)] * 2
        + [pltpu.VMEM((8, TOKENS, D), bf16)] * 2
        + [pltpu.VMEM((7, TOKENS, D), bf16)]
        + [
            pltpu.SemaphoreType.DMA((8,)),
            pltpu.SemaphoreType.DMA((18,)),
            pltpu.SemaphoreType.DMA((18,)),
        ],
        compiler_params=pltpu.CompilerParams(collective_id=9, has_side_effects=True, vmem_limit_bytes=VMEM),
        cost_estimate=pl.CostEstimate(
            flops=10 * LENGTH * LENGTH * 128, bytes_accessed=16 << 20, transcendentals=2 * LENGTH * LENGTH
        ),
        name="attend_back",
    )(heads, full, logs, grad, y_all)


def gather_kernel(in_ref, mask_ref, out_ref, masks_out, stage, block, local_sems, send_sems, recv_sems):
    here = Place()
    c, s, f = here.core, here.seq, here.z * 2 + here.xh
    sib = here.sibling()
    ways = {"seq": here.plane("seq"), "fsdp": here.plane("fsdp")}
    others = [(2, 1), (2, 0), (0, 1), (1, 1), (-1, 1), (1, 0), (-1, 0)]

    def f_at(ring, pair):
        return lax.rem(here.z + ring + 4, 4) * 2 + (1 - here.xh if pair else here.xh)

    seq_peers = [{"seq": here.seq_at(ring, pair)} for ring, pair in others]
    fsdp_peers = [{"fsdp": here.fsdp_at(ring, pair)} for ring, pair in others]
    meet([sib, *seq_peers, *fsdp_peers])
    net = Copies(send_sems, recv_sems)
    rows = pl.ds(pl.multiple_of(8 * c, 8), 8)
    join = net.start(in_ref.at[1 - c], stage.at[rows], sib)
    stage[rows, :] = in_ref[c]
    join.wait_recv()
    block[...] = stage[...].astype(bf16)
    low, high = pl.ds(0, 896), pl.ds(896, 768)
    locals_ = [
        pltpu.make_async_copy(block, out_ref.at[c, s, f], local_sems.at[0]),
        pltpu.make_async_copy(mask_ref, masks_out.at[here.fsdp], local_sems.at[1]),
    ]
    for copy in locals_:
        copy.start()
    a = [net.start(block.at[:, low], out_ref.at[c, s, f, :, low], peer) for peer in fsdp_peers]
    b = [net.start(block.at[:, high], out_ref.at[c, s, f, :, high], peer) for peer in seq_peers]
    m = [net.start(mask_ref, masks_out.at[here.fsdp], peer) for peer in [sib, *fsdp_peers]]
    for copy in locals_:
        copy.wait()
    kin = []

    def plane(part, way):
        def half(ref, which):
            return ref.at[pl.ds(4 * which, 4)]

        def go(ref, target):
            return net.start(ref, ref, target)

        ref = part(0, 0)
        across, up, down = go(ref, way["across"]), go(ref, way["up"]), go(ref, way["down"])
        kin.append(go(ref, sib))
        yield
        up.wait_recv()
        ref = part(-1, 0)
        far_low = go(half(ref, 0), way["up"])
        kin.append(go(ref, sib))
        down.wait_recv()
        ref = part(1, 0)
        far_high = go(half(ref, 1), way["down"])
        kin.append(go(ref, sib))
        yield
        across.wait_recv()
        ref = part(0, 1)
        up, down = go(ref, way["up"]), go(ref, way["down"])
        kin.append(go(ref, sib))
        yield
        far_low.wait_recv()
        far_high.wait_recv()
        kin.append(go(part(2, 0), sib))
        up.wait_recv()
        ref = part(-1, 1)
        far_low = go(half(ref, 0), way["up"])
        kin.append(go(ref, sib))
        down.wait_recv()
        ref = part(1, 1)
        far_high = go(half(ref, 1), way["down"])
        kin.append(go(ref, sib))
        yield
        far_low.wait_recv()
        far_high.wait_recv()
        kin.append(go(part(2, 1), sib))

    for copy in a:
        copy.wait_recv()
    first = plane(lambda ring, pair: out_ref.at[c, here.seq_at(ring, pair), :, :, low], ways["seq"])
    next(first)
    for copy in b:
        copy.wait_recv()
    second = plane(lambda ring, pair: out_ref.at[c, :, f_at(ring, pair), :, high], ways["fsdp"])
    next(second)
    for i in range(8):
        m[i].wait_recv()
        if i:
            ring, pair = others[i - 1]
            ref = masks_out.at[here.fsdp_at(-ring, pair)]
            kin.append(net.start(ref, ref, sib))
    for _ in range(4):
        next(first, None)
        next(second, None)
    for copy in kin:
        copy.wait_recv()
    net.finish()


def gather_weights(halves, mask):
    n = 64
    return pl.pallas_call(
        gather_kernel,
        in_specs=[pl.BlockSpec(memory_space=pltpu.VMEM)] * 2,
        out_specs=[pl.BlockSpec(memory_space=pl.ANY)] * 2,
        out_shape=[
            jax.ShapeDtypeStruct((2, 8, 8, 16, WCOLS), bf16),
            jax.ShapeDtypeStruct((16, 32, 256), bf16),
        ],
        scratch_shapes=[
            pltpu.VMEM((16, WCOLS), f32),
            pltpu.VMEM((16, WCOLS), bf16),
            pltpu.SemaphoreType.DMA((2,)),
            pltpu.SemaphoreType.DMA((n,)),
            pltpu.SemaphoreType.DMA((n,)),
        ],
        compiler_params=pltpu.CompilerParams(collective_id=1, has_side_effects=True, vmem_limit_bytes=VMEM),
        name="gather_weights",
    )(halves, mask)


def swap_kernel(in_ref, out_ref, local_sem, send_sems, recv_sems):
    here = Place()
    others = [(ring, pair) for ring in (0, -1, 1, 2) for pair in (0, 1)][1:]
    others = [(2, 1), (2, 0), (0, 1), (1, 1), (-1, 1), (1, 0), (-1, 0)]
    meet([{"seq": here.seq_at(ring, pair)} for ring, pair in others])
    net = Copies(send_sems, recv_sems)
    copies = [
        net.start(in_ref.at[here.seq_at(ring, pair)], out_ref.at[here.seq], {"seq": here.seq_at(ring, pair)})
        for ring, pair in others
    ]
    local = pltpu.make_async_copy(in_ref.at[here.seq], out_ref.at[here.seq], local_sem.at[0])
    local.start()
    local.wait()
    for copy in copies:
        copy.wait_recv()
    net.finish()


def swap(values, ident):
    return pl.pallas_call(
        swap_kernel,
        in_specs=[pl.BlockSpec(memory_space=pl.ANY)],
        out_specs=pl.BlockSpec(memory_space=pl.ANY),
        out_shape=jax.ShapeDtypeStruct(values.shape, values.dtype),
        scratch_shapes=[
            pltpu.SemaphoreType.DMA((1,)),
            pltpu.SemaphoreType.DMA((7,)),
            pltpu.SemaphoreType.DMA((7,)),
        ],
        compiler_params=pltpu.CompilerParams(collective_id=ident, has_side_effects=True),
        name="swap",
    )(values)


SLOTS=96
GROUP_ROWS=4*SLOTS
ROWS=4*GROUP_ROWS
WIDE=D+128

def moe_kernel(
    x_ref, g_ref, masks_ref, router_ref, up_hbm, down_hbm,
    row_out, gate_out, y_out, grads_out,
    slots, sib_in, hop_in, g_rows, up_ref, down_ref,
    rows_x, rows_p, rows_h, rows_u, rows_g, slot_gate, places, stage_y, stage_r, y_stage, w_stage,
    local_sems, send_sems, recv_sems,
):
    here = Place()
    sib = here.sibling()
    way = here.plane("fsdp")
    own = here.fsdp
    counter = [0]

    def local(src, dst):
        copy = pltpu.make_async_copy(src, dst, local_sems.at[counter[0]])
        counter[0] += 1
        copy.start()
        return copy

    first_x = local(x_ref, slots.at[0, :, pl.ds(0, D)])
    weights = [local(up_hbm, up_ref), local(down_hbm, down_ref)]

    def source(k):
        ring, pair, c = (0, -1, 1, 2)[k // 4], (k // 2) % 2, k % 2
        z = lax.rem(here.z + ring + 4, 4)
        xh = 1 - here.xh if pair else here.xh
        return z * 4 + xh * 2 + (1 - here.core if c else here.core)

    def fetch_g(group):
        return [local(g_ref.at[source(4 * group + s)], g_rows.at[s]) for s in range(4)]

    g_copies = fetch_g(0)
    meet([sib, *way.values()])
    net = Copies(send_sems, recv_sems)

    def block(k, low=0, rows=TOKENS):
        return slots.at[k, pl.ds(low, rows), pl.ds(0, D)]

    sent = {k: [] for k in range(16)}

    def push(k, to, target, low=0, rows=TOKENS, src=None):
        copy = net.start(block(k, low, rows) if src is None else src, block(to, low, rows), target)
        sent[k].append(copy)
        return copy

    across = push(0, 2, way["across"], src=x_ref)
    up = push(0, 4, way["up"], src=x_ref)
    down = push(0, 8, way["down"], src=x_ref)
    kin = {1: push(0, 1, sib, src=x_ref)}
    across.wait_recv()
    up_x = push(2, 6, way["up"])
    down_x = push(2, 10, way["down"])
    kin[3] = push(2, 3, sib)
    state = {}

    lanes = lax.broadcasted_iota(jnp.int32, (1, 128), 1)
    slot = lax.broadcasted_iota(jnp.int32, (2 * SLOTS, TOKENS), 0)
    slot_place = slot.astype(f32)
    first = slot < SLOTS
    expert = lax.broadcasted_iota(jnp.int32, (EXPERTS, TOKENS), 0)

    def gather(group):
        before = (
            lax.broadcasted_iota(jnp.int32, (TOKENS, TOKENS), 0)
            < lax.broadcasted_iota(jnp.int32, (TOKENS, TOKENS), 1)
        ).astype(f32).astype(bf16)
        for s in range(4):
            k = 4 * group + s
            if k in kin:
                kin[k].wait_recv()
            g_copies[s].wait()
            x_rows = slots[k, :, 0:D]
            named = masks_ref[source(k)].astype(f32)
            logits = dot_t(router_ref[...], x_rows)
            peak = jnp.max(jnp.where(named > 0.0, logits, -1e30), axis=0, keepdims=True)
            parts = jnp.where(named > 0.0, jnp.exp(logits - peak), 0.0)
            gates = parts / jnp.sum(parts, axis=0, keepdims=True)
            rank = dot(named.astype(bf16), before)
            rank = jnp.where(named > 0.0, rank, -1000.0)

            def mine(values, i):
                return jnp.sum(jnp.where(expert == 2 * own + i, values, 0.0), axis=0, keepdims=True)

            wanted = jnp.where(first, mine(rank, 0), mine(rank, 1) + SLOTS)
            hot = jnp.where(slot_place == wanted, 1.0, 0.0)
            gate = jnp.sum(hot * jnp.where(first, mine(gates, 0), mine(gates, 1)), axis=1, keepdims=True)
            hot = hot.astype(bf16)
            places[s] = hot
            picked = dot(hot, x_rows).astype(bf16)
            grads = dot(hot, g_rows[s])
            pair = (grads * gate).astype(bf16)
            grads = grads.astype(bf16)
            for i in range(2):
                part = slice(SLOTS * i, SLOTS * (i + 1))
                there = slice(group * GROUP_ROWS + SLOTS * s, group * GROUP_ROWS + SLOTS * (s + 1))
                rows_x[i, there, :] = picked[part]
                rows_p[i, there, :] = pair[part]
                rows_g[i, SLOTS * s : SLOTS * (s + 1), :] = grads[part]
                slot_gate[i, SLOTS * s : SLOTS * (s + 1), :] = jnp.broadcast_to(gate[part], (SLOTS, 128))

    def run(group):
        here_rows = pl.ds(group * GROUP_ROWS, GROUP_ROWS)

        def one(e, carry):
            x_rows = rows_x[e, here_rows, :]
            gate_part = dot(x_rows, up_ref[e, :, 0:F])
            up_part = dot(x_rows, up_ref[e, :, F : 2 * F])
            sigmoid = 1.0 / (1.0 + jnp.exp(-gate_part))
            silu = gate_part * sigmoid
            hidden = (silu * up_part).astype(bf16)
            rows_h[e, here_rows, :] = hidden
            hidden_grad = dot(rows_p[e, here_rows, :], down_ref[e])
            slope = sigmoid * (1.0 + gate_part * (1.0 - sigmoid))
            rows_u[e, here_rows, 0:F] = (hidden_grad * up_part * slope).astype(bf16)
            rows_u[e, here_rows, F : 2 * F] = (hidden_grad * silu).astype(bf16)
            out = dot_t(hidden, down_ref[e]).astype(bf16).astype(f32)
            gate_grad = jnp.sum(out * rows_g[e].astype(f32), axis=1, keepdims=True)
            stage_y[e] = (out * slot_gate[e][:, 0:1]).astype(bf16)
            stage_r[e, :, 0:D] = dot_t(rows_u[e, here_rows, :], up_ref[e]).astype(bf16)
            high = gate_grad.astype(bf16).astype(f32)
            column = 2 * own + e
            stage_r[e, :, D:WIDE] = jnp.where(
                lanes == column, high, jnp.where(lanes == column + EXPERTS, gate_grad - high, 0.0)
            ).astype(bf16)
            return carry

        lax.fori_loop(0, 2, one, 0)

    def combine(group):
        for copy in state.pop("y", ()):
            copy.wait()
        for s in range(4):
            k = 4 * group + s
            for copy in sent[k]:
                copy.wait_send()
            part = slice(SLOTS * s, SLOTS * (s + 1))
            both = jnp.concatenate([stage_y[0, part, :], stage_y[1, part, :]], axis=0)
            y_stage[s] = t_dot(places[s], both).astype(bf16)
            both = jnp.concatenate([stage_r[0, part, :], stage_r[1, part, :]], axis=0)
            slots[k] = t_dot(places[s], both).astype(bf16)
        state["y"] = [local(y_stage.at[s], y_out.at[4 * group + s]) for s in range(4)]
        for j in range(2):
            k = 4 * group + 2 * j
            state["k", group, j] = net.start(slots.at[k + 1], sib_in.at[2 * group + j], sib)

    def join(group, j):
        state["k", group, j].wait_recv()
        k = 4 * group + 2 * j
        slots[k] = (slots[k].astype(f32) + sib_in[2 * group + j].astype(f32)).astype(bf16)

    first_x.wait()
    gather(0)
    g_copies = fetch_g(1)
    for copy in weights:
        copy.wait()
    up.wait_recv()
    far_low = push(4, 12, way["up"], 0, 128)
    kin[5] = push(4, 5, sib)
    down.wait_recv()
    far_high = push(8, 12, way["down"], 128, 128)
    kin[9] = push(8, 9, sib)
    run(0)
    up_x.wait_recv()
    kin[7] = push(6, 7, sib)
    down_x.wait_recv()
    kin[11] = push(10, 11, sib)
    combine(0)
    far_low.wait_recv()
    far_high.wait_recv()
    far_x = push(12, 14, way["across"])
    kin[13] = push(12, 13, sib)
    gather(1)
    g_copies = fetch_g(3)
    run(1)
    far_x.wait_recv()
    kin[15] = push(14, 15, sib)
    combine(1)
    gather(3)
    g_copies = fetch_g(2)
    run(3)
    combine(3)
    gather(2)
    join(3, 1)
    hop_a = net.start(slots.at[14], hop_in.at[0], way["across"])
    join(3, 0)
    run(2)
    hop_a.wait_recv()
    slots[12] = (slots[12].astype(f32) + hop_in[0].astype(f32)).astype(bf16)
    hop_u = net.start(slots.at[12, pl.ds(0, 128)], hop_in.at[1, pl.ds(0, 128)], way["up"])
    hop_d = net.start(slots.at[12, pl.ds(128, 128)], hop_in.at[1, pl.ds(128, 128)], way["down"])
    combine(2)

    w_copies = [[], []]

    def weight_grad(piece):
        e, dx = piece // 2, piece % 2
        buffer = 0
        for copy in w_copies[buffer]:
            copy.wait()
        xl = 1 - here.xl if dx else here.xl
        columns = pl.ds(pl.multiple_of(xl * 512, 512), 512)
        w_stage[buffer, :, 0 : 2 * F] = t_dot(rows_x[e, :, columns], rows_u[e]).astype(bf16)
        w_stage[buffer, :, 2 * F : 3 * F] = t_dot(rows_p[e, :, columns], rows_h[e]).astype(bf16)
        w_copies[buffer] = [
            local(
                w_stage.at[buffer, pl.ds(128 * y, 128)],
                grads_out.at[e, pl.ds(pl.multiple_of(xl * 512 + 128 * y, 128), 128)],
            )
            for y in range(4)
        ]

    join(1, 1)
    hop_xd = net.start(slots.at[6], hop_in.at[2], way["down"])
    join(2, 1)
    hop_xu = net.start(slots.at[10], hop_in.at[3], way["up"])
    join(1, 0)
    join(2, 0)
    weight_grad(0)
    hop_u.wait_recv()
    slots[8, 0:128, :] = (slots[8, 0:128, :].astype(f32) + hop_in[1, 0:128, :].astype(f32)).astype(bf16)
    hop_ru = net.start(slots.at[8], hop_in.at[4], way["up"])
    hop_d.wait_recv()
    slots[4, 128:256, :] = (slots[4, 128:256, :].astype(f32) + hop_in[1, 128:256, :].astype(f32)).astype(bf16)
    hop_rd = net.start(slots.at[4], hop_in.at[5], way["down"])
    join(0, 1)
    join(0, 0)
    weight_grad(1)
    hop_xd.wait_recv()
    hop_xu.wait_recv()
    slots[2] = (slots[2].astype(f32) + hop_in[2].astype(f32) + hop_in[3].astype(f32)).astype(bf16)
    hop_rx = net.start(slots.at[2], hop_in.at[6], way["across"])
    weight_grad(2)
    weight_grad(3)
    hop_ru.wait_recv()
    hop_rd.wait_recv()
    hop_rx.wait_recv()
    total = (
        slots[0].astype(f32) + hop_in[4].astype(f32) + hop_in[5].astype(f32) + hop_in[6].astype(f32)
    )
    row_out[...] = total[:, 0:D]
    gate_out[...] = total[:, D:WIDE]
    for copies in (*w_copies, state["y"]):
        for copy in copies:
            copy.wait()
    waited = {id(copy) for k in range(16) for copy in sent[k]}
    for copy in net.all:
        if id(copy) not in waited:
            copy.wait_send()


def moe(x, g_all, masks, router_t, up, down):
    any_space = pl.BlockSpec(memory_space=pl.ANY)
    vmem = pl.BlockSpec(memory_space=pltpu.VMEM)
    return pl.pallas_call(
        moe_kernel,
        in_specs=[any_space, any_space, vmem, vmem, any_space, any_space],
        out_specs=[vmem, vmem, any_space, any_space],
        out_shape=[
            jax.ShapeDtypeStruct((TOKENS, D), f32),
            jax.ShapeDtypeStruct((TOKENS, 128), f32),
            jax.ShapeDtypeStruct((16, TOKENS, D), bf16),
            jax.ShapeDtypeStruct((2, D, 3 * F), bf16),
        ],
        scratch_shapes=[
            pltpu.VMEM((16, TOKENS, WIDE), bf16),
            pltpu.VMEM((8, TOKENS, WIDE), bf16),
            pltpu.VMEM((7, TOKENS, WIDE), bf16),
            pltpu.VMEM((4, TOKENS, D), bf16),
            pltpu.VMEM((2, D, 2 * F), bf16),
            pltpu.VMEM((2, D, F), bf16),
            pltpu.VMEM((2, ROWS, D), bf16),
            pltpu.VMEM((2, ROWS, D), bf16),
            pltpu.VMEM((2, ROWS, F), bf16),
            pltpu.VMEM((2, ROWS, 2 * F), bf16),
            pltpu.VMEM((2, GROUP_ROWS, D), bf16),
            pltpu.VMEM((2, GROUP_ROWS, 128), f32),
            pltpu.VMEM((4, 2 * SLOTS, TOKENS), bf16),
            pltpu.VMEM((2, GROUP_ROWS, D), bf16),
            pltpu.VMEM((2, GROUP_ROWS, WIDE), bf16),
            pltpu.VMEM((4, TOKENS, D), bf16),
            pltpu.VMEM((1, 512, 3 * F), bf16),
            pltpu.SemaphoreType.DMA((56,)),
            pltpu.SemaphoreType.DMA((40,)),
            pltpu.SemaphoreType.DMA((40,)),
        ],
        compiler_params=pltpu.CompilerParams(
            collective_id=4, has_side_effects=True, vmem_limit_bytes=63 * 1024 * 1024
        ),
        cost_estimate=pl.CostEstimate(flops=32 * 10**9, bytes_accessed=40 << 20, transcendentals=1 << 21),
        name="moe",
    )(x, g_all, masks, router_t, up, down)


GCOLS = 1536


def reduce_kernel(
    parts_ref, small_ref, out_ref, small_out,
    acc, sib_in, small_acc, small_sib, hop_a, hop_b, late_a, late_b, small_s, small_f, total, local_sems,
    send_sems, recv_sems,
):
    here = Place()
    c, s = here.core, here.seq
    f = here.z * 2 + here.xh
    sib = here.sibling()
    ways = {"seq": here.plane("seq"), "fsdp": here.plane("fsdp")}
    others = [(2, 1), (2, 0), (0, 1), (1, 1), (-1, 1), (1, 0), (-1, 0)]

    def f_at(ring, pair):
        return lax.rem(here.z + ring + 4, 4) * 2 + (1 - here.xh if pair else here.xh)

    seq_peers = [{"seq": here.seq_at(ring, pair)} for ring, pair in others]
    fsdp_peers = [{"fsdp": here.fsdp_at(ring, pair)} for ring, pair in others]
    own = pltpu.make_async_copy(parts_ref.at[c], acc, local_sems.at[0])
    own.start()
    meet([sib, *seq_peers, *fsdp_peers])
    net = Copies(send_sems, recv_sems)
    joins = [
        net.start(parts_ref.at[1 - c, pl.ds(2 * i, 2)], sib_in.at[pl.ds(2 * i, 2)], sib) for i in range(4)
    ]
    small_join = net.start(small_ref.at[1 - c], small_sib, sib)
    own.wait()
    small_join.wait_recv()
    small_acc[...] = small_ref[c] + small_sib[...]
    small_copies = [
        net.start(small_acc.at[here.seq_at(*others[i])], small_s.at[i], seq_peers[i]) for i in range(7)
    ]
    for i in range(4):
        joins[i].wait_recv()
        part = slice(2 * i, 2 * i + 2)
        acc[part] = (acc[part].astype(f32) + sib_in[part].astype(f32)).astype(bf16)

    def add_to(ref, *values):
        result = ref[...].astype(f32)
        for value in values:
            result = result + value[...].astype(f32)
        ref[...] = result.astype(bf16)

    def plane(part, hop, way):
        def half(ref, high):
            return ref.at[pl.ds(4 * high, 4)]

        a = net.start(part(2, 1), hop.at[0], way["across"])
        xd = net.start(part(-1, 1), hop.at[2], way["down"])
        xu = net.start(part(1, 1), hop.at[3], way["up"])
        yield
        a.wait_recv()
        add_to(part(2, 0), hop.at[0])
        u = net.start(half(part(2, 0), 0), half(hop.at[1], 0), way["up"])
        d = net.start(half(part(2, 0), 1), half(hop.at[1], 1), way["down"])
        yield
        xd.wait_recv()
        xu.wait_recv()
        add_to(part(0, 1), hop.at[2], hop.at[3])
        rx = net.start(part(0, 1), hop.at[6], way["across"])
        yield
        u.wait_recv()
        add_to(half(part(1, 0), 0), half(hop.at[1], 0))
        ru = net.start(part(1, 0), hop.at[4], way["up"])
        d.wait_recv()
        add_to(half(part(-1, 0), 1), half(hop.at[1], 1))
        rd = net.start(part(-1, 0), hop.at[5], way["down"])
        yield
        rx.wait_recv()
        ru.wait_recv()
        rd.wait_recv()
        add_to(part(0, 0), hop.at[4], hop.at[5], hop.at[6])

    low, high = pl.ds(0, GCOLS // 2), pl.ds(GCOLS // 2, GCOLS // 2)
    first = plane(lambda ring, pair: acc.at[here.seq_at(ring, pair), :, :, low], hop_a, ways["seq"])
    second = plane(lambda ring, pair: acc.at[:, f_at(ring, pair), :, high], hop_b, ways["fsdp"])
    for _ in range(4):
        next(first)
        next(second)
    for copy in small_copies:
        copy.wait_recv()
    mine = small_acc[s]
    for i in range(7):
        mine = mine + small_s[i]
    small_acc[s] = mine
    small_copies = [
        net.start(small_acc.at[s, f_at(*others[i])], small_f.at[i], fsdp_peers[i]) for i in range(7)
    ]
    next(first, None)
    a = [
        net.start(acc.at[s, f_at(*others[i]), :, low], late_a.at[i], fsdp_peers[i]) for i in range(7)
    ]
    next(second, None)
    b = [
        net.start(acc.at[here.seq_at(*others[i]), f, :, high], late_b.at[i], seq_peers[i]) for i in range(7)
    ]
    for copy in small_copies:
        copy.wait_recv()
    mine = small_acc[s, f]
    for i in range(7):
        mine = mine + small_f[i]
    small_out[...] = mine
    for cols, copies, late in ((slice(0, GCOLS // 2), a, late_a), (slice(GCOLS // 2, GCOLS), b, late_b)):
        for copy in copies:
            copy.wait_recv()
        result = acc[s, f, :, cols].astype(f32)
        for i in range(7):
            result = result + late[i].astype(f32)
        total[:, cols] = result
    theirs = pl.ds(pl.multiple_of(8 * (1 - c), 8), 8)
    last = net.start(total.at[theirs], out_ref.at[c], sib)
    out_ref[c] = total[pl.ds(pl.multiple_of(8 * c, 8), 8), :]
    last.wait_recv()
    net.finish()


def reduce_weights(parts, small):
    vmem = pl.BlockSpec(memory_space=pltpu.VMEM)
    n = 1 + 4 + 7 + 7 + 14 + 16 + 4
    return pl.pallas_call(
        reduce_kernel,
        in_specs=[pl.BlockSpec(memory_space=pl.ANY), vmem],
        out_specs=[vmem, vmem],
        out_shape=[jax.ShapeDtypeStruct((2, 8, GCOLS), f32), jax.ShapeDtypeStruct((8, 128), f32)],
        scratch_shapes=[
            pltpu.VMEM((8, 8, 16, GCOLS), bf16),
            pltpu.VMEM((8, 8, 16, GCOLS), bf16),
            pltpu.VMEM((8, 8, 8, 128), f32),
            pltpu.VMEM((8, 8, 8, 128), f32),
            pltpu.VMEM((7, 8, 16, GCOLS // 2), bf16),
            pltpu.VMEM((7, 8, 16, GCOLS // 2), bf16),
            pltpu.VMEM((7, 16, GCOLS // 2), bf16),
            pltpu.VMEM((7, 16, GCOLS // 2), bf16),
            pltpu.VMEM((7, 8, 8, 128), f32),
            pltpu.VMEM((7, 8, 128), f32),
            pltpu.VMEM((16, GCOLS), f32),
            pltpu.SemaphoreType.DMA((1,)),
            pltpu.SemaphoreType.DMA((n,)),
            pltpu.SemaphoreType.DMA((n,)),
        ],
        compiler_params=pltpu.CompilerParams(collective_id=3, has_side_effects=True, vmem_limit_bytes=VMEM),
        name="reduce_weights",
    )(parts, small)


def on_device(
    tokens, attn_gain, qkv_weight, qk_gain, out_weight, ffn_gain, router_weight,
    gate_up_weight, down_weight, routes, cotangent,
):
    layer_inputs = tokens.reshape(TOKENS, D).astype(f32)
    query_total_width = QUERY_HEADS * HEAD_SIZE
    key_total_width = KEY_VALUE_HEADS * HEAD_SIZE
    seq_place = lax.axis_index("seq")

    fsdp_place = lax.axis_index("fsdp")
    core = fsdp_place % 2
    route_ids = routes.reshape(TOKENS, TOPK)
    expert_ids = jnp.arange(EXPERTS, dtype=jnp.int32)
    named = jnp.any(route_ids[:, :, None] == expert_ids[None, None, :], axis=1)
    small = jnp.concatenate(
        [
            router_weight,
            attn_gain[:, None],
            ffn_gain[:, None],
            jnp.broadcast_to(qk_gain[:, None], (8, 1)),
            jnp.zeros((8, 93), bf16),
        ],
        axis=1,
    )
    halves = jnp.stack(
        [
            jnp.concatenate([qkv_weight[:, :1024], out_weight[:, :512], small], axis=1),
            jnp.concatenate([qkv_weight[:, 1024:], out_weight[:, 512:], small], axis=1),
        ]
    ).astype(f32)
    whole, masks = gather_weights(halves, named.T.astype(bf16))
    whole = whole.reshape(2, D, 1664)
    full_qkv = jnp.concatenate([whole[0, :, :1024], whole[1, :, :1024]], axis=1)
    full_out = jnp.concatenate([whole[0, :, 1024:1536], whole[1, :, 1024:1536]], axis=1)
    small = whole[0, :, 1536:]
    full_router = small[:, :32]
    attn_norm = small[:, 32].astype(f32)
    ffn_norm = small[:, 33].astype(f32)
    qk_norm = small[:, 34].reshape(128, 8)[:, 0].astype(f32)
    z_place, xh_place = fsdp_place // 4, (fsdp_place // 2) % 2
    y_place, xl_place = seq_place % 4, seq_place // 4

    cot = cotangent.reshape(TOKENS, D)
    g_all = lax.all_gather(cot[None], "fsdp", axis=0, tiled=True)

    normed_attn, attn_scaling = rms_forward(layer_inputs, attn_norm)
    normed_attn = normed_attn.astype(bf16)
    projected_rows = jnp.dot(normed_attn, full_qkv, preferred_element_type=f32)
    query_raw = projected_rows[:, :query_total_width].reshape(TOKENS, QUERY_HEADS, HEAD_SIZE)
    key_raw = projected_rows[:, query_total_width : query_total_width + key_total_width].reshape(
        TOKENS, KEY_VALUE_HEADS, HEAD_SIZE
    )
    value_low = projected_rows[:, query_total_width + key_total_width :].astype(bf16)
    query_normed, query_scaling = rms_forward(query_raw, qk_norm[:HEAD_SIZE])
    key_normed, key_scaling = rms_forward(key_raw, qk_norm[HEAD_SIZE:])
    positions = seq_place * TOKENS + jnp.arange(TOKENS, dtype=jnp.int32)
    cosine_values, sine_values = rotary_tables(positions, HEAD_SIZE)
    query_low = rotate(query_normed, cosine_values, sine_values).astype(bf16)
    key_low = rotate(key_normed, cosine_values, sine_values).astype(bf16)
    send = jnp.concatenate(
        [
            query_low.reshape(TOKENS, 8, 128),
            key_low.reshape(TOKENS, 8, 64),
            value_low.reshape(TOKENS, 8, 64),
        ],
        axis=2,
    ).transpose(1, 0, 2)
    heads = swap(send, 5).reshape(LENGTH, 256)
    attended_low, attended_full, logs = attend(heads)
    attended_tokens = (
        swap(attended_low.reshape(8, TOKENS, 128), 6)
        .transpose(1, 0, 2)
        .reshape(TOKENS, D)
    )
    after_attention = layer_inputs + jnp.dot(attended_tokens, full_out, preferred_element_type=f32)
    normed_ffn, ffn_scaling = rms_forward(after_attention, ffn_norm)
    normed_ffn = normed_ffn.astype(bf16)
    logits = jnp.dot(normed_ffn, full_router, preferred_element_type=f32)
    peak = jnp.max(jnp.where(named, logits, -jnp.inf), axis=1, keepdims=True)
    chosen_exp = jnp.where(named, jnp.exp(logits - peak), 0.0)
    gates = chosen_exp / jnp.sum(chosen_exp, axis=1, keepdims=True)

    g_all, masks = lax.optimization_barrier((g_all, masks))
    row_sum, gate_sum, y_all, grads = moe(normed_ffn, g_all, masks, full_router.T, gate_up_weight, down_weight)
    gate_grad = gate_sum[:, 0:32] + gate_sum[:, 32:64]
    expert_part = lax.psum_scatter(grads, "seq", scatter_dimension=1, tiled=True).astype(f32)
    gate_up_part, down_part = expert_part[:, :, : 2 * F], expert_part[:, :, 2 * F :]
    incoming = cot.astype(f32)
    chosen_grad = gates * (gate_grad - jnp.sum(gates * gate_grad, axis=1, keepdims=True))
    logits_grad = chosen_grad.astype(bf16)
    router_grad = t_dot(normed_ffn, logits_grad)
    normed_ffn_grad = row_sum + dot_t(logits_grad, full_router)
    after_extra, ffn_terms = rms_backward(after_attention, ffn_scaling, ffn_norm, normed_ffn_grad)
    after_grad = incoming + after_extra
    ffn_gain_grad = jnp.sum(ffn_terms, axis=0)
    after_low = after_grad.astype(bf16)
    out_weight_grad = t_dot(attended_tokens, after_low)
    attended_grad = dot_t(after_low, full_out).astype(bf16)
    grad_heads = swap(attended_grad.reshape(TOKENS, 8, 128).transpose(1, 0, 2), 7).reshape(LENGTH, 128)
    dq, dkv, expert_sum = attend_back(heads, attended_full, logs, grad_heads, y_all)
    layer_out = (after_attention + expert_sum).astype(bf16).reshape(1, TOKENS, D)
    back = jnp.concatenate([dq, dkv], axis=1).reshape(8, TOKENS, 256)
    back = swap(back, 8)
    token_query_grad = back[:, :, :128].transpose(1, 0, 2).reshape(TOKENS, QUERY_HEADS, HEAD_SIZE)
    token_key_grad = back[:, :, 128:192].transpose(1, 0, 2)
    token_value_grad = back[:, :, 192:].transpose(1, 0, 2).reshape(TOKENS, key_total_width)
    query_normed_grad = rotate(token_query_grad.astype(f32), cosine_values, -sine_values)
    key_normed_grad = rotate(token_key_grad.astype(f32), cosine_values, -sine_values)
    query_raw_grad, query_terms = rms_backward(query_raw, query_scaling, qk_norm[:HEAD_SIZE], query_normed_grad)
    key_raw_grad, key_terms = rms_backward(key_raw, key_scaling, qk_norm[HEAD_SIZE:], key_normed_grad)
    qk_gain_grad = jnp.concatenate(
        [jnp.sum(query_terms, axis=(0, 1)), jnp.sum(key_terms, axis=(0, 1))], axis=0
    )
    projected_grad = jnp.concatenate(
        [
            query_raw_grad.reshape(TOKENS, query_total_width).astype(bf16),
            key_raw_grad.reshape(TOKENS, key_total_width).astype(bf16),
            token_value_grad,
        ],
        axis=1,
    )
    qkv_weight_grad = t_dot(normed_attn, projected_grad)
    normed_attn_grad = dot_t(projected_grad, full_qkv)
    input_extra, attn_terms = rms_backward(layer_inputs, attn_scaling, attn_norm, normed_attn_grad)
    token_grad = (after_grad + input_extra).reshape(1, TOKENS, D)
    attn_gain_grad = jnp.sum(attn_terms, axis=0)

    qkv_low, out_low = qkv_weight_grad.astype(bf16), out_weight_grad.astype(bf16)
    parts = jnp.stack(
        [
            jnp.concatenate([qkv_low[:, :1024], out_low[:, :512]], axis=1),
            jnp.concatenate([qkv_low[:, 1024:], out_low[:, 512:]], axis=1),
        ]
    ).reshape(2, 8, 8, 16, GCOLS)
    small = jnp.concatenate(
        [
            router_grad.reshape(128, 256),
            attn_gain_grad.reshape(128, 8),
            ffn_gain_grad.reshape(128, 8),
            qk_gain_grad.reshape(128, 1),
            jnp.zeros((128, 751), f32),
        ],
        axis=1,
    ).reshape(8, 8, 2, 8, 128).transpose(2, 0, 1, 3, 4)
    parts, small = reduce_weights(parts, small)
    qkv_part = jnp.concatenate([parts[0, :, :1024], parts[1, :, :1024]], axis=1)
    out_part = jnp.concatenate([parts[0, :, 1024:], parts[1, :, 1024:]], axis=1)
    small = small.reshape(1024)
    router_part = small[:256].reshape(8, 32)
    attn_part = small[256:264]
    ffn_part = small[264:272]
    qk_part = small[272:273]
    return (
        layer_out, token_grad, attn_part, qkv_part, qk_part, out_part, ffn_part, router_part,
        gate_up_part, down_part,
    )


def solution(mesh):
    return jax.shard_map(
        on_device,
        mesh=mesh,
        in_specs=(
            P("fsdp", "seq", None),
            P(("seq", "fsdp")),
            P(("seq", "fsdp"), None),
            P(("seq", "fsdp")),
            P(("seq", "fsdp"), None),
            P(("seq", "fsdp")),
            P(("seq", "fsdp"), None),
            P("fsdp", None, None),
            P("fsdp", None, None),
            P("fsdp", "seq", None),
            P("fsdp", "seq", None),
        ),
        out_specs=(
            P("fsdp", "seq", None),
            P("fsdp", "seq", None),
            P(("seq", "fsdp")),
            P(("seq", "fsdp"), None),
            P(("seq", "fsdp")),
            P(("seq", "fsdp"), None),
            P(("seq", "fsdp")),
            P(("seq", "fsdp"), None),
            P("fsdp", "seq", None),
            P("fsdp", "seq", None),
        ),
        check_vma=False,
    )
```

time: 752 us -> 483 us (0.64)
  waiting for transfers between devices: 386 us -> 0.7 us
  Pallas kernels: 92.4 us -> 342 us
  blocking collectives: 91.4 us -> 0 us
  starting transfers between devices: 34.3 us -> 0.08 us
  matrix products: 22.8 us -> 11.9 us
  other arithmetic: 29.6 us -> 37.3 us
    pallas_call x2 -> x8, Pallas kernels: 75.2 us -> 324 us  [the longest x1 114 us: moe(): pl.pallas_call(moe_kernel, in_specs=[any_space, any_space, vmem, vmem, an...]
    reduce_scatter x4 -> x1, waiting for transfers between devices: 188 us -> 0.01 us  [on_device(): lax.psum_scatter(grads, 'seq', scatter_dimension=1, tiled=True).astype(f32)]
    all_gather x3 -> x1, waiting for transfers between devices: 125 us -> 0.01 us  [on_device(): g_all = lax.all_gather(cot[None], 'fsdp', axis=0, tiled=True)]
    all_to_all x5 -> x0, waiting for transfers between devices: 72.1 us -> none  [the longest x1 43.8 us: on_device(): lax.all_to_all(qkv_weight_grad.astype(bf16).reshape(128, 16, 1024), axes,...]
    all_to_all x4 -> x0, blocking collectives: 59.6 us -> none  [the longest x1 19.5 us: on_device(): lax.all_to_all(gates.reshape(FSDP, 2, TOKENS), 'fsdp', split_axis=0, conc...]
    all_to_all x5 -> x0, starting transfers between devices: 34 us -> none  [the longest x1 11.9 us: on_device(): lax.all_to_all(small, axes, split_axis=0, concat_axis=0, tiled=True)]
    all_gather x1 -> x0, blocking collectives: 31.8 us -> none  [on_device(): packed = lax.all_gather(packed, 'fsdp', axis=0, tiled=True)]
    reshape x16 -> x3, local copies, waits for them, and re-layouts: 30 us -> 1.45 us  [the longest x1 0.85 us: on_device(): small = jnp.concatenate([router_grad.reshape(128, 256), attn_gain_grad.re...]
  transfers between devices with their start and end apart: 12 -> 2, of which waited for: 8 -> 0; matrix products, arithmetic and copies ran while one was open for 15% -> 23% of each run, Pallas kernels for 6% -> 48%
where the time goes in v2:
time: 483 us; the launch traced here: 476 us
  Pallas kernels  342 us (71%)
  local copies, waits for them, and re-layouts  68.6 us (14%)
  other arithmetic  37.3 us (8%)
  between operations  15.8 us (3%)
  matrix products  11.9 us (2%)
    pallas_call x1, Pallas kernels, moe(): pl.pallas_call(moe_kernel, in_specs=[any_space, any_space, vmem, vmem, an...  114 us
    pallas_call x1, Pallas kernels, attend_back(): pl.pallas_call(attend_back_kernel, in_specs=[vmem] * 4 + [pl.BlockSpec(me...  61.9 us
    pallas_call x4, Pallas kernels, swap(): pl.pallas_call(swap_kernel, in_specs=[pl.BlockSpec(memory_space=pl.ANY)],...  58.5 us
    pallas_call x1, Pallas kernels, gather_weights(): pl.pallas_call(gather_kernel, in_specs=[pl.BlockSpec(memory_space=pltpu.V...  48.6 us
    pallas_call x1, Pallas kernels, reduce_weights(): pl.pallas_call(reduce_kernel, in_specs=[pl.BlockSpec(memory_space=pl.ANY)...  40.6 us
    pallas_call x1, Pallas kernels, attend(): pl.pallas_call(attend_kernel, grid=(LENGTH // TOKENS,), in_specs=[pl.Bloc...  17.5 us
  transfers between devices with their start and end apart: 2, of which 0 were waited for; matrix products, arithmetic and copies ran while one was open for 23% of the time, Pallas kernels for 48%

profile of v2, /device:TPU:1, one launch (start us, length us, event | category | flops | bytes accessed | tf_op | source)
XLA Modules:
  0.0 475.9 jit_solution(15584040362485265174)
XLA Ops:
  15.7 48.6 %gather_weights.1 = (bf16[2,8,8,16,1664]{4,3,2,1,0:T(8,128)(2,1)}, bf16[16,32,256]{2,1,0:T(8,128)(2,1)}) custom-call(f32[2,8,1664]{2,1,0:T(8,128)} %maximum_convert_fusion.in_ref, bf16[32,256]{1,0:T(8,128)(2,1)} %convert_bitcast_fusion.2.mask_ref), custom_call_target="tpu_custom_call" | custom-call | tf_op jit(solution)/shard_map/gather_weights/pallas_call | solution.py:462
  64.3 1.0 slice.196
  66.8 2.7 slice_bitcast_fusion.1
  69.5 1.3 fusion.1
  71.6 1.3 copy-done.7
  72.9 1.0 slice.200
  74.9 0.8 reshape_squeeze.3
  77.4 1.6 copy.210
  79.0 0.9 slice_convert_fusion.1
  82.7 1.0 multiply_multiply_fusion
  84.2 1.5 maximum_bitcast_fusion.in_ref
  85.6 15.3 %swap.4 = bf16[8,256,256]{2,1,0:T(8,128)(2,1)} custom-call(bf16[8,256,256]{2,1,0:T(8,128)(2,1)} %maximum_bitcast_fusion.in_ref), custom_call_target="tpu_custom_call" | custom-call | tf_op jit(solution)/shard_map/swap/pallas_call | solution.py:501
  101.0 17.5 %attend.1 = (bf16[2048,128]{1,0:T(8,128)(2,1)}, f32[2048,128]{1,0:T(8,128)}, f32[2048,128]{1,0:T(8,128)}) custom-call(bf16[2048,256]{1,0:T(8,128)(2,1)} %bitcast.126), custom_call_target="tpu_custom_call" | custom-call | flops 2147483648 | bytes 4194304 | tf_op jit(solution)/shard_map/attend/pallas_call | solution.py:108
  118.4 9.8 %swap.5 = bf16[8,256,128]{2,1,0:T(8,128)(2,1)} custom-call(bf16[8,256,128]{2,1,0:T(8,128)(2,1)} %bitcast.133), custom_call_target="tpu_custom_call" | custom-call | tf_op jit(solution)/shard_map/swap/pallas_call | solution.py:501
  128.2 1.2 copy.218
  129.5 1.9 slice_bitcast_fusion.3
  131.4 0.8 multiply_reduce_fusion.5
  134.0 0.9 multiply_convert_fusion.x_ref
  135.0 114.4 %moe.1 = (f32[256,1024]{1,0:T(8,128)}, f32[256,128]{1,0:T(8,128)}, bf16[16,256,1024]{2,1,0:T(8,128)(2,1)}, bf16[2,1024,1536]{2,1,0:T(8,128)(2,1)}) custom-call(bf16[256,1024]{1,0:T(8,128)(2,1)} %multiply_convert_fusion.x_ref, bf16[16,256,1024]{2,1,0:T(8,128)(2,1)} %all-gather.2.cloned.1.call-done.g_ref, bf16[16,32,256]{2,1,0:T(8,128)(2,1)} %get-tuple-element.32.masks_ref, ...), custom_call_target="tpu_custom_call" | custom-call | flops 32000000000 | bytes 41943040 | tf_op jit(solution)/shard_map/moe/pallas_call | solution.py:774
  250.9 1.0 copy.232
  252.7 1.0 copy.233
  254.4 1.7 copy.225
  256.3 1.4 copy.226
  259.1 1.7 multiply_reduce_fusion.1
  260.9 1.1 convert_add_fusion.1
  262.4 1.5 fusion.3
  263.9 1.2 copy.221
  265.2 1.0 copy.222
  266.2 17.3 %swap.6 = bf16[8,256,128]{2,1,0:T(8,128)(2,1)} custom-call(bf16[8,256,128]{2,1,0:T(8,128)(2,1)} %bitcast.120), custom_call_target="tpu_custom_call" | custom-call | tf_op jit(solution)/shard_map/swap/pallas_call | solution.py:501
  283.5 61.9 %attend_back.1 = (bf16[2048,128]{1,0:T(8,128)(2,1)}, bf16[2048,128]{1,0:T(8,128)(2,1)}, f32[256,1024]{1,0:T(8,128)}) custom-call(bf16[2048,256]{1,0:T(8,128)(2,1)} %bitcast.127, f32[2048,128]{1,0:T(8,128)} %get-tuple-element.28.full_ref, f32[2048,128]{1,0:T(8,128)} %get-tuple-element.29.logs_ref, bf16[2048,128]{1,0:T(8,128)(2,1)} %bitcast.132, ...), custom_call_target="tpu_custom_call" | custom-call | flops 5368709120 | bytes 16777216 | tf_op jit(solution)/shard_map/attend_back/pallas_call | solution.py:337
  345.4 2.3 pad_maximum_fusion.11
  347.8 16.1 %swap.7 = bf16[8,256,256]{2,1,0:T(8,128)(2,1)} custom-call(bf16[8,256,256]{2,1,0:T(8,128)(2,1)} %bitcast.107), custom_call_target="tpu_custom_call" | custom-call | tf_op jit(solution)/shard_map/swap/pallas_call | solution.py:501
  363.9 2.2 convert_bitcast_fusion.1
  366.1 1.2 copy.236
  367.4 0.9 copy.237
  368.2 1.4 multiply_subtract_fusion
  369.6 1.5 multiply_reduce_fusion.2
  371.1 2.4 copy.230
  373.6 2.0 copy.231
  375.6 0.8 mul.581
  376.4 2.0 copy.235
  378.5 1.0 convert_bitcast_fusion
  379.5 2.6 copy.223
  382.2 1.3 multiply_subtract_fusion.1
  383.5 1.1 pad_maximum_fusion.12
  384.6 2.5 copy.224
  387.2 1.1 mul.560
  388.2 2.5 copy.227
  390.8 1.1 fusion.36
  391.9 2.0 reshape.311
  393.9 2.2 multiply_reduce_fusion.7
  396.3 2.7 multiply_reduce_fusion
  399.7 3.0 fusion.13
  405.1 1.2 concatenate.75
  406.5 0.9 copy.254
  408.2 0.9 copy-done.24
  409.4 1.4 convolution_convert_fusion
  412.0 3.2 pad_maximum_fusion.parts_ref
  415.2 40.6 %reduce_weights.1 = (f32[2,8,1536]{2,1,0:T(8,128)}, f32[8,128]{1,0:T(8,128)}) custom-call(bf16[2,8,8,16,1536]{4,3,2,1,0:T(8,128)(2,1)} %pad_maximum_fusion.parts_ref, f32[2,8,8,8,128]{4,3,2,1,0:T(8,128)} %bitcast.123), custom_call_target="tpu_custom_call" | custom-call | tf_op jit(solution)/shard_map/reduce_weights/pallas_call | solution.py:935
  456.5 1.3 slice.189
  459.8 1.3 fusion.35
  462.6 3.1 fusion.10
  465.7 2.2 slice.223
  467.9 0.9 slice.224
  (213 shorter events, 32.5 us)
Async XLA Ops:
  7.2 58.2 %copy-start.21 = (bf16[1,256,1024]{2,1,0:T(8,128)(2,1)S(1)}, bf16[1,256,1024]{2,1,0:T(8,128)(2,1)}, u32[]{:S(2)}) copy-start(bf16[1,256,1024]{2,1,0:T(8,128)(2,1)} %param.11) | copy-start | bytes 1572868
  7.2 127.8 %all-gather.2.cloned.1.call-start = ((), (), s32[]{:S(2)}) async-start(), calls=%async_computation.1 | async-start | bytes 8912896 | tf_op jit(solution)/shard_map/all_gather | solution.py:1004
  7.9 457.8 %reduce-scatter.2.cloned.1.call-start = ((), (), s32[]{:S(2)}) async-start(), calls=%async_computation.2 | async-start | bytes 7077888 | tf_op jit(solution)/shard_map/reduce_scatter | solution.py:1046
  66.1 3.3 copy-start.63
  66.8 2.7 copy-start.54
  69.4 1.4 copy-start.17
  69.4 2.1 copy-start.19
  71.5 1.4 copy-start.7
  74.9 7.8 %copy-start.4 = (f32[256,8,64]{2,0,1:T(8,128)}, f32[256,8,64]{2,0,1:T(8,128)S(1)}, u32[]{:S(2)}) copy-start(f32[256,8,64]{2,0,1:T(8,128)S(1)} %copy.212) | copy-start | bytes 1572868
  76.6 0.8 copy-start.39
  76.6 0.8 copy-start.31
  79.0 2.7 copy-start
  79.0 2.5 copy-start.32
  79.0 2.5 copy-start.40
  82.0 1.7 copy-start.36
  82.7 1.5 copy-start.47
  129.5 1.9 copy-start.13
  129.5 1.9 copy-start.22
  131.4 1.0 copy-start.25
  131.4 1.4 copy-start.27
  131.4 2.6 copy-start.49
  132.7 1.3 copy-start.2
  133.4 125.1 %copy-start.53 = (f32[256]{0:T(256)}, f32[256]{0:T(256)S(1)}, u32[]{:S(2)}) copy-start(f32[256]{0:T(256)S(1)} %get-tuple-element.97) | copy-start | bytes 3076
  249.4 1.0 copy-start.9
  249.4 1.4 copy-start.48
  250.1 1.8 copy-start.37
  250.1 2.5 copy-start.52
  250.1 3.6 copy-start.56
  252.7 3.5 copy-start.51
  256.2 1.5 copy-start.60
  256.2 1.8 copy-start.15
  256.2 2.9 copy-start.3
  258.0 2.9 copy-start.16
  258.0 2.9 copy-start.50
  258.0 2.9 copy-start.61
  260.8 1.3 copy-start.26
  260.8 1.6 copy-start.28
  368.2 1.4 copy-start.5
  368.2 1.4 copy-start.57
  371.1 7.3 %copy-start.6 = (bf16[8,256,256]{2,1,0:T(8,128)(2,1)S(1)}, bf16[8,256,256]{2,1,0:T(8,128)(2,1)}, u32[]{:S(2)}) copy-start(bf16[8,256,256]{2,1,0:T(8,128)(2,1)} %swap.7) | copy-start | bytes 3145732
  378.5 3.7 copy-start.33
  378.5 3.7 copy-start.38
  379.5 4.0 copy-start.1
  387.2 3.6 copy-start.10
  387.2 3.6 copy-start.30
  388.2 5.7 %copy-start.58 = (f32[512]{0:T(512)S(1)}, f32[512]{0:T(512)}, u32[]{:S(2)}) copy-start(f32[512]{0:T(512)} %mul.570) | copy-start | bytes 6148
  391.9 4.1 copy-start.11
  393.9 2.4 copy-start.8
  396.3 2.7 copy-start.43
  396.3 2.7 copy-start.18
  396.3 3.3 copy-start.20
  396.3 3.3 copy-start.23
  396.3 3.4 copy-start.41
  396.3 3.4 copy-start.55
  396.3 3.4 copy-start.64
  399.0 3.7 copy-start.34
  402.6 4.7 copy-start.14
  408.0 1.0 copy-start.24
  408.0 1.2 copy-start.35
  408.1 1.3 copy-start.42
  408.1 1.3 copy-start.44
  415.2 44.6 %copy-start.65 = (f32[256]{0:T(256)S(1)}, f32[256]{0:T(256)}, u32[]{:S(2)}) copy-start(f32[256]{0:T(256)} %get-tuple-element.45) | copy-start | bytes 3076
  415.2 47.4 %copy-start.62 = (f32[256]{0:T(256)S(1)}, f32[256]{0:T(256)}, u32[]{:S(2)}) copy-start(f32[256]{0:T(256)} %get-tuple-element.94) | copy-start | bytes 3076
  465.7 2.2 copy-start.12
  (4 other events, 2.6 us)
Sparse Core Ops, SparseCore 0:
  10.5 82.8 all-gather.1
  249.6 103.0 reduce-scatter.1

commit v3 on v2

--- a/solution.py
+++ b/solution.py
@@ -1,4 +1,3 @@
-import functools
 import math
 
 import jax
@@ -9,17 +8,19 @@
 from jax.sharding import PartitionSpec as P
 
 D = 1024
-QUERY_HEADS = 16
-KEY_VALUE_HEADS = 8
 HEAD_SIZE = 64
 F = 512
 TOPK = 8
 EXPERTS = 32
+SLOTS = 96
 TOKENS = 256
 SEQ = 8
 FSDP = 16
 LENGTH = SEQ * TOKENS
-QKW = 2048
+GROUP_ROWS = 4 * SLOTS
+ROWS = 4 * GROUP_ROWS
+WIDE = D + 128
+GCOLS = 1536
 VMEM = 60 * 1024 * 1024
 
 epsilon = 1e-06
@@ -28,41 +29,6 @@
 bf16 = jnp.bfloat16
 
 
-def rms_forward(values, weights):
-    scaling = lax.rsqrt(jnp.mean(values * values, axis=-1, keepdims=True) + epsilon)
-    return (values * scaling * weights, scaling)
-
-
-def rms_backward(values, scaling, weights, incoming):
-    weighted = incoming * weights
-    scaling_cube = scaling * scaling * scaling
-    result = scaling * weighted - values * scaling_cube * jnp.mean(
-        weighted * values, axis=-1, keepdims=True
-    )
-    return (result, incoming * values * scaling)
-
-
-def rotary_tables(positions, head_dim):
-    half_dim = head_dim // 2
-    freq_index = jnp.arange(half_dim, dtype=f32)
-    inverse = jnp.exp(-(2.0 * freq_index / head_dim) * math.log(rope_base))
-    angles = positions.astype(f32)[:, None] * inverse[None, :]
-    return (jnp.cos(angles)[:, None, :], jnp.sin(angles)[:, None, :])
-
-
-def rotate(values, cosine_values, sine_values):
-    half_dim = values.shape[-1] // 2
-    first_half = values[..., :half_dim]
-    second_half = values[..., half_dim:]
-    return jnp.concatenate(
-        [
-            first_half * cosine_values - second_half * sine_values,
-            second_half * cosine_values + first_half * sine_values,
-        ],
-        axis=-1,
-    )
-
-
 def dot(a, b):
     return lax.dot_general(a, b, (((1,), (0,)), ((), ())), preferred_element_type=f32)
 
@@ -73,72 +39,6 @@
 
 def t_dot(a, b):
     return lax.dot_general(a, b, (((0,), (0,)), ((), ())), preferred_element_type=f32)
-
-
-def attend_kernel(heads_ref, out_ref, full_ref, logs_ref, key0, key1, value):
-    step = pl.program_id(0)
-    lanes = lax.broadcasted_iota(jnp.int32, (1, 128), 1)
-    low_half = lanes < HEAD_SIZE
-
-    @pl.when(step == 0)
-    def _():
-        pair = heads_ref[:, 128:256].astype(f32)
-        key0[...] = jnp.where(low_half, pair, 0.0).astype(bf16)
-        key1[...] = jnp.where(low_half, 0.0, pltpu.roll(pair, 64, 1)).astype(bf16)
-        value[...] = jnp.where(low_half, jnp.where(lanes == 0, 1.0, 0.0), pair).astype(bf16)
-
-    rows = pl.multiple_of(step * TOKENS, TOKENS)
-    query = (heads_ref[pl.ds(rows, TOKENS), 0:128].astype(f32) * (1.0 / 8.0)).astype(bf16)
-    results = []
-    for key in (key0, key1):
-        total = jnp.zeros((TOKENS, 128), f32)
-        for c in range(4):
-            part = pl.ds(c * 512, 512)
-            weights = jnp.exp(dot_t(query, key[part, :]))
-            total = total + dot(weights.astype(bf16), value[part, :])
-        results.append(total)
-    sum0, sum1 = results[0][:, 0:1], results[1][:, 0:1]
-    full = jnp.where(low_half, pltpu.roll(results[0] / sum0, 64, 1), results[1] / sum1)
-    full_ref[...] = full
-    out_ref[...] = full.astype(bf16)
-    logs_ref[...] = jnp.where(low_half, jnp.log(sum0), jnp.log(sum1))
-
-
-def attend(heads):
-    return pl.pallas_call(
-        attend_kernel,
-        grid=(LENGTH // TOKENS,),
-        in_specs=[pl.BlockSpec((LENGTH, 256), lambda i: (0, 0))],
-        out_specs=[pl.BlockSpec((TOKENS, 128), lambda i: (i, 0))] * 3,
-        out_shape=[
-            jax.ShapeDtypeStruct((LENGTH, 128), bf16),
-            jax.ShapeDtypeStruct((LENGTH, 128), f32),
-            jax.ShapeDtypeStruct((LENGTH, 128), f32),
-        ],
-        scratch_shapes=[pltpu.VMEM((LENGTH, 128), bf16)] * 3,
-        compiler_params=pltpu.CompilerParams(vmem_limit_bytes=VMEM),
-        cost_estimate=pl.CostEstimate(
-            flops=4 * LENGTH * LENGTH * 128, bytes_accessed=4 << 20, transcendentals=2 * LENGTH * LENGTH
-        ),
-        name="attend",
-    )(heads)
-
-
-def split3(values):
-    high = values.astype(bf16).astype(f32)
-    rest = values - high
-    middle = rest.astype(bf16).astype(f32)
-    return high, middle, rest - middle
-
-
-def with_terms(lanes, start, parts):
-    high, middle, low = parts
-    tail = jnp.where(
-        lanes == start,
-        high,
-        jnp.where(lanes == start + 1, middle, jnp.where(lanes == start + 2, low, 0.0)),
-    )
-    return tail
 
 
 MESH = pl.DeviceIdType.MESH
@@ -203,42 +103,369 @@
             copy.wait_send()
 
 
+OTHERS = ((2, 1), (2, 0), (0, 1), (1, 1), (-1, 1), (1, 0), (-1, 0))
 WCOLS = 1664
 
-def attend_back_kernel(
-    heads_ref, full_ref, logs_ref, grad_ref, y_ref, dq_ref, dkv_ref, sum_ref,
+
+def lane_halves():
+    lanes = lax.broadcasted_iota(jnp.int32, (1, 128), 1)
+    return lanes, lanes < HEAD_SIZE
+
+
+def head_mean(values, low_half):
+    low = jnp.sum(jnp.where(low_half, values, 0.0), axis=1, keepdims=True)
+    high = jnp.sum(jnp.where(low_half, 0.0, values), axis=1, keepdims=True)
+    return jnp.where(low_half, low, high) * (1.0 / HEAD_SIZE)
+
+
+def partner(values, lanes):
+    return jnp.where(
+        lax.rem(lanes, HEAD_SIZE) < HEAD_SIZE // 2, pltpu.roll(values, 96, 1), pltpu.roll(values, 32, 1)
+    )
+
+
+def row_scale(values):
+    return lax.rsqrt(jnp.mean(values * values, axis=1, keepdims=True) + epsilon)
+
+
+def gain_tiles(small_t, lanes):
+    pick = (
+        lax.broadcasted_iota(jnp.int32, (D, 128), 0) == 8 * lax.broadcasted_iota(jnp.int32, (D, 128), 1)
+    ).astype(f32).astype(bf16)
+    gains = dot(small_t[32:48, :], pick)[2:3, :]
+    other = pltpu.roll(gains, 64, 1)
+    low_half = lanes < HEAD_SIZE
+    return jnp.where(low_half, gains, other), jnp.where(low_half, other, gains)
+
+
+def front_kernel(
+    x_ref, w_ref, routes_ref, cos_ref, sin_ref,
+    heads_out, full_ref, logs_ref, att_ref, after_ref, normed_ref, gates_ref, small_t_ref, raw_ref,
+    wq, wkv, wo, small, send, heads, out_buf, att, key0, key1, value,
+    local_sems, send_sems, recv_sems,
+):
+    here = Place()
+    me = here.seq
+    loads = [
+        pltpu.make_async_copy(w_ref.at[h, :, pl.ds(start, width)], there, local_sems.at[k])
+        for k, (h, start, width, there) in enumerate(
+            (
+                (0, 1536, 128, small),
+                (0, 0, 1024, wq),
+                (1, 0, 1024, wkv),
+                (0, 1024, 512, wo.at[0]),
+                (1, 1024, 512, wo.at[1]),
+            )
+        )
+    ]
+    for copy in loads:
+        copy.start()
+    peers = [here.seq_at(*other) for other in OTHERS]
+    meet([{"seq": peer} for peer in peers])
+    net = Copies(send_sems, recv_sems)
+    lanes, low_half = lane_halves()
+    loads[0].wait()
+    small_t = jnp.transpose(small[...].astype(f32)).astype(bf16)
+    small_t_ref[...] = small_t
+    x = x_ref[...].astype(f32)
+    normed = (x * row_scale(x) * small_t[32:33, :].astype(f32)).astype(bf16)
+    query_gain, key_gain = gain_tiles(small_t, lanes)
+    cos, sin = cos_ref[...], sin_ref[...]
+    loads[1].wait()
+    raw_ref[:, 0:1024] = dot(normed, wq[...])
+    loads[2].wait()
+    kv = dot(normed, wkv[...])
+    raw_ref[:, 1024:1536] = kv[:, 0:512]
+
+    def turned(tile, gain):
+        normal = tile * lax.rsqrt(head_mean(tile * tile, low_half) + epsilon) * gain
+        return normal * cos + partner(normal, lanes) * sin
+
+    for j in range(4):
+        part = slice(128 * j, 128 * (j + 1))
+        keys = turned(kv[:, part], key_gain)
+        values = kv[:, 512 + 128 * j : 640 + 128 * j]
+        send[2 * j, :, 128:256] = jnp.where(low_half, keys, pltpu.roll(values, 64, 1)).astype(bf16)
+        send[2 * j + 1, :, 128:256] = jnp.where(low_half, pltpu.roll(keys, 64, 1), values).astype(bf16)
+    for h in range(8):
+        send[h, :, 0:128] = turned(raw_ref[:, 128 * h : 128 * (h + 1)], query_gain).astype(bf16)
+    copies = [net.start(send.at[peer], heads.at[me], {"seq": peer}) for peer in peers]
+    heads[me] = send[me]
+    for copy in copies:
+        copy.wait_recv()
+    save = pltpu.make_async_copy(heads, heads_out, local_sems.at[5])
+    save.start()
+    for c in range(8):
+        rows = slice(TOKENS * c, TOKENS * (c + 1))
+        pair = heads[c, :, 128:256].astype(f32)
+        key0[rows, :] = jnp.where(low_half, pair, 0.0).astype(bf16)
+        key1[rows, :] = jnp.where(low_half, 0.0, pltpu.roll(pair, 64, 1)).astype(bf16)
+        value[rows, :] = jnp.where(low_half, jnp.where(lanes == 0, 1.0, 0.0), pair).astype(bf16)
+
+    def block(i, carry):
+        j = lax.rem(me + 1 + i, 8)
+        query = (heads[j, :, 0:128].astype(f32) * (1.0 / 8.0)).astype(bf16)
+        results = []
+        for key in (key0, key1):
+            total = jnp.zeros((TOKENS, 128), f32)
+            for c in range(4):
+                part = pl.ds(c * 512, 512)
+                weights = jnp.exp(dot_t(query, key[part, :]))
+                total = total + dot(weights.astype(bf16), value[part, :])
+            results.append(total)
+        sum0, sum1 = results[0][:, 0:1], results[1][:, 0:1]
+        full = jnp.where(low_half, pltpu.roll(results[0] / sum0, 64, 1), results[1] / sum1)
+        rows = pl.ds(pl.multiple_of(j * TOKENS, TOKENS), TOKENS)
+        full_ref[rows, :] = full
+        logs_ref[rows, :] = jnp.where(low_half, jnp.log(sum0), jnp.log(sum1))
+        out_buf[j] = full.astype(bf16)
+
+        @pl.when(i < 7)
+        def _():
+            answer(i).start()
+
+        return carry
+
+    columns = pl.ds(pl.multiple_of(me * 128, 128), 128)
+
+    def answer(i):
+        j = lax.rem(me + 1 + i, 8)
+        return pltpu.make_async_remote_copy(
+            src_ref=out_buf.at[j], dst_ref=att.at[:, columns], send_sem=send_sems.at[7 + i],
+            recv_sem=recv_sems.at[7 + i], device_id={"seq": j}, device_id_type=MESH,
+        )
+
+    lax.fori_loop(0, 8, block, 0)
+    att[:, columns] = out_buf[me]
+    for k in (3, 4):
+        loads[k].wait()
+    for i in range(7):
+        answer(i).wait_recv()
+    attended = att[...]
+    att_ref[...] = attended
+    squares = jnp.zeros((TOKENS, 1), f32)
+    for h in range(2):
+        part = slice(512 * h, 512 * (h + 1))
+        after = x_ref[:, part].astype(f32) + dot(attended, wo[h])
+        after_ref[:, part] = after
+        squares = squares + jnp.sum(after * after, axis=1, keepdims=True)
+    scaling = lax.rsqrt(squares * (1.0 / D) + epsilon)
+    normed = (after_ref[...] * scaling * small_t[33:34, :].astype(f32)).astype(bf16)
+    normed_ref[...] = normed
+    logits = dot(normed, small[...])
+    named = jnp.zeros((TOKENS, 128), f32)
+    for k in range(TOPK):
+        named = jnp.where(routes_ref[:, k : k + 1] == lanes, 1.0, named)
+    peak = jnp.max(jnp.where(named > 0.0, logits, -1e30), axis=1, keepdims=True)
+    chosen = jnp.where(named > 0.0, jnp.exp(logits - peak), 0.0)
+    gates_ref[...] = chosen / jnp.sum(chosen, axis=1, keepdims=True)
+    save.wait()
+    for i in range(7):
+        answer(i).wait_send()
+    net.finish()
+
+
+def front(x, whole, routes, cos, sin):
+    vmem = pl.BlockSpec(memory_space=pltpu.VMEM)
+    hbm = pl.BlockSpec(memory_space=pl.ANY)
+    return pl.pallas_call(
+        front_kernel,
+        in_specs=[vmem, hbm, vmem, vmem, vmem],
+        out_specs=[hbm] + [vmem] * 8,
+        out_shape=[
+            jax.ShapeDtypeStruct((8, TOKENS, 256), bf16),
+            jax.ShapeDtypeStruct((LENGTH, 128), f32),
+            jax.ShapeDtypeStruct((LENGTH, 128), f32),
+            jax.ShapeDtypeStruct((TOKENS, D), bf16),
+            jax.ShapeDtypeStruct((TOKENS, D), f32),
+            jax.ShapeDtypeStruct((TOKENS, D), bf16),
+            jax.ShapeDtypeStruct((TOKENS, 128), f32),
+            jax.ShapeDtypeStruct((128, D), bf16),
+            jax.ShapeDtypeStruct((TOKENS, 1536), f32),
+        ],
+        scratch_shapes=[
+            pltpu.VMEM((D, 1024), bf16),
+            pltpu.VMEM((D, 1024), bf16),
+            pltpu.VMEM((2, D, 512), bf16),
+            pltpu.VMEM((D, 128), bf16),
+            pltpu.VMEM((8, TOKENS, 256), bf16),
+            pltpu.VMEM((8, TOKENS, 256), bf16),
+            pltpu.VMEM((8, TOKENS, 128), bf16),
+            pltpu.VMEM((TOKENS, D), bf16),
+            pltpu.VMEM((LENGTH, 128), bf16),
+            pltpu.VMEM((LENGTH, 128), bf16),
+            pltpu.VMEM((LENGTH, 128), bf16),
+            pltpu.SemaphoreType.DMA((6,)),
+            pltpu.SemaphoreType.DMA((14,)),
+            pltpu.SemaphoreType.DMA((14,)),
+        ],
+        compiler_params=pltpu.CompilerParams(collective_id=2, has_side_effects=True, vmem_limit_bytes=VMEM),
+        cost_estimate=pl.CostEstimate(
+            flops=4 * 10**9, bytes_accessed=16 << 20, transcendentals=2 * LENGTH * LENGTH
+        ),
+        name="front",
+    )(x, whole, routes, cos, sin)
+
+
+def split3(values):
+    high = values.astype(bf16).astype(f32)
+    rest = values - high
+    middle = rest.astype(bf16).astype(f32)
+    return high, middle, rest - middle
+
+
+def with_terms(lanes, start, parts):
+    high, middle, low = parts
+    return jnp.where(
+        lanes == start,
+        high,
+        jnp.where(lanes == start + 1, middle, jnp.where(lanes == start + 2, low, 0.0)),
+    )
+
+
+def back_kernel(
+    row_ref, gate_sum_ref, gates_ref, after_ref, x_ref, cot_ref, att_ref, normed_ref, small_t_ref, raw_ref,
+    heads_ref, full_ref, logs_ref, cos_ref, sin_ref, w_ref, y_ref,
+    layer_ref, token_ref, parts_ref, small_ref,
+    wq, wkv, wo, send, grads, dq_buf, dkv_buf, back_q, back_kv, pg_q, pg_kv, after_grad,
     key0, key1, value0, value1, key_t, dk_total, dv_total,
     slots, sib_in, hop_in, local_sems, send_sems, recv_sems,
 ):
     here = Place()
+    me = here.seq
     sib = here.sibling()
     way = here.plane("fsdp")
     loads = [
-        pltpu.make_async_copy(y_ref.at[2 * k], slots.at[k], local_sems.at[k]) for k in (6, 7, 5, 3, 4, 2, 1, 0)
+        pltpu.make_async_copy(w_ref.at[h, :, pl.ds(start, width)], there, local_sems.at[k])
+        for k, (h, start, width, there) in enumerate(
+            ((0, 1024, 512, wo.at[0]), (1, 1024, 512, wo.at[1]), (0, 0, 1024, wq), (1, 0, 1024, wkv))
+        )
     ]
     for copy in loads:
         copy.start()
-    meet([sib, *way.values()])
+    order = (6, 7, 3, 5, 2, 4, 1, 0)
+    y_loads = {k: pltpu.make_async_copy(y_ref.at[2 * k], slots.at[k], local_sems.at[4 + k]) for k in order}
+    for copy in y_loads.values():
+        copy.start()
+    peers = [here.seq_at(*other) for other in OTHERS]
+    meet([sib, *way.values()] + [{"seq": peer} for peer in peers])
     net = Copies(send_sems, recv_sems)
-    joins = {k: net.start(y_ref.at[2 * k + 1], sib_in.at[k], sib) for k in (7, 6, 5, 3, 4, 2, 1, 0)}
-    lanes = lax.broadcasted_iota(jnp.int32, (1, 128), 1)
-    low_half = lanes < HEAD_SIZE
-    pair = heads_ref[:, 128:256].astype(f32)
-    swapped = pltpu.roll(pair, 64, 1)
+    joins = {k: net.start(y_ref.at[2 * k + 1], sib_in.at[k], sib) for k in order}
+    lanes, low_half = lane_halves()
+
+    gate_sum = gate_sum_ref[...]
+    gate_grad = gate_sum + pltpu.roll(gate_sum, 96, 1)
+    gates = gates_ref[...]
+    gate_grad = jnp.where(lanes < EXPERTS, gate_grad, 0.0)
+    chosen = gates * (gate_grad - jnp.sum(gates * gate_grad, axis=1, keepdims=True))
+    logits_grad = chosen.astype(bf16)
+    normed_grad = row_ref[...] + dot(logits_grad, small_t_ref[...])
+    after = after_ref[...]
+    scaling = row_scale(after)
+    weighted = normed_grad * small_t_ref[33:34, :].astype(f32)
+    middle = jnp.mean(weighted * after, axis=1, keepdims=True)
+    total = cot_ref[...].astype(f32) + scaling * weighted - after * (scaling * scaling * scaling * middle)
+    after_grad[...] = total
+    after_low = total.astype(bf16)
+    ffn_gain = jnp.sum(normed_grad * after * scaling, axis=0, keepdims=True)
+    for k in (0, 1):
+        loads[k].wait()
+    for q in range(2):
+        rows = slice(512 * q, 512 * (q + 1))
+        attended_grad = dot_t(after_low[:, 0:512], wo[0, rows, :]) + dot_t(after_low[:, 512:1024], wo[1, rows, :])
+        for h in range(4):
+            send[4 * q + h] = attended_grad[:, 128 * h : 128 * (h + 1)].astype(bf16)
+    to_heads = [net.start(send.at[peer], grads.at[me], {"seq": peer}) for peer in peers]
+    grads[me] = send[me]
+    small_ref[...] = t_dot(normed_ref[...], logits_grad)
+    for h in range(2):
+        parts_ref[h, :, 1024:1536] = t_dot(att_ref[...], after_low[:, 512 * h : 512 * (h + 1)]).astype(bf16)
+
+    def add_to(ref, *values):
+        result = ref[...].astype(f32)
+        for value in values:
+            result = result + value[...].astype(f32)
+        ref[...] = result.astype(bf16)
+
+    def join(k):
+        y_loads[k].wait()
+        joins[k].wait_recv()
+        add_to(slots.at[k], sib_in.at[k])
+
+    def half(ref, which):
+        return ref.at[pl.ds(128 * which, 128)]
+
+    def expert_sum():
+        join(6)
+        join(7)
+        up = [net.start(half(slots.at[6 + j], 0), half(hop_in.at[j], 0), way["up"]) for j in range(2)]
+        down = [net.start(half(slots.at[6 + j], 1), half(hop_in.at[j], 1), way["down"]) for j in range(2)]
+        yield
+        for k in (3, 5, 2, 4):
+            join(k)
+        up[1].wait_recv()
+        down[1].wait_recv()
+        add_to(half(slots.at[5], 0), half(hop_in.at[1], 0))
+        add_to(half(slots.at[3], 1), half(hop_in.at[1], 1))
+        beside = [
+            net.start(slots.at[5], hop_in.at[2], way["up"]), net.start(slots.at[3], hop_in.at[3], way["down"])
+        ]
+        up[0].wait_recv()
+        down[0].wait_recv()
+        add_to(half(slots.at[4], 0), half(hop_in.at[0], 0))
+        add_to(half(slots.at[2], 1), half(hop_in.at[0], 1))
+        own = [
+            net.start(slots.at[4], hop_in.at[4], way["up"]), net.start(slots.at[2], hop_in.at[5], way["down"])
+        ]
+        yield
+        join(1)
+        join(0)
+        for copy in beside:
+            copy.wait_recv()
+        add_to(slots.at[1], hop_in.at[2], hop_in.at[3])
+        own.append(net.start(slots.at[1], hop_in.at[6], way["across"]))
+        yield
+        for copy in own:
+            copy.wait_recv()
+        layer_ref[...] = (
+            after_ref[...]
+            + slots[0].astype(f32)
+            + hop_in[4].astype(f32)
+            + hop_in[5].astype(f32)
+            + hop_in[6].astype(f32)
+        ).astype(bf16)
+
+    moves = expert_sum()
+    next(moves)
     ones_high = jnp.where((lanes >= 64) & (lanes < 67), 1.0, 0.0)
     ones_low = jnp.where(lanes < 3, 1.0, 0.0)
-    key0[...] = jnp.where(low_half, pair, ones_high).astype(bf16)
-    key1[...] = jnp.where(low_half, ones_low, swapped).astype(bf16)
-    value0[...] = jnp.where(low_half, swapped, ones_high).astype(bf16)
-    value1[...] = jnp.where(low_half, ones_low, pair).astype(bf16)
-    key_t[...] = jnp.transpose(pair)[0:64, :].astype(bf16)
+    for c in range(8):
+        rows = slice(TOKENS * c, TOKENS * (c + 1))
+        pair = heads_ref[c, :, 128:256].astype(f32)
+        swapped = pltpu.roll(pair, 64, 1)
+        key0[rows, :] = jnp.where(low_half, pair, ones_high).astype(bf16)
+        key1[rows, :] = jnp.where(low_half, ones_low, swapped).astype(bf16)
+        value0[rows, :] = jnp.where(low_half, swapped, ones_high).astype(bf16)
+        value1[rows, :] = jnp.where(low_half, ones_low, pair).astype(bf16)
+        key_t[:, rows] = jnp.transpose(pair)[0:64, :].astype(bf16)
     dk_total[...] = jnp.zeros_like(dk_total)
     dv_total[...] = jnp.zeros_like(dv_total)
-
-    def one(step, carry):
-        rows = pl.ds(pl.multiple_of(step * TOKENS, TOKENS), TOKENS)
-        query = heads_ref[rows, 0:128].astype(f32) * (1.0 / 8.0)
-        grad = grad_ref[rows, :].astype(f32)
+    for copy in to_heads:
+        copy.wait_recv()
+    columns = pl.ds(pl.multiple_of(me * 128, 128), 128)
+
+    def answer(i):
+        j = lax.rem(me + 1 + i, 8)
+        return pltpu.make_async_remote_copy(
+            src_ref=dq_buf.at[j], dst_ref=back_q.at[:, columns], send_sem=send_sems.at[32 + i],
+            recv_sem=recv_sems.at[32 + i], device_id={"seq": j}, device_id_type=MESH,
+        )
+
+    def block(i, carry):
+        j = lax.rem(me + 1 + i, 8)
+        rows = pl.ds(pl.multiple_of(j * TOKENS, TOKENS), TOKENS)
+        query = heads_ref[j, :, 0:128].astype(f32) * (1.0 / 8.0)
+        grad = grads[j].astype(f32)
         logs = logs_ref[rows, :]
         product = grad * full_ref[rows, :]
         delta0 = jnp.sum(jnp.where(low_half, product, 0.0), axis=1, keepdims=True)
@@ -268,97 +495,140 @@
             dv_total[part, :] = dv
             dk_total[part, :] = dk
         both = jnp.concatenate(dq, axis=0) * (1.0 / 8.0)
-        dq_ref[rows, :] = jnp.transpose(both).astype(bf16)
+        dq_buf[j] = jnp.transpose(both).astype(bf16)
+
+        @pl.when(i < 7)
+        def _():
+            answer(i).start()
+
         return carry
 
-    def run(first, last):
-        lax.fori_loop(first, last, one, 0)
-
-    def add_to(ref, *values):
-        result = ref[...].astype(f32)
-        for value in values:
-            result = result + value[...].astype(f32)
-        ref[...] = result.astype(bf16)
-
-    def join(k):
-        joins[k].wait_recv()
-        add_to(slots.at[k], sib_in.at[k])
-
-    def half(ref, which):
-        return ref.at[pl.ds(128 * which, 128)]
-
-    run(0, 1)
-    for copy in loads:
+    lax.fori_loop(0, 3, block, 0)
+    next(moves)
+    lax.fori_loop(3, 6, block, 0)
+    next(moves)
+    lax.fori_loop(6, 8, block, 0)
+    for c in range(8):
+        rows = slice(TOKENS * c, TOKENS * (c + 1))
+        dk = dk_total[rows, :]
+        dv = dv_total[rows, :]
+        dk = dk + pltpu.roll(dk, 64, 1)
+        dv = dv + pltpu.roll(dv, 64, 1)
+        dkv_buf[c] = jnp.where(low_half, dk, dv).astype(bf16)
+    to_tokens = [net.start(dkv_buf.at[peer], back_kv.at[me], {"seq": peer}) for peer in peers]
+    back_kv[me] = dkv_buf[me]
+    back_q[:, columns] = dq_buf[me]
+    x = x_ref[...].astype(f32)
+    x_scaling = row_scale(x)
+    attn_gain = small_t_ref[32:33, :].astype(f32)
+    normed = (x * x_scaling * attn_gain).astype(bf16)
+    query_gain, key_gain = gain_tiles(small_t_ref[...], lanes)
+    cos, sin = cos_ref[...], sin_ref[...]
+    for i in range(7):
+        answer(i).wait_recv()
+
+    def unturned(grad, tile, gain):
+        grad = grad * cos - partner(grad, lanes) * sin
+        scale = lax.rsqrt(head_mean(tile * tile, low_half) + epsilon)
+        weighted = grad * gain
+        middle = head_mean(weighted * tile, low_half)
+        result = scale * weighted - tile * (scale * scale * scale * middle)
+        return result.astype(bf16), jnp.sum(grad * tile * scale, axis=0, keepdims=True)
+
+    query_terms = jnp.zeros((1, 128), f32)
+    for h in range(8):
+        part = slice(128 * h, 128 * (h + 1))
+        pg_q[:, part], terms = unturned(back_q[:, part].astype(f32), raw_ref[:, part], query_gain)
+        query_terms = query_terms + terms
+    for copy in loads[2:]:
         copy.wait()
-    join(7)
-    a = net.start(slots.at[7], hop_in.at[0], way["across"])
-    join(3)
-    xd = net.start(slots.at[3], hop_in.at[2], way["down"])
-    join(5)
-    xu = net.start(slots.at[5], hop_in.at[3], way["up"])
-    join(6)
-    run(1, 4)
-    a.wait_recv()
-    add_to(slots.at[6], hop_in.at[0])
-    u = net.start(half(slots.at[6], 0), half(hop_in.at[1], 0), way["up"])
-    d = net.start(half(slots.at[6], 1), half(hop_in.at[1], 1), way["down"])
-    join(1)
-    xd.wait_recv()
-    xu.wait_recv()
-    add_to(slots.at[1], hop_in.at[2], hop_in.at[3])
-    rx = net.start(slots.at[1], hop_in.at[6], way["across"])
-    join(2)
-    join(4)
-    join(0)
-    run(4, 6)
-    u.wait_recv()
-    add_to(half(slots.at[4], 0), half(hop_in.at[1], 0))
-    ru = net.start(slots.at[4], hop_in.at[4], way["up"])
-    d.wait_recv()
-    add_to(half(slots.at[2], 1), half(hop_in.at[1], 1))
-    rd = net.start(slots.at[2], hop_in.at[5], way["down"])
-    run(6, 8)
-    dk = dk_total[...]
-    dv = dv_total[...]
-    dk = dk + pltpu.roll(dk, 64, 1)
-    dv = dv + pltpu.roll(dv, 64, 1)
-    dkv_ref[...] = jnp.where(low_half, dk, dv).astype(bf16)
-    rx.wait_recv()
-    ru.wait_recv()
-    rd.wait_recv()
-    sum_ref[...] = (
-        slots[0].astype(f32) + hop_in[4].astype(f32) + hop_in[5].astype(f32) + hop_in[6].astype(f32)
+    for r in range(4):
+        part = slice(256 * r, 256 * (r + 1))
+        parts_ref[0, part, 0:1024] = t_dot(normed[:, part], pg_q[...]).astype(bf16)
+    normed_grad = dot_t(pg_q[...], wq[...])
+    for copy in to_tokens:
+        copy.wait_recv()
+    key_terms = jnp.zeros((1, 128), f32)
+    for j in range(4):
+        first, second = back_kv[2 * j].astype(f32), back_kv[2 * j + 1].astype(f32)
+        keys = jnp.where(low_half, first, pltpu.roll(second, 64, 1))
+        values = jnp.where(low_half, pltpu.roll(first, 64, 1), second)
+        part = slice(128 * j, 128 * (j + 1))
+        pg_kv[:, part], terms = unturned(keys, raw_ref[:, 1024 + 128 * j : 1152 + 128 * j], key_gain)
+        key_terms = key_terms + terms
+        pg_kv[:, 512 + 128 * j : 640 + 128 * j] = values.astype(bf16)
+    for r in range(4):
+        part = slice(256 * r, 256 * (r + 1))
+        parts_ref[1, part, 0:1024] = t_dot(normed[:, part], pg_kv[...]).astype(bf16)
+    normed_grad = normed_grad + dot_t(pg_kv[...], wkv[...])
+    weighted = normed_grad * attn_gain
+    middle = jnp.mean(weighted * x, axis=1, keepdims=True)
+    token_ref[...] = after_grad[...] + x_scaling * weighted - x * (x_scaling * x_scaling * x_scaling * middle)
+    attn_gain_grad = jnp.sum(normed_grad * x * x_scaling, axis=0, keepdims=True)
+    query_terms = query_terms + pltpu.roll(query_terms, 64, 1)
+    key_terms = key_terms + pltpu.roll(key_terms, 64, 1)
+    head_terms = jnp.where(low_half, query_terms, key_terms)
+    spread = (
+        8 * lax.broadcasted_iota(jnp.int32, (128, D), 0) == lax.broadcasted_iota(jnp.int32, (128, D), 1)
+    ).astype(f32).astype(bf16)
+    head_row = jnp.zeros((1, D), f32)
+    for term in split3(head_terms):
+        head_row = head_row + dot(jnp.broadcast_to(term, (16, 128)).astype(bf16), spread)[0:1, :]
+    row = lax.broadcasted_iota(jnp.int32, (128, D), 0)
+    gain_rows = jnp.where(
+        row == 32, attn_gain_grad, jnp.where(row == 33, ffn_gain, jnp.where(row == 34, head_row, 0.0))
     )
+    small_ref[...] = small_ref[...] + jnp.transpose(gain_rows)
+    for _ in moves:
+        pass
+    for i in range(7):
+        answer(i).wait_send()
     net.finish()
 
 
-def attend_back(heads, full, logs, grad, y_all):
+def back(*operands):
     vmem = pl.BlockSpec(memory_space=pltpu.VMEM)
+    hbm = pl.BlockSpec(memory_space=pl.ANY)
     return pl.pallas_call(
-        attend_back_kernel,
-        in_specs=[vmem] * 4 + [pl.BlockSpec(memory_space=pl.ANY)],
-        out_specs=[vmem] * 3,
+        back_kernel,
+        in_specs=[vmem] * 15 + [hbm] * 2,
+        out_specs=[vmem] * 4,
         out_shape=[
-            jax.ShapeDtypeStruct((LENGTH, 128), bf16),
-            jax.ShapeDtypeStruct((LENGTH, 128), bf16),
+            jax.ShapeDtypeStruct((TOKENS, D), bf16),
             jax.ShapeDtypeStruct((TOKENS, D), f32),
+            jax.ShapeDtypeStruct((2, D, 1536), bf16),
+            jax.ShapeDtypeStruct((D, 128), f32),
         ],
-        scratch_shapes=[pltpu.VMEM((LENGTH, 128), bf16)] * 4
+        scratch_shapes=[
+            pltpu.VMEM((D, 1024), bf16),
+            pltpu.VMEM((D, 1024), bf16),
+            pltpu.VMEM((2, D, 512), bf16),
+            pltpu.VMEM((8, TOKENS, 128), bf16),
+            pltpu.VMEM((8, TOKENS, 128), bf16),
+            pltpu.VMEM((8, TOKENS, 128), bf16),
+            pltpu.VMEM((8, TOKENS, 128), bf16),
+            pltpu.VMEM((TOKENS, D), bf16),
+            pltpu.VMEM((8, TOKENS, 128), bf16),
+            pltpu.VMEM((TOKENS, D), bf16),
+            pltpu.VMEM((TOKENS, D), bf16),
+            pltpu.VMEM((TOKENS, D), f32),
+        ]
+        + [pltpu.VMEM((LENGTH, 128), bf16)] * 4
         + [pltpu.VMEM((64, LENGTH), bf16)]
         + [pltpu.VMEM((LENGTH, 128), f32)] * 2
         + [pltpu.VMEM((8, TOKENS, D), bf16)] * 2
         + [pltpu.VMEM((7, TOKENS, D), bf16)]
         + [
-            pltpu.SemaphoreType.DMA((8,)),
-            pltpu.SemaphoreType.DMA((18,)),
-            pltpu.SemaphoreType.DMA((18,)),
+            pltpu.SemaphoreType.DMA((12,)),
+            pltpu.SemaphoreType.DMA((40,)),
+            pltpu.SemaphoreType.DMA((40,)),
         ],
-        compiler_params=pltpu.CompilerParams(collective_id=9, has_side_effects=True, vmem_limit_bytes=VMEM),
+        compiler_params=pltpu.CompilerParams(collective_id=5, has_side_effects=True, vmem_limit_bytes=VMEM),
         cost_estimate=pl.CostEstimate(
-            flops=10 * LENGTH * LENGTH * 128, bytes_accessed=16 << 20, transcendentals=2 * LENGTH * LENGTH
+            flops=9 * 10**9, bytes_accessed=32 << 20, transcendentals=2 * LENGTH * LENGTH
         ),
-        name="attend_back",
-    )(heads, full, logs, grad, y_all)
+        name="back",
+    )(*operands)
 
 
 def gather_kernel(in_ref, mask_ref, out_ref, masks_out, stage, block, local_sems, send_sems, recv_sems):
@@ -478,45 +748,6 @@
         name="gather_weights",
     )(halves, mask)
 
-
-def swap_kernel(in_ref, out_ref, local_sem, send_sems, recv_sems):
-    here = Place()
-    others = [(ring, pair) for ring in (0, -1, 1, 2) for pair in (0, 1)][1:]
-    others = [(2, 1), (2, 0), (0, 1), (1, 1), (-1, 1), (1, 0), (-1, 0)]
-    meet([{"seq": here.seq_at(ring, pair)} for ring, pair in others])
-    net = Copies(send_sems, recv_sems)
-    copies = [
-        net.start(in_ref.at[here.seq_at(ring, pair)], out_ref.at[here.seq], {"seq": here.seq_at(ring, pair)})
-        for ring, pair in others
-    ]
-    local = pltpu.make_async_copy(in_ref.at[here.seq], out_ref.at[here.seq], local_sem.at[0])
-    local.start()
-    local.wait()
-    for copy in copies:
-        copy.wait_recv()
-    net.finish()
-
-
-def swap(values, ident):
-    return pl.pallas_call(
-        swap_kernel,
-        in_specs=[pl.BlockSpec(memory_space=pl.ANY)],
-        out_specs=pl.BlockSpec(memory_space=pl.ANY),
-        out_shape=jax.ShapeDtypeStruct(values.shape, values.dtype),
-        scratch_shapes=[
-            pltpu.SemaphoreType.DMA((1,)),
-            pltpu.SemaphoreType.DMA((7,)),
-            pltpu.SemaphoreType.DMA((7,)),
-        ],
-        compiler_params=pltpu.CompilerParams(collective_id=ident, has_side_effects=True),
-        name="swap",
-    )(values)
-
-
-SLOTS=96
-GROUP_ROWS=4*SLOTS
-ROWS=4*GROUP_ROWS
-WIDE=D+128
 
 def moe_kernel(
     x_ref, g_ref, masks_ref, router_ref, up_hbm, down_hbm,
@@ -809,11 +1040,6 @@
         cost_estimate=pl.CostEstimate(flops=32 * 10**9, bytes_accessed=40 << 20, transcendentals=1 << 21),
         name="moe",
     )(x, g_all, masks, router_t, up, down)
-
-
-GCOLS = 1536
-
-
 def reduce_kernel(
     parts_ref, small_ref, out_ref, small_out,
     acc, sib_in, small_acc, small_sib, hop_a, hop_b, late_a, late_b, small_s, small_f, total, local_sems,
@@ -838,10 +1064,10 @@
     joins = [
         net.start(parts_ref.at[1 - c, pl.ds(2 * i, 2)], sib_in.at[pl.ds(2 * i, 2)], sib) for i in range(4)
     ]
-    small_join = net.start(small_ref.at[1 - c], small_sib, sib)
+    small_join = net.start(small_ref.at[:, :, 1 - c], small_sib, sib)
     own.wait()
     small_join.wait_recv()
-    small_acc[...] = small_ref[c] + small_sib[...]
+    small_acc[...] = small_ref[:, :, c] + small_sib[...]
     small_copies = [
         net.start(small_acc.at[here.seq_at(*others[i])], small_s.at[i], seq_peers[i]) for i in range(7)
     ]
@@ -962,13 +1188,8 @@
     tokens, attn_gain, qkv_weight, qk_gain, out_weight, ffn_gain, router_weight,
     gate_up_weight, down_weight, routes, cotangent,
 ):
-    layer_inputs = tokens.reshape(TOKENS, D).astype(f32)
-    query_total_width = QUERY_HEADS * HEAD_SIZE
-    key_total_width = KEY_VALUE_HEADS * HEAD_SIZE
-    seq_place = lax.axis_index("seq")
-
-    fsdp_place = lax.axis_index("fsdp")
-    core = fsdp_place % 2
+    x = tokens.reshape(TOKENS, D)
+    cot = cotangent.reshape(TOKENS, D)
     route_ids = routes.reshape(TOKENS, TOPK)
     expert_ids = jnp.arange(EXPERTS, dtype=jnp.int32)
     named = jnp.any(route_ids[:, :, None] == expert_ids[None, None, :], axis=1)
@@ -989,130 +1210,41 @@
         ]
     ).astype(f32)
     whole, masks = gather_weights(halves, named.T.astype(bf16))
-    whole = whole.reshape(2, D, 1664)
-    full_qkv = jnp.concatenate([whole[0, :, :1024], whole[1, :, :1024]], axis=1)
-    full_out = jnp.concatenate([whole[0, :, 1024:1536], whole[1, :, 1024:1536]], axis=1)
-    small = whole[0, :, 1536:]
-    full_router = small[:, :32]
-    attn_norm = small[:, 32].astype(f32)
-    ffn_norm = small[:, 33].astype(f32)
-    qk_norm = small[:, 34].reshape(128, 8)[:, 0].astype(f32)
-    z_place, xh_place = fsdp_place // 4, (fsdp_place // 2) % 2
-    y_place, xl_place = seq_place % 4, seq_place // 4
-
-    cot = cotangent.reshape(TOKENS, D)
+    whole = whole.reshape(2, D, WCOLS)
     g_all = lax.all_gather(cot[None], "fsdp", axis=0, tiled=True)
 
-    normed_attn, attn_scaling = rms_forward(layer_inputs, attn_norm)
-    normed_attn = normed_attn.astype(bf16)
-    projected_rows = jnp.dot(normed_attn, full_qkv, preferred_element_type=f32)
-    query_raw = projected_rows[:, :query_total_width].reshape(TOKENS, QUERY_HEADS, HEAD_SIZE)
-    key_raw = projected_rows[:, query_total_width : query_total_width + key_total_width].reshape(
-        TOKENS, KEY_VALUE_HEADS, HEAD_SIZE
+    positions = lax.axis_index("seq") * TOKENS + jnp.arange(TOKENS, dtype=jnp.int32)
+    half_dim = HEAD_SIZE // 2
+    freq_index = jnp.arange(half_dim, dtype=f32)
+    inverse = jnp.exp(-(2.0 * freq_index / HEAD_SIZE) * math.log(rope_base))
+    angles = positions.astype(f32)[:, None] * inverse[None, :]
+    cos, sin = jnp.cos(angles), jnp.sin(angles)
+    cos = jnp.concatenate([cos, cos, cos, cos], axis=1)
+    sin = jnp.concatenate([-sin, sin, -sin, sin], axis=1)
+
+    heads, full, logs, attended, after, normed_ffn, gates, small_t, raw = front(x, whole, route_ids, cos, sin)
+    row_sum, gate_sum, y_all, expert_grads = moe(
+        normed_ffn, g_all, masks, small_t[:EXPERTS], gate_up_weight, down_weight
     )
-    value_low = projected_rows[:, query_total_width + key_total_width :].astype(bf16)
-    query_normed, query_scaling = rms_forward(query_raw, qk_norm[:HEAD_SIZE])
-    key_normed, key_scaling = rms_forward(key_raw, qk_norm[HEAD_SIZE:])
-    positions = seq_place * TOKENS + jnp.arange(TOKENS, dtype=jnp.int32)
-    cosine_values, sine_values = rotary_tables(positions, HEAD_SIZE)
-    query_low = rotate(query_normed, cosine_values, sine_values).astype(bf16)
-    key_low = rotate(key_normed, cosine_values, sine_values).astype(bf16)
-    send = jnp.concatenate(
-        [
-            query_low.reshape(TOKENS, 8, 128),
-            key_low.reshape(TOKENS, 8, 64),
-            value_low.reshape(TOKENS, 8, 64),
-        ],
-        axis=2,
-    ).transpose(1, 0, 2)
-    heads = swap(send, 5).reshape(LENGTH, 256)
-    attended_low, attended_full, logs = attend(heads)
-    attended_tokens = (
-        swap(attended_low.reshape(8, TOKENS, 128), 6)
-        .transpose(1, 0, 2)
-        .reshape(TOKENS, D)
+    expert_part = lax.psum_scatter(expert_grads, "seq", scatter_dimension=1, tiled=True).astype(f32)
+    layer_out, token_grad, parts, small = back(
+        row_sum, gate_sum, gates, after, x, cot, attended, normed_ffn, small_t, raw,
+        heads, full, logs, cos, sin, whole, y_all,
     )
-    after_attention = layer_inputs + jnp.dot(attended_tokens, full_out, preferred_element_type=f32)
-    normed_ffn, ffn_scaling = rms_forward(after_attention, ffn_norm)
-    normed_ffn = normed_ffn.astype(bf16)
-    logits = jnp.dot(normed_ffn, full_router, preferred_element_type=f32)
-    peak = jnp.max(jnp.where(named, logits, -jnp.inf), axis=1, keepdims=True)
-    chosen_exp = jnp.where(named, jnp.exp(logits - peak), 0.0)
-    gates = chosen_exp / jnp.sum(chosen_exp, axis=1, keepdims=True)
-
-    g_all, masks = lax.optimization_barrier((g_all, masks))
-    row_sum, gate_sum, y_all, grads = moe(normed_ffn, g_all, masks, full_router.T, gate_up_weight, down_weight)
-    gate_grad = gate_sum[:, 0:32] + gate_sum[:, 32:64]
-    expert_part = lax.psum_scatter(grads, "seq", scatter_dimension=1, tiled=True).astype(f32)
-    gate_up_part, down_part = expert_part[:, :, : 2 * F], expert_part[:, :, 2 * F :]
-    incoming = cot.astype(f32)
-    chosen_grad = gates * (gate_grad - jnp.sum(gates * gate_grad, axis=1, keepdims=True))
-    logits_grad = chosen_grad.astype(bf16)
-    router_grad = t_dot(normed_ffn, logits_grad)
-    normed_ffn_grad = row_sum + dot_t(logits_grad, full_router)
-    after_extra, ffn_terms = rms_backward(after_attention, ffn_scaling, ffn_norm, normed_ffn_grad)
-    after_grad = incoming + after_extra
-    ffn_gain_grad = jnp.sum(ffn_terms, axis=0)
-    after_low = after_grad.astype(bf16)
-    out_weight_grad = t_dot(attended_tokens, after_low)
-    attended_grad = dot_t(after_low, full_out).astype(bf16)
-    grad_heads = swap(attended_grad.reshape(TOKENS, 8, 128).transpose(1, 0, 2), 7).reshape(LENGTH, 128)
-    dq, dkv, expert_sum = attend_back(heads, attended_full, logs, grad_heads, y_all)
-    layer_out = (after_attention + expert_sum).astype(bf16).reshape(1, TOKENS, D)
-    back = jnp.concatenate([dq, dkv], axis=1).reshape(8, TOKENS, 256)
-    back = swap(back, 8)
-    token_query_grad = back[:, :, :128].transpose(1, 0, 2).reshape(TOKENS, QUERY_HEADS, HEAD_SIZE)
-    token_key_grad = back[:, :, 128:192].transpose(1, 0, 2)
-    token_value_grad = back[:, :, 192:].transpose(1, 0, 2).reshape(TOKENS, key_total_width)
-    query_normed_grad = rotate(token_query_grad.astype(f32), cosine_values, -sine_values)
-    key_normed_grad = rotate(token_key_grad.astype(f32), cosine_values, -sine_values)
-    query_raw_grad, query_terms = rms_backward(query_raw, query_scaling, qk_norm[:HEAD_SIZE], query_normed_grad)
-    key_raw_grad, key_terms = rms_backward(key_raw, key_scaling, qk_norm[HEAD_SIZE:], key_normed_grad)
-    qk_gain_grad = jnp.concatenate(
-        [jnp.sum(query_terms, axis=(0, 1)), jnp.sum(key_terms, axis=(0, 1))], axis=0
-    )
-    projected_grad = jnp.concatenate(
-        [
-            query_raw_grad.reshape(TOKENS, query_total_width).astype(bf16),
-            key_raw_grad.reshape(TOKENS, key_total_width).astype(bf16),
-            token_value_grad,
-        ],
-        axis=1,
-    )
-    qkv_weight_grad = t_dot(normed_attn, projected_grad)
-    normed_attn_grad = dot_t(projected_grad, full_qkv)
-    input_extra, attn_terms = rms_backward(layer_inputs, attn_scaling, attn_norm, normed_attn_grad)
-    token_grad = (after_grad + input_extra).reshape(1, TOKENS, D)
-    attn_gain_grad = jnp.sum(attn_terms, axis=0)
-
-    qkv_low, out_low = qkv_weight_grad.astype(bf16), out_weight_grad.astype(bf16)
-    parts = jnp.stack(
-        [
-            jnp.concatenate([qkv_low[:, :1024], out_low[:, :512]], axis=1),
-            jnp.concatenate([qkv_low[:, 1024:], out_low[:, 512:]], axis=1),
-        ]
-    ).reshape(2, 8, 8, 16, GCOLS)
-    small = jnp.concatenate(
-        [
-            router_grad.reshape(128, 256),
-            attn_gain_grad.reshape(128, 8),
-            ffn_gain_grad.reshape(128, 8),
-            qk_gain_grad.reshape(128, 1),
-            jnp.zeros((128, 751), f32),
-        ],
-        axis=1,
-    ).reshape(8, 8, 2, 8, 128).transpose(2, 0, 1, 3, 4)
-    parts, small = reduce_weights(parts, small)
+    parts, small = reduce_weights(parts.reshape(2, 8, 8, 16, GCOLS), small.reshape(8, 8, 2, 8, 128))
     qkv_part = jnp.concatenate([parts[0, :, :1024], parts[1, :, :1024]], axis=1)
     out_part = jnp.concatenate([parts[0, :, 1024:], parts[1, :, 1024:]], axis=1)
-    small = small.reshape(1024)
-    router_part = small[:256].reshape(8, 32)
-    attn_part = small[256:264]
-    ffn_part = small[264:272]
-    qk_part = small[272:273]
     return (
-        layer_out, token_grad, attn_part, qkv_part, qk_part, out_part, ffn_part, router_part,
-        gate_up_part, down_part,
+        layer_out.reshape(1, TOKENS, D),
+        token_grad.reshape(1, TOKENS, D),
+        small[:, EXPERTS],
+        qkv_part,
+        small[0:1, EXPERTS + 2],
+        out_part,
+        small[:, EXPERTS + 1],
+        small[:, :EXPERTS],
+        expert_part[:, :, : 2 * F],
+        expert_part[:, :, 2 * F :],
     )
 
 

time: 483 us -> 384 us (0.80)
  local copies, waits for them, and re-layouts: 68.6 us -> 18.1 us
  other arithmetic: 37.3 us -> 4.77 us
  matrix products: 11.9 us -> 0 us
    pallas_call x6 -> x2, Pallas kernels: 138 us -> 124 us  [the longest x1 78.5 us: back(): pl.pallas_call(back_kernel, in_specs=[vmem] * 15 + [hbm] * 2, out_specs=[...]
    mul x16 -> x0, local copies, waits for them, and re-layouts: 12.6 us -> none  [the longest x8 9.02 us: rms_backward(): values * scaling_cube * jnp.mean(weighted * values, axis=-1, keepdims=True)]
    pallas_call x1, Pallas kernels: 40.6 us -> 52.8 us  [reduce_weights(): pl.pallas_call(reduce_kernel, in_specs=[pl.BlockSpec(memory_space=pl.ANY)...]
    dot_general x9 -> x0, matrix products: 11.9 us -> none  [the longest x3 6.21 us: dot_t(): lax.dot_general(a, b, (((1,), (1,)), ((), ())), preferred_element_type=f32)]
    concatenate x4 -> x0, local copies, waits for them, and re-layouts: 8.22 us -> none  [the longest x3 6.98 us: rotate(): jnp.concatenate([first_half * cosine_values - second_half * sine_values,...]
    reshape x10 -> x0, local copies, waits for them, and re-layouts: 8.12 us -> none  [the longest x1 1.97 us: on_device(): router_grad.reshape(128, 256)]
    reduce_sum x10 -> x0, other arithmetic: 7.16 us -> none  [the longest x2 2.67 us: on_device(): jnp.sum(query_terms, axis=(0, 1))]
    convert_element_type x7 -> x1, other arithmetic: 5.92 us -> 0.01 us  [on_device(): angles = positions.astype(f32)[:, None] * inverse[None, :]]
  transfers between devices with their start and end apart: 2 -> 2, of which waited for: 0 -> 0; matrix products, arithmetic and copies ran while one was open for 23% -> 4% of each run, Pallas kernels for 48% -> 60%
where the time goes in v3:
time: 384 us; the launch traced here: 379 us
  Pallas kernels  340 us (89%)
  local copies, waits for them, and re-layouts  18.1 us (5%)
  between operations  15.2 us (4%)
  other arithmetic  4.77 us (1%)
    pallas_call x1, Pallas kernels, moe(): pl.pallas_call(moe_kernel, in_specs=[any_space, any_space, vmem, vmem, an...  114 us
    pallas_call x1, Pallas kernels, back(): pl.pallas_call(back_kernel, in_specs=[vmem] * 15 + [hbm] * 2, out_specs=[...  78.5 us
    pallas_call x1, Pallas kernels, reduce_weights(): pl.pallas_call(reduce_kernel, in_specs=[pl.BlockSpec(memory_space=pl.ANY)...  52.8 us
    pallas_call x1, Pallas kernels, gather_weights(): pl.pallas_call(gather_kernel, in_specs=[pl.BlockSpec(memory_space=pltpu.V...  49.1 us
    pallas_call x1, Pallas kernels, front(): pl.pallas_call(front_kernel, in_specs=[vmem, hbm, vmem, vmem, vmem], out_...  46 us
  transfers between devices with their start and end apart: 2, of which 0 were waited for; matrix products, arithmetic and copies ran while one was open for 4% of the time, Pallas kernels for 60%

profile of v3, /device:TPU:1, one launch (start us, length us, event | category | flops | bytes accessed | tf_op | source)
XLA Modules:
  0.0 378.8 jit_solution(1039182792549819309)
XLA Ops:
  7.2 0.0 all-gather.2.cloned.1.call-start
  7.2 0.7 all-gather.2.cloned.1.call-update
  7.9 0.0 reduce-scatter.2.cloned.1.call-start
  8.6 0.7 copy.42
  9.4 0.7 copy.43
  10.1 1.5 copy.46
  11.6 0.7 fusion.3
  12.3 0.7 fusion.2
  13.1 0.8 concatenate.21
  13.8 0.8 concatenate.22
  14.6 0.7 fusion
  15.3 0.6 convert_bitcast_fusion.mask_ref
  15.9 0.7 maximum_convert_fusion.in_ref
  16.6 49.1 %gather_weights.1 = (bf16[2,8,8,16,1664]{4,3,2,1,0:T(8,128)(2,1)}, bf16[16,32,256]{2,1,0:T(8,128)(2,1)}) custom-call(f32[2,8,1664]{2,1,0:T(8,128)} %maximum_convert_fusion.in_ref, bf16[32,256]{1,0:T(8,128)(2,1)} %convert_bitcast_fusion.mask_ref), custom_call_target="tpu_custom_call" | custom-call | tf_op jit(solution)/shard_map/gather_weights/pallas_call | solution.py:732
  65.7 0.5 fusion.1
  66.3 1.0 pad_maximum_fusion
  67.2 46.0 %front.1 = (bf16[8,256,256]{2,1,0:T(8,128)(2,1)}, f32[2048,128]{1,0:T(8,128)}, f32[2048,128]{1,0:T(8,128)}, bf16[256,1024]{1,0:T(8,128)(2,1)}, f32[256,1024]{1,0...) custom-call(bf16[256,1024]{1,0:T(8,128)(2,1)} %bitcast.41, ...), custom_call_target="tpu_custom_call" | custom-call | flops 4000000000 | bytes 16777216 | tf_op jit(solution)/shard_map/front/pallas_call | solution.py:271
  113.2 1.5 slice.49.router_ref
  114.7 0.0 all-gather.2.cloned.1.call-done.g_ref
  114.7 113.6 %moe.1 = (f32[256,1024]{1,0:T(8,128)}, f32[256,128]{1,0:T(8,128)}, bf16[16,256,1024]{2,1,0:T(8,128)(2,1)}, bf16[2,1024,1536]{2,1,0:T(8,128)(2,1)}) custom-call(bf16[256,1024]{1,0:T(8,128)(2,1)} %get-tuple-element.32.x_ref.normed_ref, bf16[16,256,1024]{2,1,0:T(8,128)(2,1)} %all-gather.2.cloned.1.call-done.g_ref, ...), custom_call_target="tpu_custom_call" | custom-call | flops 32000000000 | bytes 41943040 | tf_op jit(solution)/shard_map/moe/pallas_call | solution.py:1005
  228.3 0.0 reduce-scatter.2.cloned.1.call-update
  228.3 78.5 %back.1 = (bf16[256,1024]{1,0:T(8,128)(2,1)}, f32[256,1024]{1,0:T(8,128)}, bf16[2,1024,1536]{2,1,0:T(8,128)(2,1)}, f32[1024,128]{1,0:T(8,128)}) custom-call(f32[256,1024]{1,0:T(8,128)} %get-tuple-element.35.row_ref, f32[256,128]{1,0:T(8,128)} %get-tuple-element.36.gate_sum_ref, f32[256,128]{1,0:T(8,128)} %get-tuple-element.37.gates_ref, ...), custom_call_target="tpu_custom_call" | custom-call | flops 8999999488 | bytes 33554432 | tf_op jit(solution)/shard_map/back/pallas_call | solution.py:592
  306.8 0.0 copy-start.1
  306.8 0.0 copy-start
  306.9 52.8 %reduce_weights.1 = (f32[2,8,1536]{2,1,0:T(8,128)}, f32[8,128]{1,0:T(8,128)}) custom-call(bf16[2,8,8,16,1536]{4,3,2,1,0:T(8,128)(2,1)} %bitcast.27, f32[8,8,2,8,128]{4,3,2,1,0:T(8,128)} %bitcast.31), custom_call_target="tpu_custom_call" | custom-call | tf_op jit(solution)/shard_map/reduce_weights/pallas_call | solution.py:1161
  359.6 0.0 copy-start.2
  359.7 1.3 slice.53
  361.0 1.5 slice_reduce_fusion
  362.5 0.7 slice_bitcast_fusion.3
  363.2 0.6 pad_maximum_fusion.3
  363.8 0.8 slice_bitcast_fusion.1
  364.6 0.6 pad_maximum_fusion.2
  365.2 0.0 reduce-scatter.2.cloned.1.call-done
  365.2 1.8 slice.61
  367.0 2.1 slice.60
  369.2 0.0 copy-done.1
  369.2 0.8 copy.54
  370.0 0.0 copy-done
  370.0 1.0 copy.55
  370.9 0.0 copy-done.2
  370.9 0.6 copy.56
  (4 shorter events, 0.0 us)
Async XLA Ops:
  7.2 107.5 %all-gather.2.cloned.1.call-start = ((), (), s32[]{:S(2)}) async-start(), calls=%async_computation.1 | async-start | bytes 8912896 | tf_op jit(solution)/shard_map/all_gather | solution.py:1214
  7.9 357.3 %reduce-scatter.2.cloned.1.call-start = ((), (), s32[]{:S(2)}) async-start(), calls=%async_computation.2 | async-start | bytes 7077888 | tf_op jit(solution)/shard_map/reduce_scatter | solution.py:1229
  306.8 62.3 %copy-start.1 = (bf16[256,1024]{1,0:T(8,128)(2,1)S(1)}, bf16[256,1024]{1,0:T(8,128)(2,1)}, u32[]{:S(2)}) copy-start(bf16[256,1024]{1,0:T(8,128)(2,1)} %get-tuple-element.45) | copy-start | bytes 1572868
  306.8 63.1 %copy-start = (f32[256,1024]{1,0:T(8,128)S(1)}, f32[256,1024]{1,0:T(8,128)}, u32[]{:S(2)}) copy-start(f32[256,1024]{1,0:T(8,128)} %get-tuple-element.46) | copy-start | bytes 3145732
  359.6 11.3 %copy-start.2 = (f32[8,128]{1,0:T(8,128)S(1)}, f32[8,128]{1,0:T(8,128)}, u32[]{:S(2)}) copy-start(f32[8,128]{1,0:T(8,128)} %get-tuple-element.49) | copy-start | bytes 12292
Sparse Core Ops, SparseCore 0:
  10.5 87.3 all-gather.1
  228.5 102.2 reduce-scatter.1

commit v4 on v3

--- a/solution.py
+++ b/solution.py
@@ -98,9 +98,10 @@
         self.all.append(copy)
         return copy
 
-    def finish(self):
+    def finish(self, done=()):
         for copy in self.all:
-            copy.wait_send()
+            if all(copy is not other for other in done):
+                copy.wait_send()
 
 
 OTHERS = ((2, 1), (2, 0), (0, 1), (1, 1), (-1, 1), (1, 0), (-1, 0))
@@ -139,8 +140,8 @@
 
 
 def front_kernel(
-    x_ref, w_ref, routes_ref, cos_ref, sin_ref,
-    heads_out, full_ref, logs_ref, att_ref, after_ref, normed_ref, gates_ref, small_t_ref, raw_ref,
+    x_ref, w_ref, routes_ref, cos_ref, sin_ref, cot_ref, side_ref,
+    heads_out, g_out, full_ref, logs_ref, att_ref, after_ref, normed_ref, gates_ref, small_t_ref, raw_ref,
     wq, wkv, wo, small, send, heads, out_buf, att, key0, key1, value,
     local_sems, send_sems, recv_sems,
 ):
@@ -160,9 +161,56 @@
     ]
     for copy in loads:
         copy.start()
+    own_g = [
+        pltpu.make_async_copy(cot_ref, g_out.at[here.fsdp], local_sems.at[6]),
+        pltpu.make_async_copy(side_ref, g_out.at[here.fsdp_at(0, 1)], local_sems.at[7]),
+    ]
+    for copy in own_g:
+        copy.start()
     peers = [here.seq_at(*other) for other in OTHERS]
-    meet([{"seq": peer} for peer in peers])
+    sib = here.sibling()
+    way = here.plane("fsdp")
+    meet([sib, *way.values()] + [{"seq": peer} for peer in peers])
     net = Copies(send_sems, recv_sems)
+
+    def gather_cotangent():
+        def at(ring, pair):
+            return g_out.at[here.fsdp_at(ring, pair)]
+
+        def half(ref, which):
+            return ref.at[pl.ds(128 * which, 128)]
+
+        def go(ref, target):
+            return net.start(ref, ref, target)
+
+        up, down = [net.start(cot_ref, at(0, 0), way[w]) for w in ("up", "down")]
+        kin = [net.start(cot_ref, at(0, 0), sib), net.start(side_ref, at(0, 1), sib)]
+        yield
+        up.wait_recv()
+        far = [go(half(at(-1, 0), 0), way["up"])]
+        kin.append(go(at(-1, 0), sib))
+        down.wait_recv()
+        far.append(go(half(at(1, 0), 1), way["down"]))
+        kin.append(go(at(1, 0), sib))
+        up, down = [net.start(side_ref, at(0, 1), way[w]) for w in ("up", "down")]
+        yield
+        for copy in far:
+            copy.wait_recv()
+        across = go(at(2, 0), way["across"])
+        kin.append(go(at(2, 0), sib))
+        yield
+        up.wait_recv()
+        kin.append(go(at(-1, 1), sib))
+        down.wait_recv()
+        kin.append(go(at(1, 1), sib))
+        across.wait_recv()
+        kin.append(go(at(2, 1), sib))
+        yield
+        for copy in kin:
+            copy.wait_recv()
+
+    moves = gather_cotangent()
+    next(moves)
     lanes, low_half = lane_halves()
     loads[0].wait()
     small_t = jnp.transpose(small[...].astype(f32)).astype(bf16)
@@ -172,10 +220,9 @@
     query_gain, key_gain = gain_tiles(small_t, lanes)
     cos, sin = cos_ref[...], sin_ref[...]
     loads[1].wait()
-    raw_ref[:, 0:1024] = dot(normed, wq[...])
+    queries = dot(normed, wq[...])
     loads[2].wait()
     kv = dot(normed, wkv[...])
-    raw_ref[:, 1024:1536] = kv[:, 0:512]
 
     def turned(tile, gain):
         normal = tile * lax.rsqrt(head_mean(tile * tile, low_half) + epsilon) * gain
@@ -183,14 +230,17 @@
 
     for j in range(4):
         part = slice(128 * j, 128 * (j + 1))
+        raw_ref[8 + j] = kv[:, part]
         keys = turned(kv[:, part], key_gain)
         values = kv[:, 512 + 128 * j : 640 + 128 * j]
         send[2 * j, :, 128:256] = jnp.where(low_half, keys, pltpu.roll(values, 64, 1)).astype(bf16)
         send[2 * j + 1, :, 128:256] = jnp.where(low_half, pltpu.roll(keys, 64, 1), values).astype(bf16)
     for h in range(8):
-        send[h, :, 0:128] = turned(raw_ref[:, 128 * h : 128 * (h + 1)], query_gain).astype(bf16)
+        raw_ref[h] = queries[:, 128 * h : 128 * (h + 1)]
+        send[h, :, 0:128] = turned(raw_ref[h], query_gain).astype(bf16)
     copies = [net.start(send.at[peer], heads.at[me], {"seq": peer}) for peer in peers]
     heads[me] = send[me]
+    next(moves)
     for copy in copies:
         copy.wait_recv()
     save = pltpu.make_async_copy(heads, heads_out, local_sems.at[5])
@@ -231,11 +281,15 @@
     def answer(i):
         j = lax.rem(me + 1 + i, 8)
         return pltpu.make_async_remote_copy(
-            src_ref=out_buf.at[j], dst_ref=att.at[:, columns], send_sem=send_sems.at[7 + i],
-            recv_sem=recv_sems.at[7 + i], device_id={"seq": j}, device_id_type=MESH,
+            src_ref=out_buf.at[j], dst_ref=att.at[:, columns], send_sem=send_sems.at[24 + i],
+            recv_sem=recv_sems.at[24 + i], device_id={"seq": j}, device_id_type=MESH,
         )
 
-    lax.fori_loop(0, 8, block, 0)
+    lax.fori_loop(0, 1, block, 0)
+    next(moves)
+    lax.fori_loop(1, 7, block, 0)
+    next(moves)
+    lax.fori_loop(7, 8, block, 0)
     att[:, columns] = out_buf[me]
     for k in (3, 4):
         loads[k].wait()
@@ -259,21 +313,26 @@
     peak = jnp.max(jnp.where(named > 0.0, logits, -1e30), axis=1, keepdims=True)
     chosen = jnp.where(named > 0.0, jnp.exp(logits - peak), 0.0)
     gates_ref[...] = chosen / jnp.sum(chosen, axis=1, keepdims=True)
+    for _ in moves:
+        pass
     save.wait()
+    for copy in own_g:
+        copy.wait()
     for i in range(7):
         answer(i).wait_send()
     net.finish()
 
 
-def front(x, whole, routes, cos, sin):
+def front(x, whole, routes, cos, sin, cot, side):
     vmem = pl.BlockSpec(memory_space=pltpu.VMEM)
     hbm = pl.BlockSpec(memory_space=pl.ANY)
     return pl.pallas_call(
         front_kernel,
-        in_specs=[vmem, hbm, vmem, vmem, vmem],
-        out_specs=[hbm] + [vmem] * 8,
+        in_specs=[vmem, hbm, vmem, vmem, vmem, hbm, hbm],
+        out_specs=[hbm] * 2 + [vmem] * 8,
         out_shape=[
             jax.ShapeDtypeStruct((8, TOKENS, 256), bf16),
+            jax.ShapeDtypeStruct((FSDP, TOKENS, D), bf16),
             jax.ShapeDtypeStruct((LENGTH, 128), f32),
             jax.ShapeDtypeStruct((LENGTH, 128), f32),
             jax.ShapeDtypeStruct((TOKENS, D), bf16),
@@ -281,7 +340,7 @@
             jax.ShapeDtypeStruct((TOKENS, D), bf16),
             jax.ShapeDtypeStruct((TOKENS, 128), f32),
             jax.ShapeDtypeStruct((128, D), bf16),
-            jax.ShapeDtypeStruct((TOKENS, 1536), f32),
+            jax.ShapeDtypeStruct((12, TOKENS, 128), f32),
         ],
         scratch_shapes=[
             pltpu.VMEM((D, 1024), bf16),
@@ -295,16 +354,16 @@
             pltpu.VMEM((LENGTH, 128), bf16),
             pltpu.VMEM((LENGTH, 128), bf16),
             pltpu.VMEM((LENGTH, 128), bf16),
-            pltpu.SemaphoreType.DMA((6,)),
-            pltpu.SemaphoreType.DMA((14,)),
-            pltpu.SemaphoreType.DMA((14,)),
+            pltpu.SemaphoreType.DMA((8,)),
+            pltpu.SemaphoreType.DMA((31,)),
+            pltpu.SemaphoreType.DMA((31,)),
         ],
         compiler_params=pltpu.CompilerParams(collective_id=2, has_side_effects=True, vmem_limit_bytes=VMEM),
         cost_estimate=pl.CostEstimate(
             flops=4 * 10**9, bytes_accessed=16 << 20, transcendentals=2 * LENGTH * LENGTH
         ),
         name="front",
-    )(x, whole, routes, cos, sin)
+    )(x, whole, routes, cos, sin, cot, side)
 
 
 def split3(values):
@@ -324,12 +383,14 @@
 
 
 def back_kernel(
-    row_ref, gate_sum_ref, gates_ref, after_ref, x_ref, cot_ref, att_ref, normed_ref, small_t_ref, raw_ref,
-    heads_ref, full_ref, logs_ref, cos_ref, sin_ref, w_ref, y_ref,
-    layer_ref, token_ref, parts_ref, small_ref,
-    wq, wkv, wo, send, grads, dq_buf, dkv_buf, back_q, back_kv, pg_q, pg_kv, after_grad,
+    gate_sum_ref, gates_ref, after_ref, x_ref, cot_ref, att_ref, normed_ref, small_t_ref,
+    heads_ref, full_ref, logs_ref, cos_ref, sin_ref, row_ref, raw_ref, w_ref, y_ref, y_other, grads_ref, far_ref,
+    layer_ref, token_ref, qkv_out, wo_out, small_out, up_out, down_out,
+    wqkv, wo, send, grads, back_q, back_kv, pg, after_grad,
     key0, key1, value0, value1, key_t, dk_total, dv_total,
-    slots, sib_in, hop_in, local_sems, send_sems, recv_sems,
+    slots, y_stage, hop_in,
+    parts, parts_in, small, small_in, hop_a, hop_b, late_a, late_b, small_s, small_f, total, total_in,
+    chunks, far_in, chunk_in, local_sems, send_sems, recv_sems,
 ):
     here = Place()
     me = here.seq
@@ -338,19 +399,41 @@
     loads = [
         pltpu.make_async_copy(w_ref.at[h, :, pl.ds(start, width)], there, local_sems.at[k])
         for k, (h, start, width, there) in enumerate(
-            ((0, 1024, 512, wo.at[0]), (1, 1024, 512, wo.at[1]), (0, 0, 1024, wq), (1, 0, 1024, wkv))
+            (
+                (0, 1024, 512, wo.at[0]),
+                (1, 1024, 512, wo.at[1]),
+                (0, 0, 1024, wqkv.at[0]),
+                (1, 0, 1024, wqkv.at[1]),
+            )
         )
     ]
+    loads.append(pltpu.make_async_copy(row_ref, after_grad, local_sems.at[19]))
     for copy in loads:
         copy.start()
+    e_loads = [
+        pltpu.make_async_copy(
+            grads_ref.at[:, pl.ds(pl.multiple_of(here.seq_at(ring, pair) * 128, 128), 128)],
+            chunks.at[i, pair], local_sems.at[12 + 2 * i + pair],
+        )
+        for i, ring in enumerate((-1, 1, 0)) for pair in range(2)
+    ]
+    e_loads.append(pltpu.make_async_copy(far_ref, far_in, local_sems.at[18]))
     order = (6, 7, 3, 5, 2, 4, 1, 0)
-    y_loads = {k: pltpu.make_async_copy(y_ref.at[2 * k], slots.at[k], local_sems.at[4 + k]) for k in order}
+    y_loads = {k: pltpu.make_async_copy(y_ref.at[k], slots.at[k], local_sems.at[4 + k]) for k in order}
+    y_more = {
+        k: pltpu.make_async_copy(y_other.at[k], y_stage.at[i % 2], local_sems.at[20 + k]) for i, k in enumerate(order)
+    }
     for copy in y_loads.values():
         copy.start()
+    for k in order[:2]:
+        y_more[k].start()
     peers = [here.seq_at(*other) for other in OTHERS]
-    meet([sib, *way.values()] + [{"seq": peer} for peer in peers])
+    seq_peers = [{"seq": peer} for peer in peers]
+    fsdp_peers = [{"fsdp": here.fsdp_at(*other)} for other in OTHERS]
+    meet([sib, *seq_peers, *fsdp_peers])
     net = Copies(send_sems, recv_sems)
-    joins = {k: net.start(y_ref.at[2 * k + 1], sib_in.at[k], sib) for k in order}
+    for copy in e_loads:
+        copy.start()
     lanes, low_half = lane_halves()
 
     gate_sum = gate_sum_ref[...]
@@ -359,14 +442,16 @@
     gate_grad = jnp.where(lanes < EXPERTS, gate_grad, 0.0)
     chosen = gates * (gate_grad - jnp.sum(gates * gate_grad, axis=1, keepdims=True))
     logits_grad = chosen.astype(bf16)
-    normed_grad = row_ref[...] + dot(logits_grad, small_t_ref[...])
+    loads[4].wait()
+    normed_grad = after_grad[...] + dot(logits_grad, small_t_ref[...])
     after = after_ref[...]
     scaling = row_scale(after)
     weighted = normed_grad * small_t_ref[33:34, :].astype(f32)
     middle = jnp.mean(weighted * after, axis=1, keepdims=True)
-    total = cot_ref[...].astype(f32) + scaling * weighted - after * (scaling * scaling * scaling * middle)
-    after_grad[...] = total
-    after_low = total.astype(bf16)
+    after_grad[...] = (
+        cot_ref[...].astype(f32) + scaling * weighted - after * (scaling * scaling * scaling * middle)
+    )
+    after_low = after_grad[...].astype(bf16)
     ffn_gain = jnp.sum(normed_grad * after * scaling, axis=0, keepdims=True)
     for k in (0, 1):
         loads[k].wait()
@@ -377,9 +462,11 @@
             send[4 * q + h] = attended_grad[:, 128 * h : 128 * (h + 1)].astype(bf16)
     to_heads = [net.start(send.at[peer], grads.at[me], {"seq": peer}) for peer in peers]
     grads[me] = send[me]
-    small_ref[...] = t_dot(normed_ref[...], logits_grad)
+    router_grad = t_dot(normed_ref[...], logits_grad)
+    small[...] = router_grad.reshape(8, 8, 2, 8, 128)
     for h in range(2):
-        parts_ref[h, :, 1024:1536] = t_dot(att_ref[...], after_low[:, 512 * h : 512 * (h + 1)]).astype(bf16)
+        out_grad = t_dot(att_ref[...], after_low[:, 512 * h : 512 * (h + 1)]).astype(bf16)
+        parts[h, :, :, :, 1024:1536] = out_grad.reshape(8, 8, 16, 512)
 
     def add_to(ref, *values):
         result = ref[...].astype(f32)
@@ -388,9 +475,12 @@
         ref[...] = result.astype(bf16)
 
     def join(k):
+        i = order.index(k)
         y_loads[k].wait()
-        joins[k].wait_recv()
-        add_to(slots.at[k], sib_in.at[k])
+        y_more[k].wait()
+        add_to(slots.at[k], y_stage.at[i % 2])
+        if i + 2 < 8:
+            y_more[order[i + 2]].start()
 
     def half(ref, which):
         return ref.at[pl.ds(128 * which, 128)]
@@ -435,7 +525,37 @@
             + hop_in[6].astype(f32)
         ).astype(bf16)
 
+    def expert_grads():
+        ring = here.plane("seq")
+        for copy in e_loads:
+            copy.wait()
+        for pair in (1, 0):
+            add_to(chunks.at[0, pair, 1], far_in.at[pair, 1])
+            add_to(chunks.at[1, pair, 0], far_in.at[pair, 0])
+        beside = [
+            net.start(chunks.at[0, 1], chunk_in.at[0], ring["down"]),
+            net.start(chunks.at[1, 1], chunk_in.at[1], ring["up"]),
+        ]
+        yield
+        own = [
+            net.start(chunks.at[0, 0], chunk_in.at[2], ring["down"]),
+            net.start(chunks.at[1, 0], chunk_in.at[3], ring["up"]),
+        ]
+        for copy in beside:
+            copy.wait_recv()
+        add_to(chunks.at[2, 1], chunk_in.at[0], chunk_in.at[1])
+        own.append(net.start(chunks.at[2, 1], chunk_in.at[4], ring["across"]))
+        yield
+        for copy in own:
+            copy.wait_recv()
+        result = chunks[2, 0].astype(f32)
+        for i in range(2, 5):
+            result = result + chunk_in[i].astype(f32)
+        up_out[...] = result[:, :, 0 : 2 * F]
+        down_out[...] = result[:, :, 2 * F : 3 * F]
+
     moves = expert_sum()
+    more_moves = expert_grads()
     next(moves)
     ones_high = jnp.where((lanes >= 64) & (lanes < 67), 1.0, 0.0)
     ones_low = jnp.where(lanes < 3, 1.0, 0.0)
@@ -457,8 +577,8 @@
     def answer(i):
         j = lax.rem(me + 1 + i, 8)
         return pltpu.make_async_remote_copy(
-            src_ref=dq_buf.at[j], dst_ref=back_q.at[:, columns], send_sem=send_sems.at[32 + i],
-            recv_sem=recv_sems.at[32 + i], device_id={"seq": j}, device_id_type=MESH,
+            src_ref=grads.at[j], dst_ref=back_q.at[:, columns], send_sem=send_sems.at[92 + i],
+            recv_sem=recv_sems.at[92 + i], device_id={"seq": j}, device_id_type=MESH,
         )
 
     def block(i, carry):
@@ -495,7 +615,7 @@
             dv_total[part, :] = dv
             dk_total[part, :] = dk
         both = jnp.concatenate(dq, axis=0) * (1.0 / 8.0)
-        dq_buf[j] = jnp.transpose(both).astype(bf16)
+        grads[j] = jnp.transpose(both).astype(bf16)
 
         @pl.when(i < 7)
         def _():
@@ -503,21 +623,31 @@
 
         return carry
 
+    next(more_moves)
     lax.fori_loop(0, 3, block, 0)
     next(moves)
     lax.fori_loop(3, 6, block, 0)
     next(moves)
+    next(more_moves)
     lax.fori_loop(6, 8, block, 0)
+    for copy in to_heads:
+        copy.wait_send()
     for c in range(8):
         rows = slice(TOKENS * c, TOKENS * (c + 1))
         dk = dk_total[rows, :]
         dv = dv_total[rows, :]
         dk = dk + pltpu.roll(dk, 64, 1)
         dv = dv + pltpu.roll(dv, 64, 1)
-        dkv_buf[c] = jnp.where(low_half, dk, dv).astype(bf16)
-    to_tokens = [net.start(dkv_buf.at[peer], back_kv.at[me], {"seq": peer}) for peer in peers]
-    back_kv[me] = dkv_buf[me]
-    back_q[:, columns] = dq_buf[me]
+        send[c] = jnp.where(low_half, dk, dv).astype(bf16)
+    to_tokens = [net.start(send.at[peer], back_kv.at[me], {"seq": peer}) for peer in peers]
+    raw = [
+        pltpu.make_async_copy(raw_ref.at[h], there.at[pl.ds(TOKENS * (h % 8), TOKENS)], local_sems.at[28 + h])
+        for h, there in [(h, dk_total) for h in range(8)] + [(h, dv_total) for h in range(8, 12)]
+    ]
+    for copy in raw:
+        copy.start()
+    back_kv[me] = send[me]
+    back_q[:, columns] = grads[me]
     x = x_ref[...].astype(f32)
     x_scaling = row_scale(x)
     attn_gain = small_t_ref[32:33, :].astype(f32)
@@ -535,17 +665,13 @@
         result = scale * weighted - tile * (scale * scale * scale * middle)
         return result.astype(bf16), jnp.sum(grad * tile * scale, axis=0, keepdims=True)
 
+    for copy in raw:
+        copy.wait()
     query_terms = jnp.zeros((1, 128), f32)
     for h in range(8):
         part = slice(128 * h, 128 * (h + 1))
-        pg_q[:, part], terms = unturned(back_q[:, part].astype(f32), raw_ref[:, part], query_gain)
+        pg[0, :, part], terms = unturned(back_q[:, part].astype(f32), dk_total[TOKENS * h : TOKENS * (h + 1), :], query_gain)
         query_terms = query_terms + terms
-    for copy in loads[2:]:
-        copy.wait()
-    for r in range(4):
-        part = slice(256 * r, 256 * (r + 1))
-        parts_ref[0, part, 0:1024] = t_dot(normed[:, part], pg_q[...]).astype(bf16)
-    normed_grad = dot_t(pg_q[...], wq[...])
     for copy in to_tokens:
         copy.wait_recv()
     key_terms = jnp.zeros((1, 128), f32)
@@ -554,16 +680,69 @@
         keys = jnp.where(low_half, first, pltpu.roll(second, 64, 1))
         values = jnp.where(low_half, pltpu.roll(first, 64, 1), second)
         part = slice(128 * j, 128 * (j + 1))
-        pg_kv[:, part], terms = unturned(keys, raw_ref[:, 1024 + 128 * j : 1152 + 128 * j], key_gain)
+        pg[1, :, part], terms = unturned(keys, dv_total[TOKENS * j : TOKENS * (j + 1), :], key_gain)
         key_terms = key_terms + terms
-        pg_kv[:, 512 + 128 * j : 640 + 128 * j] = values.astype(bf16)
+        pg[1, :, 512 + 128 * j : 640 + 128 * j] = values.astype(bf16)
+
+    core = here.core
+    f = here.z * 2 + here.xh
+    sib_joins = []
+    for turn in range(2):
+        h = 1 - core if turn == 0 else core
+        for r in range(4):
+            result = t_dot(normed[:, 256 * r : 256 * (r + 1)], pg[h]).astype(bf16)
+            parts[h, 2 * r : 2 * r + 2, :, :, 0:1024] = result.reshape(2, 8, 16, 1024)
+            if turn == 0:
+                sib_joins.append(
+                    net.start(parts.at[h, pl.ds(2 * r, 2)], parts_in.at[pl.ds(2 * r, 2)], sib)
+                )
     for r in range(4):
-        part = slice(256 * r, 256 * (r + 1))
-        parts_ref[1, part, 0:1024] = t_dot(normed[:, part], pg_kv[...]).astype(bf16)
-    normed_grad = normed_grad + dot_t(pg_kv[...], wkv[...])
-    weighted = normed_grad * attn_gain
-    middle = jnp.mean(weighted * x, axis=1, keepdims=True)
-    token_ref[...] = after_grad[...] + x_scaling * weighted - x * (x_scaling * x_scaling * x_scaling * middle)
+        sib_joins[r].wait_recv()
+        for q in (2 * r, 2 * r + 1):
+            parts[core, q] = (parts[core, q].astype(f32) + parts_in[q].astype(f32)).astype(bf16)
+
+    def f_at(ring, pair):
+        return lax.rem(here.z + ring + 4, 4) * 2 + (1 - here.xh if pair else here.xh)
+
+    def plane(part, hop, way):
+        def half(ref, which):
+            return ref.at[pl.ds(4 * which, 4)]
+
+        a = net.start(part(2, 1), hop.at[0], way["across"])
+        xd = net.start(part(-1, 1), hop.at[2], way["down"])
+        xu = net.start(part(1, 1), hop.at[3], way["up"])
+        yield
+        a.wait_recv()
+        add_to(part(2, 0), hop.at[0])
+        u = net.start(half(part(2, 0), 0), half(hop.at[1], 0), way["up"])
+        d = net.start(half(part(2, 0), 1), half(hop.at[1], 1), way["down"])
+        yield
+        xd.wait_recv()
+        xu.wait_recv()
+        add_to(part(0, 1), hop.at[2], hop.at[3])
+        rx = net.start(part(0, 1), hop.at[6], way["across"])
+        u.wait_recv()
+        add_to(half(part(1, 0), 0), half(hop.at[1], 0))
+        ru = net.start(part(1, 0), hop.at[4], way["up"])
+        d.wait_recv()
+        add_to(half(part(-1, 0), 1), half(hop.at[1], 1))
+        rd = net.start(part(-1, 0), hop.at[5], way["down"])
+        yield
+        rx.wait_recv()
+        ru.wait_recv()
+        rd.wait_recv()
+        add_to(part(0, 0), hop.at[4], hop.at[5], hop.at[6])
+
+    low, high = pl.ds(0, GCOLS // 2), pl.ds(GCOLS // 2, GCOLS // 2)
+    first_plane = plane(
+        lambda ring, pair: parts.at[core, here.seq_at(ring, pair), :, :, low], hop_a, here.plane("seq")
+    )
+    second_plane = plane(lambda ring, pair: parts.at[core, :, f_at(ring, pair), :, high], hop_b, way)
+    next(first_plane)
+    next(second_plane)
+    for copy in loads[2:4]:
+        copy.wait()
+    normed_grad = dot_t(pg[0], wqkv[0]) + dot_t(pg[1], wqkv[1])
     attn_gain_grad = jnp.sum(normed_grad * x * x_scaling, axis=0, keepdims=True)
     query_terms = query_terms + pltpu.roll(query_terms, 64, 1)
     key_terms = key_terms + pltpu.roll(key_terms, 64, 1)
@@ -578,12 +757,69 @@
     gain_rows = jnp.where(
         row == 32, attn_gain_grad, jnp.where(row == 33, ffn_gain, jnp.where(row == 34, head_row, 0.0))
     )
-    small_ref[...] = small_ref[...] + jnp.transpose(gain_rows)
+    small[...] = small[...] + jnp.transpose(gain_rows).reshape(8, 8, 2, 8, 128)
+    small_join = net.start(small.at[:, :, 1 - core], small_in, sib)
+    next(first_plane)
+    next(second_plane)
+    weighted = normed_grad * attn_gain
+    middle = jnp.mean(weighted * x, axis=1, keepdims=True)
+    token_ref[...] = after_grad[...] + x_scaling * weighted - x * (x_scaling * x_scaling * x_scaling * middle)
+    small_join.wait_recv()
+    small_in[...] = small_in[...] + small[:, :, core]
+    small_copies = [
+        net.start(small_in.at[peers[i]], small_s.at[i], seq_peers[i]) for i in range(7)
+    ]
+    next(first_plane)
+    next(second_plane)
     for _ in moves:
         pass
+    for _ in more_moves:
+        pass
+    for copy in small_copies:
+        copy.wait_recv()
+    mine = small_in[me]
+    for i in range(7):
+        mine = mine + small_s[i]
+    small_in[me] = mine
+    small_copies = [
+        net.start(small_in.at[me, f_at(*OTHERS[i])], small_f.at[i], fsdp_peers[i]) for i in range(7)
+    ]
+    next(first_plane, None)
+    late = [
+        [net.start(parts.at[core, me, f_at(*OTHERS[i]), :, low], late_a.at[i], fsdp_peers[i]) for i in range(7)]
+    ]
+    next(second_plane, None)
+    late.append(
+        [net.start(parts.at[core, peers[i], f, :, high], late_b.at[i], seq_peers[i]) for i in range(7)]
+    )
+    for copy in small_copies:
+        copy.wait_recv()
+    mine = small_in[me, f]
+    for i in range(7):
+        mine = mine + small_f[i]
+    small_out[...] = mine
+    for cols, copies, there in (
+        (slice(0, GCOLS // 2), late[0], late_a), (slice(GCOLS // 2, GCOLS), late[1], late_b)
+    ):
+        for copy in copies:
+            copy.wait_recv()
+        result = parts[core, me, f, :, cols].astype(f32)
+        for i in range(7):
+            result = result + there[i].astype(f32)
+        total[:, cols] = result
+    last = net.start(total.at[pl.ds(pl.multiple_of(8 * (1 - core), 8), 8)], total_in, sib)
+    mine = total[pl.ds(pl.multiple_of(8 * core, 8), 8), :]
+    last.wait_recv()
+    theirs = total_in[...]
+    is_low = core == 0
+    left, right = jnp.where(is_low, mine, theirs), jnp.where(is_low, theirs, mine)
+    qkv_out[:, 0:1024] = left[:, 0:1024]
+    qkv_out[:, 1024:2048] = right[:, 0:1024]
+    wo_out[:, 0:512] = left[:, 1024:1536]
+    wo_out[:, 512:1024] = right[:, 1024:1536]
     for i in range(7):
         answer(i).wait_send()
-    net.finish()
+    net.finish(to_heads)
 
 
 def back(*operands):
@@ -591,39 +827,53 @@
     hbm = pl.BlockSpec(memory_space=pl.ANY)
     return pl.pallas_call(
         back_kernel,
-        in_specs=[vmem] * 15 + [hbm] * 2,
-        out_specs=[vmem] * 4,
+        in_specs=[vmem] * 13 + [hbm] * 7,
+        out_specs=[vmem] * 7,
         out_shape=[
             jax.ShapeDtypeStruct((TOKENS, D), bf16),
             jax.ShapeDtypeStruct((TOKENS, D), f32),
-            jax.ShapeDtypeStruct((2, D, 1536), bf16),
-            jax.ShapeDtypeStruct((D, 128), f32),
+            jax.ShapeDtypeStruct((8, 2048), f32),
+            jax.ShapeDtypeStruct((8, 1024), f32),
+            jax.ShapeDtypeStruct((8, 128), f32),
+            jax.ShapeDtypeStruct((2, 128, 2 * F), f32),
+            jax.ShapeDtypeStruct((2, 128, F), f32),
         ],
         scratch_shapes=[
-            pltpu.VMEM((D, 1024), bf16),
-            pltpu.VMEM((D, 1024), bf16),
+            pltpu.VMEM((2, D, 1024), bf16),
             pltpu.VMEM((2, D, 512), bf16),
-            pltpu.VMEM((8, TOKENS, 128), bf16),
-            pltpu.VMEM((8, TOKENS, 128), bf16),
             pltpu.VMEM((8, TOKENS, 128), bf16),
             pltpu.VMEM((8, TOKENS, 128), bf16),
             pltpu.VMEM((TOKENS, D), bf16),
             pltpu.VMEM((8, TOKENS, 128), bf16),
-            pltpu.VMEM((TOKENS, D), bf16),
-            pltpu.VMEM((TOKENS, D), bf16),
+            pltpu.VMEM((2, TOKENS, D), bf16),
             pltpu.VMEM((TOKENS, D), f32),
         ]
         + [pltpu.VMEM((LENGTH, 128), bf16)] * 4
         + [pltpu.VMEM((64, LENGTH), bf16)]
         + [pltpu.VMEM((LENGTH, 128), f32)] * 2
-        + [pltpu.VMEM((8, TOKENS, D), bf16)] * 2
+        + [pltpu.VMEM((8, TOKENS, D), bf16), pltpu.VMEM((2, TOKENS, D), bf16)]
         + [pltpu.VMEM((7, TOKENS, D), bf16)]
         + [
-            pltpu.SemaphoreType.DMA((12,)),
+            pltpu.VMEM((2, 8, 8, 16, GCOLS), bf16),
+            pltpu.VMEM((8, 8, 16, GCOLS), bf16),
+            pltpu.VMEM((8, 8, 2, 8, 128), f32),
+            pltpu.VMEM((8, 8, 8, 128), f32),
+            pltpu.VMEM((7, 8, 16, GCOLS // 2), bf16),
+            pltpu.VMEM((7, 8, 16, GCOLS // 2), bf16),
+            pltpu.VMEM((7, 16, GCOLS // 2), bf16),
+            pltpu.VMEM((7, 16, GCOLS // 2), bf16),
+            pltpu.VMEM((7, 8, 8, 128), f32),
+            pltpu.VMEM((7, 8, 128), f32),
+            pltpu.VMEM((16, GCOLS), f32),
+            pltpu.VMEM((8, GCOLS), f32),
+            pltpu.VMEM((3, 2, 2, 128, 3 * F), bf16),
+            pltpu.VMEM((2, 2, 128, 3 * F), bf16),
+            pltpu.VMEM((5, 2, 128, 3 * F), bf16),
             pltpu.SemaphoreType.DMA((40,)),
-            pltpu.SemaphoreType.DMA((40,)),
+            pltpu.SemaphoreType.DMA((100,)),
+            pltpu.SemaphoreType.DMA((100,)),
         ],
-        compiler_params=pltpu.CompilerParams(collective_id=5, has_side_effects=True, vmem_limit_bytes=VMEM),
+        compiler_params=pltpu.CompilerParams(collective_id=5, has_side_effects=True, vmem_limit_bytes=63 * 1024 * 1024),
         cost_estimate=pl.CostEstimate(
             flops=9 * 10**9, bytes_accessed=32 << 20, transcendentals=2 * LENGTH * LENGTH
         ),
@@ -631,7 +881,30 @@
     )(*operands)
 
 
-def gather_kernel(in_ref, mask_ref, out_ref, masks_out, stage, block, local_sems, send_sems, recv_sems):
+def gather_kernel(
+    qkv_ref, wo_ref, router_ref, attn_ref, ffn_ref, head_ref, routes_ref, cot_ref, out_ref, masks_out, side_out,
+    in_ref, mask_ref, stage, block, local_sems, send_sems, recv_sems,
+):
+    lanes = lax.broadcasted_iota(jnp.int32, (1, 128), 1)
+    same = lax.broadcasted_iota(jnp.int32, (8, 8), 0) == lax.broadcasted_iota(jnp.int32, (8, 8), 1)
+
+    def column(row):
+        return jnp.sum(jnp.where(same, row[...].astype(f32), 0.0), axis=1, keepdims=True)
+
+    gains = jnp.where(
+        lanes == 32,
+        column(attn_ref),
+        jnp.where(lanes == 33, column(ffn_ref), jnp.where(lanes == 34, head_ref[...].astype(f32), 0.0)),
+    )
+    for h in range(2):
+        in_ref[h, :, 0:1024] = qkv_ref[:, 1024 * h : 1024 * (h + 1)].astype(f32)
+        in_ref[h, :, 1024:1536] = wo_ref[:, 512 * h : 512 * (h + 1)].astype(f32)
+        in_ref[h, :, 1536:1664] = gains
+        in_ref[h, :, 1536:1568] = router_ref[...].astype(f32)
+    named = jnp.zeros((256, 128), f32)
+    for k in range(8):
+        named = jnp.where(routes_ref[:, k : k + 1] == lanes, 1.0, named)
+    mask_ref[...] = jnp.transpose(named)[0:32, :].astype(bf16)
     here = Place()
     c, s, f = here.core, here.seq, here.z * 2 + here.xh
     sib = here.sibling()
@@ -719,25 +992,30 @@
             ring, pair = others[i - 1]
             ref = masks_out.at[here.fsdp_at(-ring, pair)]
             kin.append(net.start(ref, ref, sib))
-    for _ in range(4):
+    for turn in range(4):
         next(first, None)
         next(second, None)
+        if turn == 1:
+            kin.append(net.start(cot_ref, side_out, ways["fsdp"]["across"]))
     for copy in kin:
         copy.wait_recv()
     net.finish()
 
 
-def gather_weights(halves, mask):
-    n = 64
+def gather_weights(*operands):
+    n = 65
     return pl.pallas_call(
         gather_kernel,
-        in_specs=[pl.BlockSpec(memory_space=pltpu.VMEM)] * 2,
-        out_specs=[pl.BlockSpec(memory_space=pl.ANY)] * 2,
+        in_specs=[pl.BlockSpec(memory_space=pltpu.VMEM)] * 7 + [pl.BlockSpec(memory_space=pl.ANY)],
+        out_specs=[pl.BlockSpec(memory_space=pl.ANY)] * 3,
         out_shape=[
             jax.ShapeDtypeStruct((2, 8, 8, 16, WCOLS), bf16),
             jax.ShapeDtypeStruct((16, 32, 256), bf16),
+            jax.ShapeDtypeStruct((256, 1024), bf16),
         ],
         scratch_shapes=[
+            pltpu.VMEM((2, 8, WCOLS), f32),
+            pltpu.VMEM((32, 256), bf16),
             pltpu.VMEM((16, WCOLS), f32),
             pltpu.VMEM((16, WCOLS), bf16),
             pltpu.SemaphoreType.DMA((2,)),
@@ -746,14 +1024,14 @@
         ],
         compiler_params=pltpu.CompilerParams(collective_id=1, has_side_effects=True, vmem_limit_bytes=VMEM),
         name="gather_weights",
-    )(halves, mask)
+    )(*operands)
 
 
 def moe_kernel(
     x_ref, g_ref, masks_ref, router_ref, up_hbm, down_hbm,
-    row_out, gate_out, y_out, grads_out,
+    row_out, gate_out, y_out, y_in, grads_out, far_out,
     slots, sib_in, hop_in, g_rows, up_ref, down_ref,
-    rows_x, rows_p, rows_h, rows_u, rows_g, slot_gate, places, stage_y, stage_r, y_stage, w_stage,
+    rows_x, rows_p, rows_h, rows_u, rows_g, slot_gate, places, stage_y, stage_r, stage,
     local_sems, send_sems, recv_sems,
 ):
     here = Place()
@@ -777,11 +1055,14 @@
         xh = 1 - here.xh if pair else here.xh
         return z * 4 + xh * 2 + (1 - here.core if c else here.core)
 
+    groups = ((4, 5, 8, 9), (6, 7, 10, 11), (12, 13, 14, 15), (0, 1, 2, 3))
+
     def fetch_g(group):
-        return [local(g_ref.at[source(4 * group + s)], g_rows.at[s]) for s in range(4)]
+        return [local(g_ref.at[source(groups[group][s])], g_rows.at[s]) for s in range(4)]
 
     g_copies = fetch_g(0)
-    meet([sib, *way.values()])
+    ring = here.plane("seq")
+    meet([sib, *way.values(), ring["up"], ring["down"]])
     net = Copies(send_sems, recv_sems)
 
     def block(k, low=0, rows=TOKENS):
@@ -798,6 +1079,12 @@
     up = push(0, 4, way["up"], src=x_ref)
     down = push(0, 8, way["down"], src=x_ref)
     kin = {1: push(0, 1, sib, src=x_ref)}
+    up.wait_recv()
+    far_low = push(4, 12, way["up"], 0, 128)
+    kin[5] = push(4, 5, sib)
+    down.wait_recv()
+    far_high = push(8, 12, way["down"], 128, 128)
+    kin[9] = push(8, 9, sib)
     across.wait_recv()
     up_x = push(2, 6, way["up"])
     down_x = push(2, 10, way["down"])
@@ -816,13 +1103,13 @@
             < lax.broadcasted_iota(jnp.int32, (TOKENS, TOKENS), 1)
         ).astype(f32).astype(bf16)
         for s in range(4):
-            k = 4 * group + s
+            k = groups[group][s]
             if k in kin:
                 kin[k].wait_recv()
             g_copies[s].wait()
             x_rows = slots[k, :, 0:D]
             named = masks_ref[source(k)].astype(f32)
-            logits = dot_t(router_ref[...], x_rows)
+            logits = dot_t(router_ref[0:EXPERTS, :], x_rows)
             peak = jnp.max(jnp.where(named > 0.0, logits, -1e30), axis=0, keepdims=True)
             parts = jnp.where(named > 0.0, jnp.exp(logits - peak), 0.0)
             gates = parts / jnp.sum(parts, axis=0, keepdims=True)
@@ -877,123 +1164,151 @@
 
         lax.fori_loop(0, 2, one, 0)
 
+    y_sent = []
+
+    def free_stage():
+        for copy, remote in state.pop("y", ()):
+            if remote:
+                copy.wait_send()
+            else:
+                copy.wait()
+
     def combine(group):
-        for copy in state.pop("y", ()):
-            copy.wait()
+        free_stage()
         for s in range(4):
-            k = 4 * group + s
+            k = groups[group][s]
             for copy in sent[k]:
                 copy.wait_send()
             part = slice(SLOTS * s, SLOTS * (s + 1))
             both = jnp.concatenate([stage_y[0, part, :], stage_y[1, part, :]], axis=0)
-            y_stage[s] = t_dot(places[s], both).astype(bf16)
+            stage[s, :, 0:D] = t_dot(places[s], both).astype(bf16)
             both = jnp.concatenate([stage_r[0, part, :], stage_r[1, part, :]], axis=0)
             slots[k] = t_dot(places[s], both).astype(bf16)
-        state["y"] = [local(y_stage.at[s], y_out.at[4 * group + s]) for s in range(4)]
-        for j in range(2):
-            k = 4 * group + 2 * j
-            state["k", group, j] = net.start(slots.at[k + 1], sib_in.at[2 * group + j], sib)
-
-    def join(group, j):
-        state["k", group, j].wait_recv()
-        k = 4 * group + 2 * j
-        slots[k] = (slots[k].astype(f32) + sib_in[2 * group + j].astype(f32)).astype(bf16)
-
-    first_x.wait()
+        state["y"] = []
+        for s in range(4):
+            k = groups[group][s]
+            ready = stage.at[s, :, pl.ds(0, D)]
+            if k % 2:
+                y_sent.append(net.start(ready, y_in.at[k // 2], sib))
+                state["y"].append((y_sent[-1], True))
+            else:
+                state["y"].append((local(ready, y_out.at[k // 2]), False))
+        for k in groups[group][::2]:
+            state[k] = net.start(slots.at[k + 1], sib_in.at[k // 2], sib)
+
+    def join(k):
+        state[k].wait_recv()
+        slots[k] = (slots[k].astype(f32) + sib_in[k // 2].astype(f32)).astype(bf16)
+
+    def half(ref, which):
+        return ref.at[pl.ds(128 * which, 128)]
+
     gather(0)
     g_copies = fetch_g(1)
     for copy in weights:
         copy.wait()
-    up.wait_recv()
-    far_low = push(4, 12, way["up"], 0, 128)
-    kin[5] = push(4, 5, sib)
-    down.wait_recv()
-    far_high = push(8, 12, way["down"], 128, 128)
-    kin[9] = push(8, 9, sib)
     run(0)
+    far_low.wait_recv()
+    far_high.wait_recv()
+    far_x = push(12, 14, way["across"])
+    kin[13] = push(12, 13, sib)
     up_x.wait_recv()
     kin[7] = push(6, 7, sib)
     down_x.wait_recv()
     kin[11] = push(10, 11, sib)
     combine(0)
-    far_low.wait_recv()
-    far_high.wait_recv()
-    far_x = push(12, 14, way["across"])
-    kin[13] = push(12, 13, sib)
     gather(1)
-    g_copies = fetch_g(3)
+    g_copies = fetch_g(2)
+    join(4)
+    hop_rd = net.start(slots.at[4], hop_in.at[5], way["down"])
+    join(8)
+    hop_ru = net.start(slots.at[8], hop_in.at[4], way["up"])
     run(1)
     far_x.wait_recv()
     kin[15] = push(14, 15, sib)
     combine(1)
+    gather(2)
+    g_copies = fetch_g(3)
+    join(6)
+    hop_xd = net.start(slots.at[6], hop_in.at[2], way["down"])
+    join(10)
+    hop_xu = net.start(slots.at[10], hop_in.at[3], way["up"])
+    run(2)
+    combine(2)
+    first_x.wait()
     gather(3)
-    g_copies = fetch_g(2)
+    join(14)
+    hop_a = [net.start(half(slots.at[14], i), half(hop_in.at[0], i), way["across"]) for i in range(2)]
+    join(12)
     run(3)
+    far = []
+    for i, to in enumerate(("up", "down")):
+        hop_a[i].wait_recv()
+        ref, other = half(slots.at[12], i), half(hop_in.at[0], i)
+        ref[...] = (ref[...].astype(f32) + other[...].astype(f32)).astype(bf16)
+        far.append(net.start(ref, half(hop_in.at[1], i), way[to]))
     combine(3)
-    gather(2)
-    join(3, 1)
-    hop_a = net.start(slots.at[14], hop_in.at[0], way["across"])
-    join(3, 0)
-    run(2)
-    hop_a.wait_recv()
-    slots[12] = (slots[12].astype(f32) + hop_in[0].astype(f32)).astype(bf16)
-    hop_u = net.start(slots.at[12, pl.ds(0, 128)], hop_in.at[1, pl.ds(0, 128)], way["up"])
-    hop_d = net.start(slots.at[12, pl.ds(128, 128)], hop_in.at[1, pl.ds(128, 128)], way["down"])
-    combine(2)
-
-    w_copies = [[], []]
-
-    def weight_grad(piece):
-        e, dx = piece // 2, piece % 2
-        buffer = 0
-        for copy in w_copies[buffer]:
+
+    w_copies = []
+
+    far_grads = []
+
+    def send_far(dx):
+        for copy in w_copies:
+            copy.wait()
+        w_copies.clear()
+        rows = pl.ds(pl.multiple_of(here.seq_at(2, dx) * 128, 128), 128)
+        for e, to in enumerate(("up", "down")):
+            far_grads.append(net.start(grads_out.at[e, rows], far_out.at[dx, e], ring[to]))
+
+    def weight_grad(e, dx):
+        free_stage()
+        for copy in w_copies:
             copy.wait()
         xl = 1 - here.xl if dx else here.xl
         columns = pl.ds(pl.multiple_of(xl * 512, 512), 512)
-        w_stage[buffer, :, 0 : 2 * F] = t_dot(rows_x[e, :, columns], rows_u[e]).astype(bf16)
-        w_stage[buffer, :, 2 * F : 3 * F] = t_dot(rows_p[e, :, columns], rows_h[e]).astype(bf16)
-        w_copies[buffer] = [
+        for wide, left, right in (
+            (slice(0, 2 * F), rows_x, rows_u), (slice(2 * F, 3 * F), rows_p, rows_h)
+        ):
+            result = t_dot(left[e, :, columns], right[e]).astype(bf16)
+            for y in range(4):
+                stage[y, 0:128, wide] = result[128 * y : 128 * (y + 1)]
+        w_copies[:] = [
             local(
-                w_stage.at[buffer, pl.ds(128 * y, 128)],
+                stage.at[y, pl.ds(0, 128)],
                 grads_out.at[e, pl.ds(pl.multiple_of(xl * 512 + 128 * y, 128), 128)],
             )
             for y in range(4)
         ]
 
-    join(1, 1)
-    hop_xd = net.start(slots.at[6], hop_in.at[2], way["down"])
-    join(2, 1)
-    hop_xu = net.start(slots.at[10], hop_in.at[3], way["up"])
-    join(1, 0)
-    join(2, 0)
-    weight_grad(0)
-    hop_u.wait_recv()
-    slots[8, 0:128, :] = (slots[8, 0:128, :].astype(f32) + hop_in[1, 0:128, :].astype(f32)).astype(bf16)
-    hop_ru = net.start(slots.at[8], hop_in.at[4], way["up"])
-    hop_d.wait_recv()
-    slots[4, 128:256, :] = (slots[4, 128:256, :].astype(f32) + hop_in[1, 128:256, :].astype(f32)).astype(bf16)
-    hop_rd = net.start(slots.at[4], hop_in.at[5], way["down"])
-    join(0, 1)
-    join(0, 0)
-    weight_grad(1)
+    weight_grad(0, 1)
+    relay = []
+    for i, to in enumerate(("up", "down")):
+        far[i].wait_recv()
+        relay.append(net.start(half(hop_in.at[1], i), half(hop_in.at[7], i), way[to]))
+    join(2)
     hop_xd.wait_recv()
     hop_xu.wait_recv()
     slots[2] = (slots[2].astype(f32) + hop_in[2].astype(f32) + hop_in[3].astype(f32)).astype(bf16)
     hop_rx = net.start(slots.at[2], hop_in.at[6], way["across"])
-    weight_grad(2)
-    weight_grad(3)
-    hop_ru.wait_recv()
-    hop_rd.wait_recv()
-    hop_rx.wait_recv()
+    join(0)
+    weight_grad(1, 1)
+    send_far(1)
+    weight_grad(0, 0)
+    weight_grad(1, 0)
+    send_far(0)
+    for copy in (hop_ru, hop_rd, hop_rx, *relay, *far_grads, *y_sent):
+        copy.wait_recv()
     total = (
-        slots[0].astype(f32) + hop_in[4].astype(f32) + hop_in[5].astype(f32) + hop_in[6].astype(f32)
+        slots[0].astype(f32)
+        + hop_in[4].astype(f32)
+        + hop_in[5].astype(f32)
+        + hop_in[6].astype(f32)
+        + hop_in[7].astype(f32)
     )
     row_out[...] = total[:, 0:D]
     gate_out[...] = total[:, D:WIDE]
-    for copies in (*w_copies, state["y"]):
-        for copy in copies:
-            copy.wait()
-    waited = {id(copy) for k in range(16) for copy in sent[k]}
+    waited = {id(copy) for copies in (*sent.values(), y_sent) for copy in copies}
     for copy in net.all:
         if id(copy) not in waited:
             copy.wait_send()
@@ -1005,17 +1320,19 @@
     return pl.pallas_call(
         moe_kernel,
         in_specs=[any_space, any_space, vmem, vmem, any_space, any_space],
-        out_specs=[vmem, vmem, any_space, any_space],
+        out_specs=[vmem, vmem, any_space, any_space, any_space, any_space],
         out_shape=[
             jax.ShapeDtypeStruct((TOKENS, D), f32),
             jax.ShapeDtypeStruct((TOKENS, 128), f32),
-            jax.ShapeDtypeStruct((16, TOKENS, D), bf16),
+            jax.ShapeDtypeStruct((8, TOKENS, D), bf16),
+            jax.ShapeDtypeStruct((8, TOKENS, D), bf16),
             jax.ShapeDtypeStruct((2, D, 3 * F), bf16),
+            jax.ShapeDtypeStruct((2, 2, 128, 3 * F), bf16),
         ],
         scratch_shapes=[
             pltpu.VMEM((16, TOKENS, WIDE), bf16),
             pltpu.VMEM((8, TOKENS, WIDE), bf16),
-            pltpu.VMEM((7, TOKENS, WIDE), bf16),
+            pltpu.VMEM((8, TOKENS, WIDE), bf16),
             pltpu.VMEM((4, TOKENS, D), bf16),
             pltpu.VMEM((2, D, 2 * F), bf16),
             pltpu.VMEM((2, D, F), bf16),
@@ -1028,11 +1345,10 @@
             pltpu.VMEM((4, 2 * SLOTS, TOKENS), bf16),
             pltpu.VMEM((2, GROUP_ROWS, D), bf16),
             pltpu.VMEM((2, GROUP_ROWS, WIDE), bf16),
-            pltpu.VMEM((4, TOKENS, D), bf16),
-            pltpu.VMEM((1, 512, 3 * F), bf16),
+            pltpu.VMEM((4, TOKENS, 3 * F), bf16),
             pltpu.SemaphoreType.DMA((56,)),
-            pltpu.SemaphoreType.DMA((40,)),
-            pltpu.SemaphoreType.DMA((40,)),
+            pltpu.SemaphoreType.DMA((50,)),
+            pltpu.SemaphoreType.DMA((50,)),
         ],
         compiler_params=pltpu.CompilerParams(
             collective_id=4, has_side_effects=True, vmem_limit_bytes=63 * 1024 * 1024
@@ -1040,148 +1356,6 @@
         cost_estimate=pl.CostEstimate(flops=32 * 10**9, bytes_accessed=40 << 20, transcendentals=1 << 21),
         name="moe",
     )(x, g_all, masks, router_t, up, down)
-def reduce_kernel(
-    parts_ref, small_ref, out_ref, small_out,
-    acc, sib_in, small_acc, small_sib, hop_a, hop_b, late_a, late_b, small_s, small_f, total, local_sems,
-    send_sems, recv_sems,
-):
-    here = Place()
-    c, s = here.core, here.seq
-    f = here.z * 2 + here.xh
-    sib = here.sibling()
-    ways = {"seq": here.plane("seq"), "fsdp": here.plane("fsdp")}
-    others = [(2, 1), (2, 0), (0, 1), (1, 1), (-1, 1), (1, 0), (-1, 0)]
-
-    def f_at(ring, pair):
-        return lax.rem(here.z + ring + 4, 4) * 2 + (1 - here.xh if pair else here.xh)
-
-    seq_peers = [{"seq": here.seq_at(ring, pair)} for ring, pair in others]
-    fsdp_peers = [{"fsdp": here.fsdp_at(ring, pair)} for ring, pair in others]
-    own = pltpu.make_async_copy(parts_ref.at[c], acc, local_sems.at[0])
-    own.start()
-    meet([sib, *seq_peers, *fsdp_peers])
-    net = Copies(send_sems, recv_sems)
-    joins = [
-        net.start(parts_ref.at[1 - c, pl.ds(2 * i, 2)], sib_in.at[pl.ds(2 * i, 2)], sib) for i in range(4)
-    ]
-    small_join = net.start(small_ref.at[:, :, 1 - c], small_sib, sib)
-    own.wait()
-    small_join.wait_recv()
-    small_acc[...] = small_ref[:, :, c] + small_sib[...]
-    small_copies = [
-        net.start(small_acc.at[here.seq_at(*others[i])], small_s.at[i], seq_peers[i]) for i in range(7)
-    ]
-    for i in range(4):
-        joins[i].wait_recv()
-        part = slice(2 * i, 2 * i + 2)
-        acc[part] = (acc[part].astype(f32) + sib_in[part].astype(f32)).astype(bf16)
-
-    def add_to(ref, *values):
-        result = ref[...].astype(f32)
-        for value in values:
-            result = result + value[...].astype(f32)
-        ref[...] = result.astype(bf16)
-
-    def plane(part, hop, way):
-        def half(ref, high):
-            return ref.at[pl.ds(4 * high, 4)]
-
-        a = net.start(part(2, 1), hop.at[0], way["across"])
-        xd = net.start(part(-1, 1), hop.at[2], way["down"])
-        xu = net.start(part(1, 1), hop.at[3], way["up"])
-        yield
-        a.wait_recv()
-        add_to(part(2, 0), hop.at[0])
-        u = net.start(half(part(2, 0), 0), half(hop.at[1], 0), way["up"])
-        d = net.start(half(part(2, 0), 1), half(hop.at[1], 1), way["down"])
-        yield
-        xd.wait_recv()
-        xu.wait_recv()
-        add_to(part(0, 1), hop.at[2], hop.at[3])
-        rx = net.start(part(0, 1), hop.at[6], way["across"])
-        yield
-        u.wait_recv()
-        add_to(half(part(1, 0), 0), half(hop.at[1], 0))
-        ru = net.start(part(1, 0), hop.at[4], way["up"])
-        d.wait_recv()
-        add_to(half(part(-1, 0), 1), half(hop.at[1], 1))
-        rd = net.start(part(-1, 0), hop.at[5], way["down"])
-        yield
-        rx.wait_recv()
-        ru.wait_recv()
-        rd.wait_recv()
-        add_to(part(0, 0), hop.at[4], hop.at[5], hop.at[6])
-
-    low, high = pl.ds(0, GCOLS // 2), pl.ds(GCOLS // 2, GCOLS // 2)
-    first = plane(lambda ring, pair: acc.at[here.seq_at(ring, pair), :, :, low], hop_a, ways["seq"])
-    second = plane(lambda ring, pair: acc.at[:, f_at(ring, pair), :, high], hop_b, ways["fsdp"])
-    for _ in range(4):
-        next(first)
-        next(second)
-    for copy in small_copies:
-        copy.wait_recv()
-    mine = small_acc[s]
-    for i in range(7):
-        mine = mine + small_s[i]
-    small_acc[s] = mine
-    small_copies = [
-        net.start(small_acc.at[s, f_at(*others[i])], small_f.at[i], fsdp_peers[i]) for i in range(7)
-    ]
-    next(first, None)
-    a = [
-        net.start(acc.at[s, f_at(*others[i]), :, low], late_a.at[i], fsdp_peers[i]) for i in range(7)
-    ]
-    next(second, None)
-    b = [
-        net.start(acc.at[here.seq_at(*others[i]), f, :, high], late_b.at[i], seq_peers[i]) for i in range(7)
-    ]
-    for copy in small_copies:
-        copy.wait_recv()
-    mine = small_acc[s, f]
-    for i in range(7):
-        mine = mine + small_f[i]
-    small_out[...] = mine
-    for cols, copies, late in ((slice(0, GCOLS // 2), a, late_a), (slice(GCOLS // 2, GCOLS), b, late_b)):
-        for copy in copies:
-            copy.wait_recv()
-        result = acc[s, f, :, cols].astype(f32)
-        for i in range(7):
-            result = result + late[i].astype(f32)
-        total[:, cols] = result
-    theirs = pl.ds(pl.multiple_of(8 * (1 - c), 8), 8)
-    last = net.start(total.at[theirs], out_ref.at[c], sib)
-    out_ref[c] = total[pl.ds(pl.multiple_of(8 * c, 8), 8), :]
-    last.wait_recv()
-    net.finish()
-
-
-def reduce_weights(parts, small):
-    vmem = pl.BlockSpec(memory_space=pltpu.VMEM)
-    n = 1 + 4 + 7 + 7 + 14 + 16 + 4
-    return pl.pallas_call(
-        reduce_kernel,
-        in_specs=[pl.BlockSpec(memory_space=pl.ANY), vmem],
-        out_specs=[vmem, vmem],
-        out_shape=[jax.ShapeDtypeStruct((2, 8, GCOLS), f32), jax.ShapeDtypeStruct((8, 128), f32)],
-        scratch_shapes=[
-            pltpu.VMEM((8, 8, 16, GCOLS), bf16),
-            pltpu.VMEM((8, 8, 16, GCOLS), bf16),
-            pltpu.VMEM((8, 8, 8, 128), f32),
-            pltpu.VMEM((8, 8, 8, 128), f32),
-            pltpu.VMEM((7, 8, 16, GCOLS // 2), bf16),
-            pltpu.VMEM((7, 8, 16, GCOLS // 2), bf16),
-            pltpu.VMEM((7, 16, GCOLS // 2), bf16),
-            pltpu.VMEM((7, 16, GCOLS // 2), bf16),
-            pltpu.VMEM((7, 8, 8, 128), f32),
-            pltpu.VMEM((7, 8, 128), f32),
-            pltpu.VMEM((16, GCOLS), f32),
-            pltpu.SemaphoreType.DMA((1,)),
-            pltpu.SemaphoreType.DMA((n,)),
-            pltpu.SemaphoreType.DMA((n,)),
-        ],
-        compiler_params=pltpu.CompilerParams(collective_id=3, has_side_effects=True, vmem_limit_bytes=VMEM),
-        name="reduce_weights",
-    )(parts, small)
 
 
 def on_device(
@@ -1191,27 +1365,11 @@
     x = tokens.reshape(TOKENS, D)
     cot = cotangent.reshape(TOKENS, D)
     route_ids = routes.reshape(TOKENS, TOPK)
-    expert_ids = jnp.arange(EXPERTS, dtype=jnp.int32)
-    named = jnp.any(route_ids[:, :, None] == expert_ids[None, None, :], axis=1)
-    small = jnp.concatenate(
-        [
-            router_weight,
-            attn_gain[:, None],
-            ffn_gain[:, None],
-            jnp.broadcast_to(qk_gain[:, None], (8, 1)),
-            jnp.zeros((8, 93), bf16),
-        ],
-        axis=1,
+    whole, masks, side = gather_weights(
+        qkv_weight, out_weight, router_weight, attn_gain.reshape(1, 8), ffn_gain.reshape(1, 8),
+        qk_gain.reshape(1, 1), route_ids, cot,
     )
-    halves = jnp.stack(
-        [
-            jnp.concatenate([qkv_weight[:, :1024], out_weight[:, :512], small], axis=1),
-            jnp.concatenate([qkv_weight[:, 1024:], out_weight[:, 512:], small], axis=1),
-        ]
-    ).astype(f32)
-    whole, masks = gather_weights(halves, named.T.astype(bf16))
     whole = whole.reshape(2, D, WCOLS)
-    g_all = lax.all_gather(cot[None], "fsdp", axis=0, tiled=True)
 
     positions = lax.axis_index("seq") * TOKENS + jnp.arange(TOKENS, dtype=jnp.int32)
     half_dim = HEAD_SIZE // 2
@@ -1222,18 +1380,16 @@
     cos = jnp.concatenate([cos, cos, cos, cos], axis=1)
     sin = jnp.concatenate([-sin, sin, -sin, sin], axis=1)
 
-    heads, full, logs, attended, after, normed_ffn, gates, small_t, raw = front(x, whole, route_ids, cos, sin)
-    row_sum, gate_sum, y_all, expert_grads = moe(
-        normed_ffn, g_all, masks, small_t[:EXPERTS], gate_up_weight, down_weight
+    heads, g_all, full, logs, attended, after, normed_ffn, gates, small_t, raw = front(
+        x, whole, route_ids, cos, sin, cot, side
     )
-    expert_part = lax.psum_scatter(expert_grads, "seq", scatter_dimension=1, tiled=True).astype(f32)
-    layer_out, token_grad, parts, small = back(
-        row_sum, gate_sum, gates, after, x, cot, attended, normed_ffn, small_t, raw,
-        heads, full, logs, cos, sin, whole, y_all,
+    row_sum, gate_sum, y_own, y_other, expert_grads, far = moe(
+        normed_ffn, g_all, masks, small_t, gate_up_weight, down_weight
     )
-    parts, small = reduce_weights(parts.reshape(2, 8, 8, 16, GCOLS), small.reshape(8, 8, 2, 8, 128))
-    qkv_part = jnp.concatenate([parts[0, :, :1024], parts[1, :, :1024]], axis=1)
-    out_part = jnp.concatenate([parts[0, :, 1024:], parts[1, :, 1024:]], axis=1)
+    layer_out, token_grad, qkv_part, out_part, small, up_part, down_part = back(
+        gate_sum, gates, after, x, cot, attended, normed_ffn, small_t, heads, full, logs, cos, sin,
+        row_sum, raw, whole, y_own, y_other, expert_grads, far,
+    )
     return (
         layer_out.reshape(1, TOKENS, D),
         token_grad.reshape(1, TOKENS, D),
@@ -1243,8 +1399,8 @@
         out_part,
         small[:, EXPERTS + 1],
         small[:, :EXPERTS],
-        expert_part[:, :, : 2 * F],
-        expert_part[:, :, 2 * F :],
+        up_part,
+        down_part,
     )
 
 

time: 384 us -> 344 us (0.90)
  Pallas kernels: 340 us -> 318 us
  between operations: 15.2 us -> 1.8 us
    pallas_call x3 -> x2, Pallas kernels: 177 us -> 162 us  [the longest x1 116 us: back(): pl.pallas_call(back_kernel, in_specs=[vmem] * 13 + [hbm] * 7, out_specs=[...]
    unnamed x10, local copies, waits for them, and re-layouts: 3.85 us -> 12.9 us
    slice x5 -> x0, local copies, waits for them, and re-layouts: 6.85 us -> none  [the longest x1 2.12 us: on_device(): expert_part[:, :, :2 * F]]
    pallas_call x1, Pallas kernels: 49.1 us -> 43.1 us  [gather_weights(): pl.pallas_call(gather_kernel, in_specs=[pl.BlockSpec(memory_space=pltpu.V...]
  transfers between devices with their start and end apart: 2 -> 0, of which waited for: 0 -> 0; matrix products, arithmetic and copies ran while one was open for 4% -> 0% of each run, Pallas kernels for 60% -> 0%
where the time goes in v4:
time: 344 us; the launch traced here: 337 us
  Pallas kernels  318 us (92%)
  local copies, waits for them, and re-layouts  15.7 us (5%)
    pallas_call x1, Pallas kernels, back(): pl.pallas_call(back_kernel, in_specs=[vmem] * 13 + [hbm] * 7, out_specs=[...  116 us
    pallas_call x1, Pallas kernels, moe(): pl.pallas_call(moe_kernel, in_specs=[any_space, any_space, vmem, vmem, an...  113 us
    pallas_call x1, Pallas kernels, front(): pl.pallas_call(front_kernel, in_specs=[vmem, hbm, vmem, vmem, vmem, hbm,...  46.6 us
    pallas_call x1, Pallas kernels, gather_weights(): pl.pallas_call(gather_kernel, in_specs=[pl.BlockSpec(memory_space=pltpu.V...  43.1 us
    unnamed x10, local copies, waits for them, and re-layouts  12.9 us

profile of v4, /device:TPU:1, one launch (start us, length us, event | category | flops | bytes accessed | tf_op | source)
XLA Modules:
  0.0 337.5 jit_solution(9992574376547090810)
XLA Ops:
  1.3 1.5 copy.23
  2.8 0.5 fusion
  3.4 1.0 pad_maximum_fusion
  4.3 43.1 %gather_weights.1 = (bf16[2,8,8,16,1664]{4,3,2,1,0:T(8,128)(2,1)}, bf16[16,32,256]{2,1,0:T(8,128)(2,1)}, bf16[256,1024]{1,0:T(8,128)(2,1)}) custom-call(bf16[8,2048]{1,0:T(8,128)(2,1)} %qkv_ref.1, bf16[8,1024]{1,0:T(8,128)(2,1)} %wo_ref.1, bf16[8,32]{1,0:T(8,128)(2,1)} %router_ref.1, bf16[1,8]{1,0:T(2,128)(2,1)} %bitcast.20, bf16[1,8]{1,0:T(2,128)(2,1)} %bitcast.21, ...), custom_call_target="tpu_custom_call" | custom-call | tf_op jit(solution)/shard_map/gather_weights/pallas_call | solution.py:1007
  47.4 46.6 %front.1 = (bf16[8,256,256]{2,1,0:T(8,128)(2,1)}, bf16[16,256,1024]{2,1,0:T(8,128)(2,1)}, f32[2048,128]{1,0:T(8,128)}, f32[2048,128]{1,0:T(8,128)}, bf16[256,102...) custom-call(bf16[256,1024]{1,0:T(8,128)(2,1)} %bitcast.24, ...), custom_call_target="tpu_custom_call" | custom-call | flops 4000000000 | bytes 16777216 | tf_op jit(solution)/shard_map/front/pallas_call | solution.py:329
  94.1 113.3 %moe.1 = (f32[256,1024]{1,0:T(8,128)}, f32[256,128]{1,0:T(8,128)}, bf16[8,256,1024]{2,1,0:T(8,128)(2,1)}, bf16[8,256,1024]{2,1,0:T(8,128)(2,1)}, bf16[2,1024,153...) custom-call(bf16[256,1024]{1,0:T(8,128)(2,1)} %get-tuple-element.38.x_ref.normed_ref, ...), custom_call_target="tpu_custom_call" | custom-call | flops 32000000000 | bytes 41943040 | tf_op jit(solution)/shard_map/moe/pallas_call | solution.py:1320
  207.3 115.5 %back.1 = (bf16[256,1024]{1,0:T(8,128)(2,1)}, f32[256,1024]{1,0:T(8,128)}, f32[8,2048]{1,0:T(8,128)}, f32[8,1024]{1,0:T(8,128)}, f32[8,128]{1,0:T(8,128)}, /*ind...) custom-call(f32[256,128]{1,0:T(8,128)} %get-tuple-element.42.gate_sum_ref, f32[256,128]{1,0:T(8,128)} %get-tuple-element.43.gates_ref, ...), custom_call_target="tpu_custom_call" | custom-call | flops 8999999488 | bytes 33554432 | tf_op jit(solution)/shard_map/back/pallas_call | solution.py:828
  322.9 0.0 copy-start
  322.9 1.3 slice.13
  324.2 1.5 slice_reduce_fusion
  325.7 1.9 copy.33
  327.5 2.3 copy.34
  329.8 1.5 copy.35
  331.3 1.4 copy.36
  332.7 1.3 copy.37
  334.0 2.3 copy.38
  336.3 0.0 copy-done
  336.3 0.8 copy.39
  (2 shorter events, 0.0 us)
Async XLA Ops:
  322.9 13.4 %copy-start = (f32[2,128,512]{2,1,0:T(8,128)S(1)}, f32[2,128,512]{2,1,0:T(8,128)}, u32[]{:S(2)}) copy-start(f32[2,128,512]{2,1,0:T(8,128)} %get-tuple-element.88) | copy-start | bytes 1572868

commit v5 on v4

--- a/solution.py
+++ b/solution.py
@@ -1,7 +1,6 @@
-import math
-
 import jax
 import jax.numpy as jnp
+import numpy as np
 from jax import lax
 from jax.experimental import pallas as pl
 from jax.experimental.pallas import tpu as pltpu
@@ -19,7 +18,6 @@
 LENGTH = SEQ * TOKENS
 GROUP_ROWS = 4 * SLOTS
 ROWS = 4 * GROUP_ROWS
-WIDE = D + 128
 GCOLS = 1536
 VMEM = 60 * 1024 * 1024
 
@@ -125,6 +123,22 @@
     )
 
 
+def rotary_tables():
+    inverse = rope_base ** (-2.0 * (np.arange(128) % 32) / HEAD_SIZE)
+    near = np.arange(TOKENS)[:, None] * inverse[None, :]
+    far = TOKENS * np.arange(SEQ)[:, None] * inverse[None, :]
+    return [jnp.asarray(np.stack([np.cos(a), np.sin(a)]), f32) for a in (near, far)]
+
+
+def rotary(near_ref, far_ref, block, lanes):
+    pick = lax.broadcasted_iota(jnp.int32, (SEQ, 128), 0) == block
+    far_cos = jnp.sum(jnp.where(pick, far_ref[0], 0.0), axis=0, keepdims=True)
+    far_sin = jnp.sum(jnp.where(pick, far_ref[1], 0.0), axis=0, keepdims=True)
+    cos = near_ref[0] * far_cos - near_ref[1] * far_sin
+    sin = near_ref[1] * far_cos + near_ref[0] * far_sin
+    return cos, jnp.where(lax.rem(lanes, HEAD_SIZE) < HEAD_SIZE // 2, -sin, sin)
+
+
 def row_scale(values):
     return lax.rsqrt(jnp.mean(values * values, axis=1, keepdims=True) + epsilon)
 
@@ -140,8 +154,8 @@
 
 
 def front_kernel(
-    x_ref, w_ref, routes_ref, cos_ref, sin_ref, cot_ref, side_ref,
-    heads_out, g_out, full_ref, logs_ref, att_ref, after_ref, normed_ref, gates_ref, small_t_ref, raw_ref,
+    x_ref, w_ref, routes_ref, near_ref, far_place_ref, cot_ref, side_ref,
+    heads_out, g_out, full_ref, logs_ref, att_ref, after_ref, normed_ref, gates_ref, small_t_ref, raw_ref, gates_t_ref,
     wq, wkv, wo, small, send, heads, out_buf, att, key0, key1, value,
     local_sems, send_sems, recv_sems,
 ):
@@ -160,12 +174,6 @@
         )
     ]
     for copy in loads:
-        copy.start()
-    own_g = [
-        pltpu.make_async_copy(cot_ref, g_out.at[here.fsdp], local_sems.at[6]),
-        pltpu.make_async_copy(side_ref, g_out.at[here.fsdp_at(0, 1)], local_sems.at[7]),
-    ]
-    for copy in own_g:
         copy.start()
     peers = [here.seq_at(*other) for other in OTHERS]
     sib = here.sibling()
@@ -218,7 +226,7 @@
     x = x_ref[...].astype(f32)
     normed = (x * row_scale(x) * small_t[32:33, :].astype(f32)).astype(bf16)
     query_gain, key_gain = gain_tiles(small_t, lanes)
-    cos, sin = cos_ref[...], sin_ref[...]
+    cos, sin = rotary(near_ref, far_place_ref, me, lanes)
     loads[1].wait()
     queries = dot(normed, wq[...])
     loads[2].wait()
@@ -307,29 +315,34 @@
     normed = (after_ref[...] * scaling * small_t[33:34, :].astype(f32)).astype(bf16)
     normed_ref[...] = normed
     logits = dot(normed, small[...])
-    named = jnp.zeros((TOKENS, 128), f32)
+    expert = lax.broadcasted_iota(jnp.int32, (128, TOKENS), 0)
+    named = jnp.zeros((128, TOKENS), f32)
     for k in range(TOPK):
-        named = jnp.where(routes_ref[:, k : k + 1] == lanes, 1.0, named)
+        named = jnp.where(routes_ref[k : k + 1, :] == expert, 1.0, named)
+    named = jnp.transpose(named)
     peak = jnp.max(jnp.where(named > 0.0, logits, -1e30), axis=1, keepdims=True)
     chosen = jnp.where(named > 0.0, jnp.exp(logits - peak), 0.0)
-    gates_ref[...] = chosen / jnp.sum(chosen, axis=1, keepdims=True)
+    gates = chosen / jnp.sum(chosen, axis=1, keepdims=True)
+    gates_ref[...] = gates
+    across = jnp.transpose(gates)
+    gates_t_ref[...] = jnp.zeros_like(gates_t_ref)
+    for i in range(FSDP):
+        gates_t_ref[i, 0:2, :] = across[2 * i : 2 * i + 2, :]
     for _ in moves:
         pass
     save.wait()
-    for copy in own_g:
-        copy.wait()
     for i in range(7):
         answer(i).wait_send()
     net.finish()
 
 
-def front(x, whole, routes, cos, sin, cot, side):
+def front(x, whole, routes, near, far, cot, side):
     vmem = pl.BlockSpec(memory_space=pltpu.VMEM)
     hbm = pl.BlockSpec(memory_space=pl.ANY)
     return pl.pallas_call(
         front_kernel,
         in_specs=[vmem, hbm, vmem, vmem, vmem, hbm, hbm],
-        out_specs=[hbm] * 2 + [vmem] * 8,
+        out_specs=[hbm] * 2 + [vmem] * 9,
         out_shape=[
             jax.ShapeDtypeStruct((8, TOKENS, 256), bf16),
             jax.ShapeDtypeStruct((FSDP, TOKENS, D), bf16),
@@ -341,6 +354,7 @@
             jax.ShapeDtypeStruct((TOKENS, 128), f32),
             jax.ShapeDtypeStruct((128, D), bf16),
             jax.ShapeDtypeStruct((12, TOKENS, 128), f32),
+            jax.ShapeDtypeStruct((FSDP, 8, TOKENS), f32),
         ],
         scratch_shapes=[
             pltpu.VMEM((D, 1024), bf16),
@@ -363,7 +377,7 @@
             flops=4 * 10**9, bytes_accessed=16 << 20, transcendentals=2 * LENGTH * LENGTH
         ),
         name="front",
-    )(x, whole, routes, cos, sin, cot, side)
+    )(x, whole, routes, near, far, cot, side)
 
 
 def split3(values):
@@ -384,7 +398,7 @@
 
 def back_kernel(
     gate_sum_ref, gates_ref, after_ref, x_ref, cot_ref, att_ref, normed_ref, small_t_ref,
-    heads_ref, full_ref, logs_ref, cos_ref, sin_ref, row_ref, raw_ref, w_ref, y_ref, y_other, grads_ref, far_ref,
+    heads_ref, full_ref, logs_ref, near_ref, far_place_ref, row_ref, raw_ref, w_ref, y_ref, y_other, grads_ref, far_ref,
     layer_ref, token_ref, qkv_out, wo_out, small_out, up_out, down_out,
     wqkv, wo, send, grads, back_q, back_kv, pg, after_grad,
     key0, key1, value0, value1, key_t, dk_total, dv_total,
@@ -436,10 +450,8 @@
         copy.start()
     lanes, low_half = lane_halves()
 
-    gate_sum = gate_sum_ref[...]
-    gate_grad = gate_sum + pltpu.roll(gate_sum, 96, 1)
+    gate_grad = gate_sum_ref[...]
     gates = gates_ref[...]
-    gate_grad = jnp.where(lanes < EXPERTS, gate_grad, 0.0)
     chosen = gates * (gate_grad - jnp.sum(gates * gate_grad, axis=1, keepdims=True))
     logits_grad = chosen.astype(bf16)
     loads[4].wait()
@@ -460,13 +472,25 @@
         attended_grad = dot_t(after_low[:, 0:512], wo[0, rows, :]) + dot_t(after_low[:, 512:1024], wo[1, rows, :])
         for h in range(4):
             send[4 * q + h] = attended_grad[:, 128 * h : 128 * (h + 1)].astype(bf16)
-    to_heads = [net.start(send.at[peer], grads.at[me], {"seq": peer}) for peer in peers]
+
+    def delivery(d):
+        peer = lax.rem(me + d, 8)
+        return pltpu.make_async_remote_copy(
+            src_ref=send.at[peer], dst_ref=grads.at[me], send_sem=send_sems.at[92 + d],
+            recv_sem=recv_sems.at[92 + d], device_id={"seq": peer}, device_id_type=MESH,
+        )
+
+    for d in range(7, 0, -1):
+        delivery(d).start()
     grads[me] = send[me]
     router_grad = t_dot(normed_ref[...], logits_grad)
     small[...] = router_grad.reshape(8, 8, 2, 8, 128)
     for h in range(2):
         out_grad = t_dot(att_ref[...], after_low[:, 512 * h : 512 * (h + 1)]).astype(bf16)
         parts[h, :, :, :, 1024:1536] = out_grad.reshape(8, 8, 16, 512)
+    out_join = net.start(
+        parts.at[1 - here.core, :, :, :, pl.ds(1024, 512)], parts_in.at[:, :, :, pl.ds(1024, 512)], sib
+    )
 
     def add_to(ref, *values):
         result = ref[...].astype(f32)
@@ -570,19 +594,22 @@
         key_t[:, rows] = jnp.transpose(pair)[0:64, :].astype(bf16)
     dk_total[...] = jnp.zeros_like(dk_total)
     dv_total[...] = jnp.zeros_like(dv_total)
-    for copy in to_heads:
-        copy.wait_recv()
     columns = pl.ds(pl.multiple_of(me * 128, 128), 128)
 
     def answer(i):
-        j = lax.rem(me + 1 + i, 8)
+        j = lax.rem(me + i, 8)
         return pltpu.make_async_remote_copy(
-            src_ref=grads.at[j], dst_ref=back_q.at[:, columns], send_sem=send_sems.at[92 + i],
-            recv_sem=recv_sems.at[92 + i], device_id={"seq": j}, device_id_type=MESH,
+            src_ref=grads.at[j], dst_ref=back_q.at[:, columns], send_sem=send_sems.at[84 + i],
+            recv_sem=recv_sems.at[84 + i], device_id={"seq": j}, device_id_type=MESH,
         )
 
     def block(i, carry):
-        j = lax.rem(me + 1 + i, 8)
+        j = lax.rem(me + i, 8)
+
+        @pl.when(i > 0)
+        def _():
+            delivery(8 - i).wait_recv()
+
         rows = pl.ds(pl.multiple_of(j * TOKENS, TOKENS), TOKENS)
         query = heads_ref[j, :, 0:128].astype(f32) * (1.0 / 8.0)
         grad = grads[j].astype(f32)
@@ -617,21 +644,20 @@
         both = jnp.concatenate(dq, axis=0) * (1.0 / 8.0)
         grads[j] = jnp.transpose(both).astype(bf16)
 
-        @pl.when(i < 7)
+        @pl.when(i > 0)
         def _():
             answer(i).start()
 
         return carry
 
+    lax.fori_loop(0, 3, block, 0)
     next(more_moves)
-    lax.fori_loop(0, 3, block, 0)
     next(moves)
     lax.fori_loop(3, 6, block, 0)
     next(moves)
-    next(more_moves)
     lax.fori_loop(6, 8, block, 0)
-    for copy in to_heads:
-        copy.wait_send()
+    for d in range(1, 8):
+        delivery(d).wait_send()
     for c in range(8):
         rows = slice(TOKENS * c, TOKENS * (c + 1))
         dk = dk_total[rows, :]
@@ -653,8 +679,8 @@
     attn_gain = small_t_ref[32:33, :].astype(f32)
     normed = (x * x_scaling * attn_gain).astype(bf16)
     query_gain, key_gain = gain_tiles(small_t_ref[...], lanes)
-    cos, sin = cos_ref[...], sin_ref[...]
-    for i in range(7):
+    cos, sin = rotary(near_ref, far_place_ref, me, lanes)
+    for i in range(1, 8):
         answer(i).wait_recv()
 
     def unturned(grad, tile, gain):
@@ -667,6 +693,7 @@
 
     for copy in raw:
         copy.wait()
+    next(more_moves)
     query_terms = jnp.zeros((1, 128), f32)
     for h in range(8):
         part = slice(128 * h, 128 * (h + 1))
@@ -694,8 +721,13 @@
             parts[h, 2 * r : 2 * r + 2, :, :, 0:1024] = result.reshape(2, 8, 16, 1024)
             if turn == 0:
                 sib_joins.append(
-                    net.start(parts.at[h, pl.ds(2 * r, 2)], parts_in.at[pl.ds(2 * r, 2)], sib)
+                    net.start(
+                        parts.at[h, pl.ds(2 * r, 2), :, :, pl.ds(0, 1024)],
+                        parts_in.at[pl.ds(2 * r, 2), :, :, pl.ds(0, 1024)],
+                        sib,
+                    )
                 )
+    out_join.wait_recv()
     for r in range(4):
         sib_joins[r].wait_recv()
         for q in (2 * r, 2 * r + 1):
@@ -817,9 +849,9 @@
     qkv_out[:, 1024:2048] = right[:, 0:1024]
     wo_out[:, 0:512] = left[:, 1024:1536]
     wo_out[:, 512:1024] = right[:, 1024:1536]
-    for i in range(7):
+    for i in range(1, 8):
         answer(i).wait_send()
-    net.finish(to_heads)
+    net.finish()
 
 
 def back(*operands):
@@ -881,6 +913,32 @@
     )(*operands)
 
 
+def finish_kernel(layer, token, up, down, qkv, wo, small, *outs):
+    for src, dst in zip((layer, token, up, down, qkv, wo), outs):
+        dst[...] = src[...]
+    router, attn, ffn, head = outs[6:]
+    same = lax.broadcasted_iota(jnp.int32, (8, 8), 0) == lax.broadcasted_iota(jnp.int32, (8, 8), 1)
+    values = small[...]
+    router[...] = values[:, 0:EXPERTS]
+    for ref, lane in ((attn, EXPERTS), (ffn, EXPERTS + 1)):
+        ref[...] = jnp.sum(jnp.where(same, values[:, lane : lane + 1], 0.0), axis=0, keepdims=True)
+    head[...] = values[0:1, EXPERTS + 2 : EXPERTS + 3]
+
+
+def finish(*operands):
+    vmem = pl.BlockSpec(memory_space=pltpu.VMEM)
+    small = [(8, EXPERTS), (1, 8), (1, 8), (1, 1)]
+    return pl.pallas_call(
+        finish_kernel,
+        in_specs=[vmem] * 7,
+        out_specs=[vmem] * 10,
+        out_shape=[jax.ShapeDtypeStruct(a.shape, a.dtype) for a in operands[:6]]
+        + [jax.ShapeDtypeStruct(shape, f32) for shape in small],
+        compiler_params=pltpu.CompilerParams(vmem_limit_bytes=VMEM),
+        name="finish",
+    )(*operands)
+
+
 def gather_kernel(
     qkv_ref, wo_ref, router_ref, attn_ref, ffn_ref, head_ref, routes_ref, cot_ref, out_ref, masks_out, side_out,
     in_ref, mask_ref, stage, block, local_sems, send_sems, recv_sems,
@@ -901,10 +959,11 @@
         in_ref[h, :, 1024:1536] = wo_ref[:, 512 * h : 512 * (h + 1)].astype(f32)
         in_ref[h, :, 1536:1664] = gains
         in_ref[h, :, 1536:1568] = router_ref[...].astype(f32)
-    named = jnp.zeros((256, 128), f32)
+    expert = lax.broadcasted_iota(jnp.int32, (32, 256), 0)
+    named = jnp.zeros((32, 256), f32)
     for k in range(8):
-        named = jnp.where(routes_ref[:, k : k + 1] == lanes, 1.0, named)
-    mask_ref[...] = jnp.transpose(named)[0:32, :].astype(bf16)
+        named = jnp.where(routes_ref[k : k + 1, :] == expert, 1.0, named)
+    mask_ref[...] = named.astype(bf16)
     here = Place()
     c, s, f = here.core, here.seq, here.z * 2 + here.xh
     sib = here.sibling()
@@ -1028,10 +1087,10 @@
 
 
 def moe_kernel(
-    x_ref, g_ref, masks_ref, router_ref, up_hbm, down_hbm,
+    x_ref, cot_ref, side_ref, g_ref, masks_ref, gates_ref, up_hbm, down_hbm,
     row_out, gate_out, y_out, y_in, grads_out, far_out,
-    slots, sib_in, hop_in, g_rows, up_ref, down_ref,
-    rows_x, rows_p, rows_h, rows_u, rows_g, slot_gate, places, stage_y, stage_r, stage,
+    slots, spare, gates_in, grads_stage, grads_in, sib_in, hop_in, g_rows, up_ref, down_ref,
+    rows_x, rows_p, rows_h, rows_u, rows_g, slot_gate, places, ranks, stage_y, stage_r, stage,
     local_sems, send_sems, recv_sems,
 ):
     here = Place()
@@ -1046,7 +1105,7 @@
         copy.start()
         return copy
 
-    first_x = local(x_ref, slots.at[0, :, pl.ds(0, D)])
+    first_x = local(x_ref, slots.at[0])
     weights = [local(up_hbm, up_ref), local(down_hbm, down_ref)]
 
     def source(k):
@@ -1055,18 +1114,23 @@
         xh = 1 - here.xh if pair else here.xh
         return z * 4 + xh * 2 + (1 - here.core if c else here.core)
 
-    groups = ((4, 5, 8, 9), (6, 7, 10, 11), (12, 13, 14, 15), (0, 1, 2, 3))
+    groups = ((4, 5, 8, 9), (0, 1, 2, 3), (6, 7, 10, 11), (12, 13, 14, 15))
 
     def fetch_g(group):
-        return [local(g_ref.at[source(groups[group][s])], g_rows.at[s]) for s in range(4)]
+        near = {0: cot_ref, 2: side_ref}
+        return [
+            local(near[k] if k in near else g_ref.at[source(k)], g_rows.at[s])
+            for s, k in enumerate(groups[group])
+        ]
 
     g_copies = fetch_g(0)
     ring = here.plane("seq")
-    meet([sib, *way.values(), ring["up"], ring["down"]])
+    others = [{"fsdp": source(k)} for k in range(1, 16)]
+    meet([*others, ring["up"], ring["down"]])
     net = Copies(send_sems, recv_sems)
 
     def block(k, low=0, rows=TOKENS):
-        return slots.at[k, pl.ds(low, rows), pl.ds(0, D)]
+        return slots.at[k, pl.ds(low, rows)]
 
     sent = {k: [] for k in range(16)}
 
@@ -1075,10 +1139,26 @@
         sent[k].append(copy)
         return copy
 
+    small = [net.start(gates_ref.at[source(k)], gates_in.at[own], others[k - 1]) for k in range(1, 16)]
+    gates_in[own] = gates_ref[own]
     across = push(0, 2, way["across"], src=x_ref)
     up = push(0, 4, way["up"], src=x_ref)
     down = push(0, 8, way["down"], src=x_ref)
     kin = {1: push(0, 1, sib, src=x_ref)}
+    expert = lax.broadcasted_iota(jnp.int32, (EXPERTS, TOKENS), 0)
+    for k in range(16):
+        named = masks_ref[source(k)].astype(f32)
+        for i in range(2):
+            ranks[2 * k + i : 2 * k + i + 1, :] = jnp.sum(
+                jnp.where(expert == 2 * own + i, named, 0.0), axis=0, keepdims=True
+            )
+    before = (
+        lax.broadcasted_iota(jnp.int32, (TOKENS, TOKENS), 0)
+        < lax.broadcasted_iota(jnp.int32, (TOKENS, TOKENS), 1)
+    ).astype(f32).astype(bf16)
+    second = lax.rem(lax.broadcasted_iota(jnp.int32, (2 * 16, 1), 0), 2).astype(f32)
+    named = ranks[...]
+    ranks[...] = jnp.where(named > 0.0, dot(named.astype(bf16), before) + SLOTS * second, -1000.0)
     up.wait_recv()
     far_low = push(4, 12, way["up"], 0, 128)
     kin[5] = push(4, 5, sib)
@@ -1098,33 +1178,18 @@
     expert = lax.broadcasted_iota(jnp.int32, (EXPERTS, TOKENS), 0)
 
     def gather(group):
-        before = (
-            lax.broadcasted_iota(jnp.int32, (TOKENS, TOKENS), 0)
-            < lax.broadcasted_iota(jnp.int32, (TOKENS, TOKENS), 1)
-        ).astype(f32).astype(bf16)
         for s in range(4):
             k = groups[group][s]
             if k in kin:
                 kin[k].wait_recv()
             g_copies[s].wait()
-            x_rows = slots[k, :, 0:D]
-            named = masks_ref[source(k)].astype(f32)
-            logits = dot_t(router_ref[0:EXPERTS, :], x_rows)
-            peak = jnp.max(jnp.where(named > 0.0, logits, -1e30), axis=0, keepdims=True)
-            parts = jnp.where(named > 0.0, jnp.exp(logits - peak), 0.0)
-            gates = parts / jnp.sum(parts, axis=0, keepdims=True)
-            rank = dot(named.astype(bf16), before)
-            rank = jnp.where(named > 0.0, rank, -1000.0)
-
-            def mine(values, i):
-                return jnp.sum(jnp.where(expert == 2 * own + i, values, 0.0), axis=0, keepdims=True)
-
-            wanted = jnp.where(first, mine(rank, 0), mine(rank, 1) + SLOTS)
+            wanted = jnp.where(first, ranks[2 * k : 2 * k + 1, :], ranks[2 * k + 1 : 2 * k + 2, :])
             hot = jnp.where(slot_place == wanted, 1.0, 0.0)
-            gate = jnp.sum(hot * jnp.where(first, mine(gates, 0), mine(gates, 1)), axis=1, keepdims=True)
+            gates = gates_in[source(k)]
+            gate = jnp.sum(hot * jnp.where(first, gates[0:1, :], gates[1:2, :]), axis=1, keepdims=True)
             hot = hot.astype(bf16)
             places[s] = hot
-            picked = dot(hot, x_rows).astype(bf16)
+            picked = dot(hot, slots[k]).astype(bf16)
             grads = dot(hot, g_rows[s])
             pair = (grads * gate).astype(bf16)
             grads = grads.astype(bf16)
@@ -1154,15 +1219,23 @@
             out = dot_t(hidden, down_ref[e]).astype(bf16).astype(f32)
             gate_grad = jnp.sum(out * rows_g[e].astype(f32), axis=1, keepdims=True)
             stage_y[e] = (out * slot_gate[e][:, 0:1]).astype(bf16)
-            stage_r[e, :, 0:D] = dot_t(rows_u[e, here_rows, :], up_ref[e]).astype(bf16)
-            high = gate_grad.astype(bf16).astype(f32)
-            column = 2 * own + e
-            stage_r[e, :, D:WIDE] = jnp.where(
-                lanes == column, high, jnp.where(lanes == column + EXPERTS, gate_grad - high, 0.0)
-            ).astype(bf16)
+            stage_r[e] = dot_t(rows_u[e, here_rows, :], up_ref[e]).astype(bf16)
+            for s in range(4):
+                hot = places[s, pl.ds(pl.multiple_of(SLOTS * e, SLOTS), SLOTS), :].astype(f32)
+                grads_stage[groups[group][s], e, 0:1, :] = jnp.sum(
+                    hot * gate_grad[SLOTS * s : SLOTS * (s + 1)], axis=0, keepdims=True
+                )
             return carry
 
         lax.fori_loop(0, 2, one, 0)
+        for k in groups[group]:
+            if k:
+                small.append(net.start(grads_stage.at[k], grads_in.at[own], others[k - 1]))
+            else:
+                grads_in[own] = grads_stage[0]
+
+    def result(k):
+        return spare.at[k // 4 - 1] if k in (4, 8) else slots.at[k]
 
     y_sent = []
 
@@ -1177,13 +1250,14 @@
         free_stage()
         for s in range(4):
             k = groups[group][s]
-            for copy in sent[k]:
-                copy.wait_send()
+            if k not in (4, 8):
+                for copy in sent[k]:
+                    copy.wait_send()
             part = slice(SLOTS * s, SLOTS * (s + 1))
             both = jnp.concatenate([stage_y[0, part, :], stage_y[1, part, :]], axis=0)
             stage[s, :, 0:D] = t_dot(places[s], both).astype(bf16)
             both = jnp.concatenate([stage_r[0, part, :], stage_r[1, part, :]], axis=0)
-            slots[k] = t_dot(places[s], both).astype(bf16)
+            result(k)[...] = t_dot(places[s], both).astype(bf16)
         state["y"] = []
         for s in range(4):
             k = groups[group][s]
@@ -1198,55 +1272,52 @@
 
     def join(k):
         state[k].wait_recv()
-        slots[k] = (slots[k].astype(f32) + sib_in[k // 2].astype(f32)).astype(bf16)
+        there = result(k)
+        there[...] = (there[...].astype(f32) + sib_in[k // 2].astype(f32)).astype(bf16)
 
     def half(ref, which):
         return ref.at[pl.ds(128 * which, 128)]
 
+    first_x.wait()
+    for copy in small:
+        copy.wait_recv()
+    small.clear()
     gather(0)
     g_copies = fetch_g(1)
     for copy in weights:
         copy.wait()
     run(0)
+    combine(0)
     far_low.wait_recv()
     far_high.wait_recv()
     far_x = push(12, 14, way["across"])
     kin[13] = push(12, 13, sib)
+    gather(1)
+    g_copies = fetch_g(2)
+    join(4)
+    hop_rd = net.start(result(4), hop_in.at[5], way["down"])
+    join(8)
+    hop_ru = net.start(result(8), hop_in.at[4], way["up"])
+    run(1)
     up_x.wait_recv()
     kin[7] = push(6, 7, sib)
     down_x.wait_recv()
     kin[11] = push(10, 11, sib)
-    combine(0)
-    gather(1)
-    g_copies = fetch_g(2)
-    join(4)
-    hop_rd = net.start(slots.at[4], hop_in.at[5], way["down"])
-    join(8)
-    hop_ru = net.start(slots.at[8], hop_in.at[4], way["up"])
-    run(1)
-    far_x.wait_recv()
-    kin[15] = push(14, 15, sib)
     combine(1)
     gather(2)
     g_copies = fetch_g(3)
+    run(2)
+    far_x.wait_recv()
+    kin[15] = push(14, 15, sib)
+    combine(2)
+    gather(3)
     join(6)
     hop_xd = net.start(slots.at[6], hop_in.at[2], way["down"])
     join(10)
     hop_xu = net.start(slots.at[10], hop_in.at[3], way["up"])
-    run(2)
-    combine(2)
-    first_x.wait()
-    gather(3)
-    join(14)
-    hop_a = [net.start(half(slots.at[14], i), half(hop_in.at[0], i), way["across"]) for i in range(2)]
-    join(12)
+    join(2)
+    join(0)
     run(3)
-    far = []
-    for i, to in enumerate(("up", "down")):
-        hop_a[i].wait_recv()
-        ref, other = half(slots.at[12], i), half(hop_in.at[0], i)
-        ref[...] = (ref[...].astype(f32) + other[...].astype(f32)).astype(bf16)
-        far.append(net.start(ref, half(hop_in.at[1], i), way[to]))
     combine(3)
 
     w_copies = []
@@ -1282,22 +1353,29 @@
         ]
 
     weight_grad(0, 1)
+    join(14)
+    hop_a = [net.start(half(slots.at[14], i), half(hop_in.at[0], i), way["across"]) for i in range(2)]
+    join(12)
+    weight_grad(1, 1)
+    send_far(1)
+    far = []
+    for i, to in enumerate(("up", "down")):
+        hop_a[i].wait_recv()
+        ref, other = half(slots.at[12], i), half(hop_in.at[0], i)
+        ref[...] = (ref[...].astype(f32) + other[...].astype(f32)).astype(bf16)
+        far.append(net.start(ref, half(hop_in.at[1], i), way[to]))
+    weight_grad(0, 0)
+    hop_xd.wait_recv()
+    hop_xu.wait_recv()
+    slots[2] = (slots[2].astype(f32) + hop_in[2].astype(f32) + hop_in[3].astype(f32)).astype(bf16)
+    hop_rx = net.start(slots.at[2], hop_in.at[6], way["across"])
     relay = []
     for i, to in enumerate(("up", "down")):
         far[i].wait_recv()
         relay.append(net.start(half(hop_in.at[1], i), half(hop_in.at[7], i), way[to]))
-    join(2)
-    hop_xd.wait_recv()
-    hop_xu.wait_recv()
-    slots[2] = (slots[2].astype(f32) + hop_in[2].astype(f32) + hop_in[3].astype(f32)).astype(bf16)
-    hop_rx = net.start(slots.at[2], hop_in.at[6], way["across"])
-    join(0)
-    weight_grad(1, 1)
-    send_far(1)
-    weight_grad(0, 0)
     weight_grad(1, 0)
     send_far(0)
-    for copy in (hop_ru, hop_rd, hop_rx, *relay, *far_grads, *y_sent):
+    for copy in (hop_ru, hop_rd, hop_rx, *relay, *far_grads, *y_sent, *small):
         copy.wait_recv()
     total = (
         slots[0].astype(f32)
@@ -1306,20 +1384,25 @@
         + hop_in[6].astype(f32)
         + hop_in[7].astype(f32)
     )
-    row_out[...] = total[:, 0:D]
-    gate_out[...] = total[:, D:WIDE]
-    waited = {id(copy) for copies in (*sent.values(), y_sent) for copy in copies}
+    row_out[...] = total
+    row = lax.broadcasted_iota(jnp.int32, (128, TOKENS), 0)
+    gate_grads = jnp.zeros((128, TOKENS), f32)
+    for f in range(16):
+        for e in range(2):
+            gate_grads = jnp.where(row == 2 * f + e, grads_in[f, e, 0:1, :], gate_grads)
+    gate_out[...] = jnp.transpose(gate_grads)
+    waited = {id(copy) for copies in (*(sent[k] for k in sent if k not in (4, 8)), y_sent) for copy in copies}
     for copy in net.all:
         if id(copy) not in waited:
             copy.wait_send()
 
 
-def moe(x, g_all, masks, router_t, up, down):
+def moe(x, cot, side, g_all, masks, gates, up, down):
     any_space = pl.BlockSpec(memory_space=pl.ANY)
     vmem = pl.BlockSpec(memory_space=pltpu.VMEM)
     return pl.pallas_call(
         moe_kernel,
-        in_specs=[any_space, any_space, vmem, vmem, any_space, any_space],
+        in_specs=[any_space] * 4 + [vmem, vmem, any_space, any_space],
         out_specs=[vmem, vmem, any_space, any_space, any_space, any_space],
         out_shape=[
             jax.ShapeDtypeStruct((TOKENS, D), f32),
@@ -1330,9 +1413,13 @@
             jax.ShapeDtypeStruct((2, 2, 128, 3 * F), bf16),
         ],
         scratch_shapes=[
-            pltpu.VMEM((16, TOKENS, WIDE), bf16),
-            pltpu.VMEM((8, TOKENS, WIDE), bf16),
-            pltpu.VMEM((8, TOKENS, WIDE), bf16),
+            pltpu.VMEM((16, TOKENS, D), bf16),
+            pltpu.VMEM((2, TOKENS, D), bf16),
+            pltpu.VMEM((16, 8, TOKENS), f32),
+            pltpu.VMEM((16, 2, 8, TOKENS), f32),
+            pltpu.VMEM((16, 2, 8, TOKENS), f32),
+            pltpu.VMEM((8, TOKENS, D), bf16),
+            pltpu.VMEM((8, TOKENS, D), bf16),
             pltpu.VMEM((4, TOKENS, D), bf16),
             pltpu.VMEM((2, D, 2 * F), bf16),
             pltpu.VMEM((2, D, F), bf16),
@@ -1343,19 +1430,20 @@
             pltpu.VMEM((2, GROUP_ROWS, D), bf16),
             pltpu.VMEM((2, GROUP_ROWS, 128), f32),
             pltpu.VMEM((4, 2 * SLOTS, TOKENS), bf16),
+            pltpu.VMEM((2 * 16, TOKENS), f32),
             pltpu.VMEM((2, GROUP_ROWS, D), bf16),
-            pltpu.VMEM((2, GROUP_ROWS, WIDE), bf16),
+            pltpu.VMEM((2, GROUP_ROWS, D), bf16),
             pltpu.VMEM((4, TOKENS, 3 * F), bf16),
             pltpu.SemaphoreType.DMA((56,)),
-            pltpu.SemaphoreType.DMA((50,)),
-            pltpu.SemaphoreType.DMA((50,)),
+            pltpu.SemaphoreType.DMA((80,)),
+            pltpu.SemaphoreType.DMA((80,)),
         ],
         compiler_params=pltpu.CompilerParams(
             collective_id=4, has_side_effects=True, vmem_limit_bytes=63 * 1024 * 1024
         ),
         cost_estimate=pl.CostEstimate(flops=32 * 10**9, bytes_accessed=40 << 20, transcendentals=1 << 21),
         name="moe",
-    )(x, g_all, masks, router_t, up, down)
+    )(x, cot, side, g_all, masks, gates, up, down)
 
 
 def on_device(
@@ -1364,41 +1452,36 @@
 ):
     x = tokens.reshape(TOKENS, D)
     cot = cotangent.reshape(TOKENS, D)
-    route_ids = routes.reshape(TOKENS, TOPK)
+    route_ids = routes.reshape(TOKENS, TOPK).T
     whole, masks, side = gather_weights(
         qkv_weight, out_weight, router_weight, attn_gain.reshape(1, 8), ffn_gain.reshape(1, 8),
         qk_gain.reshape(1, 1), route_ids, cot,
     )
     whole = whole.reshape(2, D, WCOLS)
 
-    positions = lax.axis_index("seq") * TOKENS + jnp.arange(TOKENS, dtype=jnp.int32)
-    half_dim = HEAD_SIZE // 2
-    freq_index = jnp.arange(half_dim, dtype=f32)
-    inverse = jnp.exp(-(2.0 * freq_index / HEAD_SIZE) * math.log(rope_base))
-    angles = positions.astype(f32)[:, None] * inverse[None, :]
-    cos, sin = jnp.cos(angles), jnp.sin(angles)
-    cos = jnp.concatenate([cos, cos, cos, cos], axis=1)
-    sin = jnp.concatenate([-sin, sin, -sin, sin], axis=1)
-
-    heads, g_all, full, logs, attended, after, normed_ffn, gates, small_t, raw = front(
-        x, whole, route_ids, cos, sin, cot, side
+    near, far_place = rotary_tables()
+    heads, g_all, full, logs, attended, after, normed_ffn, gates, small_t, raw, gates_t = front(
+        x, whole, route_ids, near, far_place, cot, side
     )
     row_sum, gate_sum, y_own, y_other, expert_grads, far = moe(
-        normed_ffn, g_all, masks, small_t, gate_up_weight, down_weight
+        normed_ffn, cot, side, g_all, masks, gates_t, gate_up_weight, down_weight
     )
     layer_out, token_grad, qkv_part, out_part, small, up_part, down_part = back(
-        gate_sum, gates, after, x, cot, attended, normed_ffn, small_t, heads, full, logs, cos, sin,
+        gate_sum, gates, after, x, cot, attended, normed_ffn, small_t, heads, full, logs, near, far_place,
         row_sum, raw, whole, y_own, y_other, expert_grads, far,
+    )
+    layer_out, token_grad, up_part, down_part, qkv_part, out_part, router_part, attn_part, ffn_part, head_part = finish(
+        layer_out, token_grad, up_part, down_part, qkv_part, out_part, small
     )
     return (
         layer_out.reshape(1, TOKENS, D),
         token_grad.reshape(1, TOKENS, D),
-        small[:, EXPERTS],
+        attn_part.reshape(8),
         qkv_part,
-        small[0:1, EXPERTS + 2],
+        head_part.reshape(1),
         out_part,
-        small[:, EXPERTS + 1],
-        small[:, :EXPERTS],
+        ffn_part.reshape(8),
+        router_part,
         up_part,
         down_part,
     )

time: 344 us -> 313 us (0.910)
  local copies, waits for them, and re-layouts: 15.7 us -> 0 us
  Pallas kernels: 318 us -> 306 us
    unnamed x10 -> x0, local copies, waits for them, and re-layouts: 12.9 us -> none
    pallas_call x1, Pallas kernels: 116 us -> 104 us  [back(): pl.pallas_call(back_kernel, in_specs=[vmem] * 13 + [hbm] * 7, out_specs=[...]
    pallas_call x1 -> x2, Pallas kernels: 113 us -> 113 us  [the longest x1 109 us: moe(): pl.pallas_call(moe_kernel, in_specs=[any_space] * 4 + [vmem, vmem, any_sp...]
where the time goes in v5:
time: 313 us; the launch traced here: 308 us
  Pallas kernels  306 us (98%)
    pallas_call x1, Pallas kernels, moe(): pl.pallas_call(moe_kernel, in_specs=[any_space] * 4 + [vmem, vmem, any_sp...  109 us
    pallas_call x1, Pallas kernels, back(): pl.pallas_call(back_kernel, in_specs=[vmem] * 13 + [hbm] * 7, out_specs=[...  104 us
    pallas_call x1, Pallas kernels, front(): pl.pallas_call(front_kernel, in_specs=[vmem, hbm, vmem, vmem, vmem, hbm,...  46.6 us
    pallas_call x1, Pallas kernels, gather_weights(): pl.pallas_call(gather_kernel, in_specs=[pl.BlockSpec(memory_space=pltpu.V...  42.7 us

profile of v5, /device:TPU:1, one launch (start us, length us, event | category | flops | bytes accessed | tf_op | source)
XLA Modules:
  0.0 307.7 jit_solution(9832742932426825699)
XLA Ops:
  1.3 42.7 %gather_weights.1 = (bf16[2,8,8,16,1664]{4,3,2,1,0:T(8,128)(2,1)}, bf16[16,32,256]{2,1,0:T(8,128)(2,1)}, bf16[256,1024]{1,0:T(8,128)(2,1)}) custom-call(bf16[8,2048]{1,0:T(8,128)(2,1)} %qkv_ref.1, bf16[8,1024]{1,0:T(8,128)(2,1)} %wo_ref.1, bf16[8,32]{1,0:T(8,128)(2,1)} %router_ref.1, bf16[1,8]{1,0:T(2,128)(2,1)} %bitcast.21, bf16[1,8]{1,0:T(2,128)(2,1)} %bitcast.22, ...), custom_call_target="tpu_custom_call" | custom-call | tf_op jit(solution)/shard_map/gather_weights/pallas_call | solution.py:1066
  44.0 46.6 %front.1 = (bf16[8,256,256]{2,1,0:T(8,128)(2,1)}, bf16[16,256,1024]{2,1,0:T(8,128)(2,1)}, f32[2048,128]{1,0:T(8,128)}, f32[2048,128]{1,0:T(8,128)}, bf16[256,102...) custom-call(bf16[256,1024]{1,0:T(8,128)(2,1)} %bitcast.26, ...), custom_call_target="tpu_custom_call" | custom-call | flops 4000000000 | bytes 16777216 | tf_op jit(solution)/shard_map/front/pallas_call | solution.py:342
  90.6 108.9 %moe.1 = (f32[256,1024]{1,0:T(8,128)}, f32[256,128]{1,0:T(8,128)}, bf16[8,256,1024]{2,1,0:T(8,128)(2,1)}, bf16[8,256,1024]{2,1,0:T(8,128)(2,1)}, bf16[2,1024,153...) custom-call(bf16[256,1024]{1,0:T(8,128)(2,1)} %get-tuple-element.49.x_ref.normed_ref, bf16[256,1024]{1,0:T(8,128)(2,1)} %bitcast.17, ...), custom_call_target="tpu_custom_call" | custom-call | flops 32000000000 | bytes 41943040 | tf_op jit(solution)/shard_map/moe/pallas_call | solution.py:1403
  199.5 104.1 %back.1 = (bf16[256,1024]{1,0:T(8,128)(2,1)}, f32[256,1024]{1,0:T(8,128)}, f32[8,2048]{1,0:T(8,128)}, f32[8,1024]{1,0:T(8,128)}, f32[8,128]{1,0:T(8,128)}, /*ind...) custom-call(f32[256,128]{1,0:T(8,128)} %get-tuple-element.53.gate_sum_ref, f32[256,128]{1,0:T(8,128)} %get-tuple-element.54.gates_ref, ...), custom_call_target="tpu_custom_call" | custom-call | flops 8999999488 | bytes 33554432 | tf_op jit(solution)/shard_map/back/pallas_call | solution.py:860
  303.6 3.6 %finish.1 = (bf16[256,1024]{1,0:T(8,128)(2,1)}, f32[256,1024]{1,0:T(8,128)}, f32[2,128,1024]{2,1,0:T(8,128)}, f32[2,128,512]{2,1,0:T(8,128)}, f32[8,2048]{1,0:T(...) custom-call(bf16[256,1024]{1,0:T(8,128)(2,1)} %get-tuple-element.67.layer, ...), custom_call_target="tpu_custom_call" | custom-call | tf_op jit(solution)/shard_map/finish/pallas_call | solution.py:931

commit v6 on v5

--- a/solution.py
+++ b/solution.py
@@ -431,7 +431,7 @@
         )
         for i, ring in enumerate((-1, 1, 0)) for pair in range(2)
     ]
-    e_loads.append(pltpu.make_async_copy(far_ref, far_in, local_sems.at[18]))
+    e_loads.append(pltpu.make_async_copy(far_ref, far_in.at[1], local_sems.at[18]))
     order = (6, 7, 3, 5, 2, 4, 1, 0)
     y_loads = {k: pltpu.make_async_copy(y_ref.at[k], slots.at[k], local_sems.at[4 + k]) for k in order}
     y_more = {
@@ -448,6 +448,11 @@
     net = Copies(send_sems, recv_sems)
     for copy in e_loads:
         copy.start()
+    rows = pl.ds(pl.multiple_of(here.seq_at(2, 0) * 128, 128), 128)
+    ring = here.plane("seq")
+    far_sent = [
+        net.start(grads_ref.at[e, rows], far_in.at[0, e], ring[to]) for e, to in enumerate(("up", "down"))
+    ]
     lanes, low_half = lane_halves()
 
     gate_grad = gate_sum_ref[...]
@@ -550,10 +555,12 @@
         ).astype(bf16)
 
     def expert_grads():
-        ring = here.plane("seq")
         for copy in e_loads:
             copy.wait()
         for pair in (1, 0):
+            if pair == 0:
+                for copy in far_sent:
+                    copy.wait_recv()
             add_to(chunks.at[0, pair, 1], far_in.at[pair, 1])
             add_to(chunks.at[1, pair, 0], far_in.at[pair, 0])
         beside = [
@@ -699,6 +706,21 @@
         part = slice(128 * h, 128 * (h + 1))
         pg[0, :, part], terms = unturned(back_q[:, part].astype(f32), dk_total[TOKENS * h : TOKENS * (h + 1), :], query_gain)
         query_terms = query_terms + terms
+    core = here.core
+    f = here.z * 2 + here.xh
+    sib_joins = [out_join]
+
+    def weight_part(i):
+        columns = pl.ds(512 * i, 512)
+        for r in range(4):
+            result = t_dot(normed[:, 256 * r : 256 * (r + 1)], pg[i]).astype(bf16).reshape(2, 8, 16, 1024)
+            for h in range(2):
+                parts[h, 2 * r : 2 * r + 2, :, :, 512 * i : 512 * (i + 1)] = result[:, :, :, 512 * h : 512 * (h + 1)]
+        sib_joins.append(
+            net.start(parts.at[1 - core, :, :, :, columns], parts_in.at[:, :, :, columns], sib)
+        )
+
+    weight_part(0)
     for copy in to_tokens:
         copy.wait_recv()
     key_terms = jnp.zeros((1, 128), f32)
@@ -711,27 +733,13 @@
         key_terms = key_terms + terms
         pg[1, :, 512 + 128 * j : 640 + 128 * j] = values.astype(bf16)
 
-    core = here.core
-    f = here.z * 2 + here.xh
-    sib_joins = []
-    for turn in range(2):
-        h = 1 - core if turn == 0 else core
-        for r in range(4):
-            result = t_dot(normed[:, 256 * r : 256 * (r + 1)], pg[h]).astype(bf16)
-            parts[h, 2 * r : 2 * r + 2, :, :, 0:1024] = result.reshape(2, 8, 16, 1024)
-            if turn == 0:
-                sib_joins.append(
-                    net.start(
-                        parts.at[h, pl.ds(2 * r, 2), :, :, pl.ds(0, 1024)],
-                        parts_in.at[pl.ds(2 * r, 2), :, :, pl.ds(0, 1024)],
-                        sib,
-                    )
-                )
-    out_join.wait_recv()
-    for r in range(4):
-        sib_joins[r].wait_recv()
-        for q in (2 * r, 2 * r + 1):
-            parts[core, q] = (parts[core, q].astype(f32) + parts_in[q].astype(f32)).astype(bf16)
+    weight_part(1)
+    for copy, columns in zip(sib_joins, (slice(1024, 1536), slice(0, 512), slice(512, 1024))):
+        copy.wait_recv()
+        for q in range(8):
+            parts[core, q, :, :, columns] = (
+                parts[core, q, :, :, columns].astype(f32) + parts_in[q, :, :, columns].astype(f32)
+            ).astype(bf16)
 
     def f_at(ring, pair):
         return lax.rem(here.z + ring + 4, 4) * 2 + (1 - here.xh if pair else here.xh)
@@ -740,29 +748,26 @@
         def half(ref, which):
             return ref.at[pl.ds(4 * which, 4)]
 
-        a = net.start(part(2, 1), hop.at[0], way["across"])
-        xd = net.start(part(-1, 1), hop.at[2], way["down"])
-        xu = net.start(part(1, 1), hop.at[3], way["up"])
+        up = [net.start(half(part(2, j), 0), half(hop.at[j], 0), way["up"]) for j in (1, 0)]
+        down = [net.start(half(part(2, j), 1), half(hop.at[j], 1), way["down"]) for j in (1, 0)]
         yield
-        a.wait_recv()
-        add_to(part(2, 0), hop.at[0])
-        u = net.start(half(part(2, 0), 0), half(hop.at[1], 0), way["up"])
-        d = net.start(half(part(2, 0), 1), half(hop.at[1], 1), way["down"])
+        on = []
+        for i, j in enumerate((1, 0)):
+            up[i].wait_recv()
+            add_to(half(part(1, j), 0), half(hop.at[j], 0))
+            on.append(net.start(part(1, j), hop.at[2 + 2 * i], way["up"]))
+            down[i].wait_recv()
+            add_to(half(part(-1, j), 1), half(hop.at[j], 1))
+            on.append(net.start(part(-1, j), hop.at[3 + 2 * i], way["down"]))
         yield
-        xd.wait_recv()
-        xu.wait_recv()
+        on[0].wait_recv()
+        on[1].wait_recv()
         add_to(part(0, 1), hop.at[2], hop.at[3])
-        rx = net.start(part(0, 1), hop.at[6], way["across"])
-        u.wait_recv()
-        add_to(half(part(1, 0), 0), half(hop.at[1], 0))
-        ru = net.start(part(1, 0), hop.at[4], way["up"])
-        d.wait_recv()
-        add_to(half(part(-1, 0), 1), half(hop.at[1], 1))
-        rd = net.start(part(-1, 0), hop.at[5], way["down"])
+        across = net.start(part(0, 1), hop.at[6], way["across"])
         yield
-        rx.wait_recv()
-        ru.wait_recv()
-        rd.wait_recv()
+        on[2].wait_recv()
+        on[3].wait_recv()
+        across.wait_recv()
         add_to(part(0, 0), hop.at[4], hop.at[5], hop.at[6])
 
     low, high = pl.ds(0, GCOLS // 2), pl.ds(GCOLS // 2, GCOLS // 2)
@@ -845,8 +850,9 @@
     theirs = total_in[...]
     is_low = core == 0
     left, right = jnp.where(is_low, mine, theirs), jnp.where(is_low, theirs, mine)
-    qkv_out[:, 0:1024] = left[:, 0:1024]
-    qkv_out[:, 1024:2048] = right[:, 0:1024]
+    for i in range(2):
+        qkv_out[:, 1024 * i : 1024 * i + 512] = left[:, 512 * i : 512 * (i + 1)]
+        qkv_out[:, 1024 * i + 512 : 1024 * (i + 1)] = right[:, 512 * i : 512 * (i + 1)]
     wo_out[:, 0:512] = left[:, 1024:1536]
     wo_out[:, 512:1024] = right[:, 1024:1536]
     for i in range(1, 8):
@@ -1114,7 +1120,8 @@
         xh = 1 - here.xh if pair else here.xh
         return z * 4 + xh * 2 + (1 - here.core if c else here.core)
 
-    groups = ((4, 5, 8, 9), (0, 1, 2, 3), (6, 7, 10, 11), (12, 13, 14, 15))
+    groups = ((0, 1), (4, 5, 8, 9), (6, 7, 10, 11), (12, 13, 14, 15), (2, 3))
+    starts = [SLOTS * sum(len(g) for g in groups[:i]) for i in range(5)]
 
     def fetch_g(group):
         near = {0: cot_ref, 2: side_ref}
@@ -1159,16 +1166,6 @@
     second = lax.rem(lax.broadcasted_iota(jnp.int32, (2 * 16, 1), 0), 2).astype(f32)
     named = ranks[...]
     ranks[...] = jnp.where(named > 0.0, dot(named.astype(bf16), before) + SLOTS * second, -1000.0)
-    up.wait_recv()
-    far_low = push(4, 12, way["up"], 0, 128)
-    kin[5] = push(4, 5, sib)
-    down.wait_recv()
-    far_high = push(8, 12, way["down"], 128, 128)
-    kin[9] = push(8, 9, sib)
-    across.wait_recv()
-    up_x = push(2, 6, way["up"])
-    down_x = push(2, 10, way["down"])
-    kin[3] = push(2, 3, sib)
     state = {}
 
     lanes = lax.broadcasted_iota(jnp.int32, (1, 128), 1)
@@ -1178,8 +1175,7 @@
     expert = lax.broadcasted_iota(jnp.int32, (EXPERTS, TOKENS), 0)
 
     def gather(group):
-        for s in range(4):
-            k = groups[group][s]
+        for s, k in enumerate(groups[group]):
             if k in kin:
                 kin[k].wait_recv()
             g_copies[s].wait()
@@ -1195,14 +1191,15 @@
             grads = grads.astype(bf16)
             for i in range(2):
                 part = slice(SLOTS * i, SLOTS * (i + 1))
-                there = slice(group * GROUP_ROWS + SLOTS * s, group * GROUP_ROWS + SLOTS * (s + 1))
+                there = slice(starts[group] + SLOTS * s, starts[group] + SLOTS * (s + 1))
                 rows_x[i, there, :] = picked[part]
                 rows_p[i, there, :] = pair[part]
                 rows_g[i, SLOTS * s : SLOTS * (s + 1), :] = grads[part]
                 slot_gate[i, SLOTS * s : SLOTS * (s + 1), :] = jnp.broadcast_to(gate[part], (SLOTS, 128))
 
     def run(group):
-        here_rows = pl.ds(group * GROUP_ROWS, GROUP_ROWS)
+        count = SLOTS * len(groups[group])
+        here_rows = pl.ds(starts[group], count)
 
         def one(e, carry):
             x_rows = rows_x[e, here_rows, :]
@@ -1217,12 +1214,12 @@
             rows_u[e, here_rows, 0:F] = (hidden_grad * up_part * slope).astype(bf16)
             rows_u[e, here_rows, F : 2 * F] = (hidden_grad * silu).astype(bf16)
             out = dot_t(hidden, down_ref[e]).astype(bf16).astype(f32)
-            gate_grad = jnp.sum(out * rows_g[e].astype(f32), axis=1, keepdims=True)
-            stage_y[e] = (out * slot_gate[e][:, 0:1]).astype(bf16)
-            stage_r[e] = dot_t(rows_u[e, here_rows, :], up_ref[e]).astype(bf16)
-            for s in range(4):
+            gate_grad = jnp.sum(out * rows_g[e, 0:count, :].astype(f32), axis=1, keepdims=True)
+            stage_y[e, 0:count, :] = (out * slot_gate[e, 0:count, 0:1]).astype(bf16)
+            stage_r[e, 0:count, :] = dot_t(rows_u[e, here_rows, :], up_ref[e]).astype(bf16)
+            for s, k in enumerate(groups[group]):
                 hot = places[s, pl.ds(pl.multiple_of(SLOTS * e, SLOTS), SLOTS), :].astype(f32)
-                grads_stage[groups[group][s], e, 0:1, :] = jnp.sum(
+                grads_stage[k, e, 0:1, :] = jnp.sum(
                     hot * gate_grad[SLOTS * s : SLOTS * (s + 1)], axis=0, keepdims=True
                 )
             return carry
@@ -1247,36 +1244,34 @@
                 copy.wait()
 
     def combine(group):
-        free_stage()
-        for s in range(4):
+        order = (2, 3, 0, 1) if group == 3 else range(len(groups[group]))
+        for s in order:
             k = groups[group][s]
             if k not in (4, 8):
                 for copy in sent[k]:
                     copy.wait_send()
             part = slice(SLOTS * s, SLOTS * (s + 1))
+            both = jnp.concatenate([stage_r[0, part, :], stage_r[1, part, :]], axis=0)
+            result(k)[...] = t_dot(places[s], both).astype(bf16)
+            if k % 2:
+                state[k - 1] = net.start(slots.at[k], sib_in.at[k // 2], sib)
+        free_stage()
+        state["y"] = []
+        for s, k in enumerate(groups[group]):
+            part = slice(SLOTS * s, SLOTS * (s + 1))
             both = jnp.concatenate([stage_y[0, part, :], stage_y[1, part, :]], axis=0)
             stage[s, :, 0:D] = t_dot(places[s], both).astype(bf16)
-            both = jnp.concatenate([stage_r[0, part, :], stage_r[1, part, :]], axis=0)
-            result(k)[...] = t_dot(places[s], both).astype(bf16)
-        state["y"] = []
-        for s in range(4):
-            k = groups[group][s]
             ready = stage.at[s, :, pl.ds(0, D)]
             if k % 2:
                 y_sent.append(net.start(ready, y_in.at[k // 2], sib))
                 state["y"].append((y_sent[-1], True))
             else:
                 state["y"].append((local(ready, y_out.at[k // 2]), False))
-        for k in groups[group][::2]:
-            state[k] = net.start(slots.at[k + 1], sib_in.at[k // 2], sib)
 
     def join(k):
         state[k].wait_recv()
         there = result(k)
         there[...] = (there[...].astype(f32) + sib_in[k // 2].astype(f32)).astype(bf16)
-
-    def half(ref, which):
-        return ref.at[pl.ds(128 * which, 128)]
 
     first_x.wait()
     for copy in small:
@@ -1287,38 +1282,61 @@
     for copy in weights:
         copy.wait()
     run(0)
+    up.wait_recv()
+    far_low = push(4, 12, way["up"], 0, 128)
+    kin[5] = push(4, 5, sib)
+    down.wait_recv()
+    far_high = push(8, 12, way["down"], 128, 128)
+    kin[9] = push(8, 9, sib)
+    across.wait_recv()
+    up_x = push(2, 6, way["up"])
+    down_x = push(2, 10, way["down"])
+    kin[3] = push(2, 3, sib)
     combine(0)
+    gather(1)
+    g_copies = fetch_g(2)
+    run(1)
+    combine(1)
     far_low.wait_recv()
     far_high.wait_recv()
     far_x = push(12, 14, way["across"])
     kin[13] = push(12, 13, sib)
-    gather(1)
-    g_copies = fetch_g(2)
+    up_x.wait_recv()
+    kin[7] = push(6, 7, sib)
+    down_x.wait_recv()
+    kin[11] = push(10, 11, sib)
+    gather(2)
+    g_copies = fetch_g(3)
     join(4)
     hop_rd = net.start(result(4), hop_in.at[5], way["down"])
     join(8)
     hop_ru = net.start(result(8), hop_in.at[4], way["up"])
-    run(1)
-    up_x.wait_recv()
-    kin[7] = push(6, 7, sib)
-    down_x.wait_recv()
-    kin[11] = push(10, 11, sib)
-    combine(1)
-    gather(2)
-    g_copies = fetch_g(3)
     run(2)
     far_x.wait_recv()
     kin[15] = push(14, 15, sib)
     combine(2)
     gather(3)
+    g_copies = fetch_g(4)
     join(6)
     hop_xd = net.start(slots.at[6], hop_in.at[2], way["down"])
     join(10)
     hop_xu = net.start(slots.at[10], hop_in.at[3], way["up"])
-    join(2)
-    join(0)
     run(3)
     combine(3)
+    gather(4)
+    join(14)
+
+    def quarter(ref, i):
+        return ref.at[pl.ds((0, 128, 64, 192)[i], 64)]
+
+    ways = ("up", "down", "up", "down")
+    hop_a = [
+        net.start(quarter(slots.at[14], i), quarter(hop_in.at[0], i), way["across"]) for i in range(4)
+    ]
+    join(12)
+    join(0)
+    run(4)
+    combine(4)
 
     w_copies = []
 
@@ -1330,7 +1348,7 @@
         w_copies.clear()
         rows = pl.ds(pl.multiple_of(here.seq_at(2, dx) * 128, 128), 128)
         for e, to in enumerate(("up", "down")):
-            far_grads.append(net.start(grads_out.at[e, rows], far_out.at[dx, e], ring[to]))
+            far_grads.append(net.start(grads_out.at[e, rows], far_out.at[e], ring[to]))
 
     def weight_grad(e, dx):
         free_stage()
@@ -1353,28 +1371,27 @@
         ]
 
     weight_grad(0, 1)
-    join(14)
-    hop_a = [net.start(half(slots.at[14], i), half(hop_in.at[0], i), way["across"]) for i in range(2)]
-    join(12)
-    weight_grad(1, 1)
-    send_far(1)
-    far = []
-    for i, to in enumerate(("up", "down")):
-        hop_a[i].wait_recv()
-        ref, other = half(slots.at[12], i), half(hop_in.at[0], i)
-        ref[...] = (ref[...].astype(f32) + other[...].astype(f32)).astype(bf16)
-        far.append(net.start(ref, half(hop_in.at[1], i), way[to]))
-    weight_grad(0, 0)
+    join(2)
     hop_xd.wait_recv()
     hop_xu.wait_recv()
     slots[2] = (slots[2].astype(f32) + hop_in[2].astype(f32) + hop_in[3].astype(f32)).astype(bf16)
     hop_rx = net.start(slots.at[2], hop_in.at[6], way["across"])
+    far = []
+    for i in range(4):
+        hop_a[i].wait_recv()
+        ref, other = quarter(slots.at[12], i), quarter(hop_in.at[0], i)
+        ref[...] = (ref[...].astype(f32) + other[...].astype(f32)).astype(bf16)
+        far.append(net.start(ref, quarter(hop_in.at[1], i), way[ways[i]]))
+    weight_grad(1, 1)
+    send_far(1)
     relay = []
-    for i, to in enumerate(("up", "down")):
+    for i in range(4):
         far[i].wait_recv()
-        relay.append(net.start(half(hop_in.at[1], i), half(hop_in.at[7], i), way[to]))
+        relay.append(net.start(quarter(hop_in.at[1], i), quarter(hop_in.at[7], i), way[ways[i]]))
+    weight_grad(0, 0)
     weight_grad(1, 0)
-    send_far(0)
+    for copy in w_copies:
+        copy.wait()
     for copy in (hop_ru, hop_rd, hop_rx, *relay, *far_grads, *y_sent, *small):
         copy.wait_recv()
     total = (
@@ -1410,7 +1427,7 @@
             jax.ShapeDtypeStruct((8, TOKENS, D), bf16),
             jax.ShapeDtypeStruct((8, TOKENS, D), bf16),
             jax.ShapeDtypeStruct((2, D, 3 * F), bf16),
-            jax.ShapeDtypeStruct((2, 2, 128, 3 * F), bf16),
+            jax.ShapeDtypeStruct((2, 128, 3 * F), bf16),
         ],
         scratch_shapes=[
             pltpu.VMEM((16, TOKENS, D), bf16),
@@ -1435,8 +1452,8 @@
             pltpu.VMEM((2, GROUP_ROWS, D), bf16),
             pltpu.VMEM((4, TOKENS, 3 * F), bf16),
             pltpu.SemaphoreType.DMA((56,)),
-            pltpu.SemaphoreType.DMA((80,)),
-            pltpu.SemaphoreType.DMA((80,)),
+            pltpu.SemaphoreType.DMA((96,)),
+            pltpu.SemaphoreType.DMA((96,)),
         ],
         compiler_params=pltpu.CompilerParams(
             collective_id=4, has_side_effects=True, vmem_limit_bytes=63 * 1024 * 1024

time: 313 us -> 295 us (0.942)
  Pallas kernels: 306 us -> 288 us
    pallas_call x1, Pallas kernels: 109 us -> 91.9 us  [moe(): pl.pallas_call(moe_kernel, in_specs=[any_space] * 4 + [vmem, vmem, any_sp...]
where the time goes in v6:
time: 295 us; the launch traced here: 290 us
  Pallas kernels  288 us (98%)
    pallas_call x1, Pallas kernels, back(): pl.pallas_call(back_kernel, in_specs=[vmem] * 13 + [hbm] * 7, out_specs=[...  103 us
    pallas_call x1, Pallas kernels, moe(): pl.pallas_call(moe_kernel, in_specs=[any_space] * 4 + [vmem, vmem, any_sp...  91.9 us
    pallas_call x1, Pallas kernels, front(): pl.pallas_call(front_kernel, in_specs=[vmem, hbm, vmem, vmem, vmem, hbm,...  46.7 us
    pallas_call x1, Pallas kernels, gather_weights(): pl.pallas_call(gather_kernel, in_specs=[pl.BlockSpec(memory_space=pltpu.V...  42.7 us

profile of v6, /device:TPU:1, one launch (start us, length us, event | category | flops | bytes accessed | tf_op | source)
XLA Modules:
  0.0 290.1 jit_solution(1134594318551938651)
XLA Ops:
  1.3 42.7 %gather_weights.1 = (bf16[2,8,8,16,1664]{4,3,2,1,0:T(8,128)(2,1)}, bf16[16,32,256]{2,1,0:T(8,128)(2,1)}, bf16[256,1024]{1,0:T(8,128)(2,1)}) custom-call(bf16[8,2048]{1,0:T(8,128)(2,1)} %qkv_ref.1, bf16[8,1024]{1,0:T(8,128)(2,1)} %wo_ref.1, bf16[8,32]{1,0:T(8,128)(2,1)} %router_ref.1, bf16[1,8]{1,0:T(2,128)(2,1)} %bitcast.21, bf16[1,8]{1,0:T(2,128)(2,1)} %bitcast.22, ...), custom_call_target="tpu_custom_call" | custom-call | tf_op jit(solution)/shard_map/gather_weights/pallas_call | solution.py:1072
  44.0 46.7 %front.1 = (bf16[8,256,256]{2,1,0:T(8,128)(2,1)}, bf16[16,256,1024]{2,1,0:T(8,128)(2,1)}, f32[2048,128]{1,0:T(8,128)}, f32[2048,128]{1,0:T(8,128)}, bf16[256,102...) custom-call(bf16[256,1024]{1,0:T(8,128)(2,1)} %bitcast.26, ...), custom_call_target="tpu_custom_call" | custom-call | flops 4000000000 | bytes 16777216 | tf_op jit(solution)/shard_map/front/pallas_call | solution.py:342
  90.7 91.9 %moe.1 = (f32[256,1024]{1,0:T(8,128)}, f32[256,128]{1,0:T(8,128)}, bf16[8,256,1024]{2,1,0:T(8,128)(2,1)}, bf16[8,256,1024]{2,1,0:T(8,128)(2,1)}, bf16[2,1024,153...) custom-call(bf16[256,1024]{1,0:T(8,128)(2,1)} %get-tuple-element.49.x_ref.normed_ref, bf16[256,1024]{1,0:T(8,128)(2,1)} %bitcast.17, ...), custom_call_target="tpu_custom_call" | custom-call | flops 32000000000 | bytes 41943040 | tf_op jit(solution)/shard_map/moe/pallas_call | solution.py:1420
  182.5 103.4 %back.1 = (bf16[256,1024]{1,0:T(8,128)(2,1)}, f32[256,1024]{1,0:T(8,128)}, f32[8,2048]{1,0:T(8,128)}, f32[8,1024]{1,0:T(8,128)}, f32[8,128]{1,0:T(8,128)}, /*ind...) custom-call(f32[256,128]{1,0:T(8,128)} %get-tuple-element.53.gate_sum_ref, f32[256,128]{1,0:T(8,128)} %get-tuple-element.54.gates_ref, ...), custom_call_target="tpu_custom_call" | custom-call | flops 8999999488 | bytes 33554432 | tf_op jit(solution)/shard_map/back/pallas_call | solution.py:866
  285.9 3.6 %finish.1 = (bf16[256,1024]{1,0:T(8,128)(2,1)}, f32[256,1024]{1,0:T(8,128)}, f32[2,128,1024]{2,1,0:T(8,128)}, f32[2,128,512]{2,1,0:T(8,128)}, f32[8,2048]{1,0:T(...) custom-call(bf16[256,1024]{1,0:T(8,128)(2,1)} %get-tuple-element.67.layer, ...), custom_call_target="tpu_custom_call" | custom-call | tf_op jit(solution)/shard_map/finish/pallas_call | solution.py:937

commit v7 on v6

--- a/solution.py
+++ b/solution.py
@@ -403,7 +403,7 @@
     wqkv, wo, send, grads, back_q, back_kv, pg, after_grad,
     key0, key1, value0, value1, key_t, dk_total, dv_total,
     slots, y_stage, hop_in,
-    parts, parts_in, small, small_in, hop_a, hop_b, late_a, late_b, small_s, small_f, total, total_in,
+    parts, parts_in, small, small_in, hops, late, small_s, small_f, total, total_in,
     chunks, far_in, chunk_in, local_sems, send_sems, recv_sems,
 ):
     here = Place()
@@ -481,8 +481,8 @@
     def delivery(d):
         peer = lax.rem(me + d, 8)
         return pltpu.make_async_remote_copy(
-            src_ref=send.at[peer], dst_ref=grads.at[me], send_sem=send_sems.at[92 + d],
-            recv_sem=recv_sems.at[92 + d], device_id={"seq": peer}, device_id_type=MESH,
+            src_ref=send.at[peer], dst_ref=grads.at[me], send_sem=send_sems.at[104 + d],
+            recv_sem=recv_sems.at[104 + d], device_id={"seq": peer}, device_id_type=MESH,
         )
 
     for d in range(7, 0, -1):
@@ -606,8 +606,8 @@
     def answer(i):
         j = lax.rem(me + i, 8)
         return pltpu.make_async_remote_copy(
-            src_ref=grads.at[j], dst_ref=back_q.at[:, columns], send_sem=send_sems.at[84 + i],
-            recv_sem=recv_sems.at[84 + i], device_id={"seq": j}, device_id_type=MESH,
+            src_ref=grads.at[j], dst_ref=back_q.at[:, columns], send_sem=send_sems.at[96 + i],
+            recv_sem=recv_sems.at[96 + i], device_id={"seq": j}, device_id_type=MESH,
         )
 
     def block(i, carry):
@@ -657,8 +657,9 @@
 
         return carry
 
-    lax.fori_loop(0, 3, block, 0)
+    lax.fori_loop(0, 2, block, 0)
     next(more_moves)
+    lax.fori_loop(2, 3, block, 0)
     next(moves)
     lax.fori_loop(3, 6, block, 0)
     next(moves)
@@ -700,46 +701,8 @@
 
     for copy in raw:
         copy.wait()
-    next(more_moves)
-    query_terms = jnp.zeros((1, 128), f32)
-    for h in range(8):
-        part = slice(128 * h, 128 * (h + 1))
-        pg[0, :, part], terms = unturned(back_q[:, part].astype(f32), dk_total[TOKENS * h : TOKENS * (h + 1), :], query_gain)
-        query_terms = query_terms + terms
     core = here.core
     f = here.z * 2 + here.xh
-    sib_joins = [out_join]
-
-    def weight_part(i):
-        columns = pl.ds(512 * i, 512)
-        for r in range(4):
-            result = t_dot(normed[:, 256 * r : 256 * (r + 1)], pg[i]).astype(bf16).reshape(2, 8, 16, 1024)
-            for h in range(2):
-                parts[h, 2 * r : 2 * r + 2, :, :, 512 * i : 512 * (i + 1)] = result[:, :, :, 512 * h : 512 * (h + 1)]
-        sib_joins.append(
-            net.start(parts.at[1 - core, :, :, :, columns], parts_in.at[:, :, :, columns], sib)
-        )
-
-    weight_part(0)
-    for copy in to_tokens:
-        copy.wait_recv()
-    key_terms = jnp.zeros((1, 128), f32)
-    for j in range(4):
-        first, second = back_kv[2 * j].astype(f32), back_kv[2 * j + 1].astype(f32)
-        keys = jnp.where(low_half, first, pltpu.roll(second, 64, 1))
-        values = jnp.where(low_half, pltpu.roll(first, 64, 1), second)
-        part = slice(128 * j, 128 * (j + 1))
-        pg[1, :, part], terms = unturned(keys, dv_total[TOKENS * j : TOKENS * (j + 1), :], key_gain)
-        key_terms = key_terms + terms
-        pg[1, :, 512 + 128 * j : 640 + 128 * j] = values.astype(bf16)
-
-    weight_part(1)
-    for copy, columns in zip(sib_joins, (slice(1024, 1536), slice(0, 512), slice(512, 1024))):
-        copy.wait_recv()
-        for q in range(8):
-            parts[core, q, :, :, columns] = (
-                parts[core, q, :, :, columns].astype(f32) + parts_in[q, :, :, columns].astype(f32)
-            ).astype(bf16)
 
     def f_at(ring, pair):
         return lax.rem(here.z + ring + 4, 4) * 2 + (1 - here.xh if pair else here.xh)
@@ -770,13 +733,68 @@
         across.wait_recv()
         add_to(part(0, 0), hop.at[4], hop.at[5], hop.at[6])
 
-    low, high = pl.ds(0, GCOLS // 2), pl.ds(GCOLS // 2, GCOLS // 2)
-    first_plane = plane(
-        lambda ring, pair: parts.at[core, here.seq_at(ring, pair), :, :, low], hop_a, here.plane("seq")
-    )
-    second_plane = plane(lambda ring, pair: parts.at[core, :, f_at(ring, pair), :, high], hop_b, way)
-    next(first_plane)
-    next(second_plane)
+    def columns_of(group):
+        return pl.ds(512 * group, 512)
+
+    def by_seq(ring, pair):
+        return parts.at[core, here.seq_at(ring, pair), :, :, columns_of(0)]
+
+    def by_fsdp(group):
+        return lambda ring, pair: parts.at[core, :, f_at(ring, pair), :, columns_of(group)]
+
+    def joined(copy, group):
+        copy.wait_recv()
+        there = slice(512 * group, 512 * (group + 1))
+        for q in range(8):
+            parts[core, q, :, :, there] = (
+                parts[core, q, :, :, there].astype(f32) + parts_in[q, :, :, there].astype(f32)
+            ).astype(bf16)
+
+    planes = [
+        plane(by_seq, hops.at[0], here.plane("seq")),
+        plane(by_fsdp(1), hops.at[1], way),
+        plane(by_fsdp(2), hops.at[2], way),
+    ]
+    joined(out_join, 2)
+    next(planes[2])
+    next(more_moves)
+    query_terms = jnp.zeros((1, 128), f32)
+    for h in range(8):
+        part = slice(128 * h, 128 * (h + 1))
+        pg[0, :, part], terms = unturned(back_q[:, part].astype(f32), dk_total[TOKENS * h : TOKENS * (h + 1), :], query_gain)
+        query_terms = query_terms + terms
+    sib_joins = []
+
+    def weight_part(i):
+        columns = pl.ds(512 * i, 512)
+        for r in range(4):
+            result = t_dot(normed[:, 256 * r : 256 * (r + 1)], pg[i]).astype(bf16).reshape(2, 8, 16, 1024)
+            for h in range(2):
+                parts[h, 2 * r : 2 * r + 2, :, :, 512 * i : 512 * (i + 1)] = result[:, :, :, 512 * h : 512 * (h + 1)]
+        sib_joins.append(
+            net.start(parts.at[1 - core, :, :, :, columns], parts_in.at[:, :, :, columns], sib)
+        )
+
+    weight_part(0)
+    for copy in to_tokens:
+        copy.wait_recv()
+    key_terms = jnp.zeros((1, 128), f32)
+    for j in range(4):
+        first, second = back_kv[2 * j].astype(f32), back_kv[2 * j + 1].astype(f32)
+        keys = jnp.where(low_half, first, pltpu.roll(second, 64, 1))
+        values = jnp.where(low_half, pltpu.roll(first, 64, 1), second)
+        part = slice(128 * j, 128 * (j + 1))
+        pg[1, :, part], terms = unturned(keys, dv_total[TOKENS * j : TOKENS * (j + 1), :], key_gain)
+        key_terms = key_terms + terms
+        pg[1, :, 512 + 128 * j : 640 + 128 * j] = values.astype(bf16)
+
+    weight_part(1)
+    next(planes[2])
+    joined(sib_joins[0], 0)
+    next(planes[0])
+    joined(sib_joins[1], 1)
+    next(planes[1])
+    next(planes[2])
     for copy in loads[2:4]:
         copy.wait()
     normed_grad = dot_t(pg[0], wqkv[0]) + dot_t(pg[1], wqkv[1])
@@ -796,8 +814,9 @@
     )
     small[...] = small[...] + jnp.transpose(gain_rows).reshape(8, 8, 2, 8, 128)
     small_join = net.start(small.at[:, :, 1 - core], small_in, sib)
-    next(first_plane)
-    next(second_plane)
+    next(planes[0])
+    next(planes[1])
+    next(planes[2], None)
     weighted = normed_grad * attn_gain
     middle = jnp.mean(weighted * x, axis=1, keepdims=True)
     token_ref[...] = after_grad[...] + x_scaling * weighted - x * (x_scaling * x_scaling * x_scaling * middle)
@@ -806,8 +825,8 @@
     small_copies = [
         net.start(small_in.at[peers[i]], small_s.at[i], seq_peers[i]) for i in range(7)
     ]
-    next(first_plane)
-    next(second_plane)
+    next(planes[0])
+    next(planes[1])
     for _ in moves:
         pass
     for _ in more_moves:
@@ -821,28 +840,32 @@
     small_copies = [
         net.start(small_in.at[me, f_at(*OTHERS[i])], small_f.at[i], fsdp_peers[i]) for i in range(7)
     ]
-    next(first_plane, None)
-    late = [
-        [net.start(parts.at[core, me, f_at(*OTHERS[i]), :, low], late_a.at[i], fsdp_peers[i]) for i in range(7)]
-    ]
-    next(second_plane, None)
-    late.append(
-        [net.start(parts.at[core, peers[i], f, :, high], late_b.at[i], seq_peers[i]) for i in range(7)]
-    )
+    def last_exchange(group):
+        return [
+            net.start(parts.at[core, me, f_at(*OTHERS[i]), :, columns_of(0)], late.at[0, i], fsdp_peers[i])
+            if group == 0
+            else net.start(parts.at[core, peers[i], f, :, columns_of(group)], late.at[group, i], seq_peers[i])
+            for i in range(7)
+        ]
+
+    late_copies = {2: last_exchange(2)}
+    next(planes[0], None)
+    late_copies[0] = last_exchange(0)
+    next(planes[1], None)
+    late_copies[1] = last_exchange(1)
     for copy in small_copies:
         copy.wait_recv()
     mine = small_in[me, f]
     for i in range(7):
         mine = mine + small_f[i]
     small_out[...] = mine
-    for cols, copies, there in (
-        (slice(0, GCOLS // 2), late[0], late_a), (slice(GCOLS // 2, GCOLS), late[1], late_b)
-    ):
-        for copy in copies:
+    for group in (2, 0, 1):
+        for copy in late_copies[group]:
             copy.wait_recv()
+        cols = slice(512 * group, 512 * (group + 1))
         result = parts[core, me, f, :, cols].astype(f32)
         for i in range(7):
-            result = result + there[i].astype(f32)
+            result = result + late[group, i].astype(f32)
         total[:, cols] = result
     last = net.start(total.at[pl.ds(pl.multiple_of(8 * (1 - core), 8), 8)], total_in, sib)
     mine = total[pl.ds(pl.multiple_of(8 * core, 8), 8), :]
@@ -896,10 +919,8 @@
             pltpu.VMEM((8, 8, 16, GCOLS), bf16),
             pltpu.VMEM((8, 8, 2, 8, 128), f32),
             pltpu.VMEM((8, 8, 8, 128), f32),
-            pltpu.VMEM((7, 8, 16, GCOLS // 2), bf16),
-            pltpu.VMEM((7, 8, 16, GCOLS // 2), bf16),
-            pltpu.VMEM((7, 16, GCOLS // 2), bf16),
-            pltpu.VMEM((7, 16, GCOLS // 2), bf16),
+            pltpu.VMEM((3, 7, 8, 16, 512), bf16),
+            pltpu.VMEM((3, 7, 16, 512), bf16),
             pltpu.VMEM((7, 8, 8, 128), f32),
             pltpu.VMEM((7, 8, 128), f32),
             pltpu.VMEM((16, GCOLS), f32),
@@ -908,8 +929,8 @@
             pltpu.VMEM((2, 2, 128, 3 * F), bf16),
             pltpu.VMEM((5, 2, 128, 3 * F), bf16),
             pltpu.SemaphoreType.DMA((40,)),
-            pltpu.SemaphoreType.DMA((100,)),
-            pltpu.SemaphoreType.DMA((100,)),
+            pltpu.SemaphoreType.DMA((112,)),
+            pltpu.SemaphoreType.DMA((112,)),
         ],
         compiler_params=pltpu.CompilerParams(collective_id=5, has_side_effects=True, vmem_limit_bytes=63 * 1024 * 1024),
         cost_estimate=pl.CostEstimate(

time: 295 us -> 291 us (0.986)
  Pallas kernels: 288 us -> 284 us
    pallas_call x1, Pallas kernels: 103 us -> 99.6 us  [back(): pl.pallas_call(back_kernel, in_specs=[vmem] * 13 + [hbm] * 7, out_specs=[...]
where the time goes in v7:
time: 291 us; the launch traced here: 286 us
  Pallas kernels  284 us (98%)
    pallas_call x1, Pallas kernels, back(): pl.pallas_call(back_kernel, in_specs=[vmem] * 13 + [hbm] * 7, out_specs=[...  99.6 us
    pallas_call x1, Pallas kernels, moe(): pl.pallas_call(moe_kernel, in_specs=[any_space] * 4 + [vmem, vmem, any_sp...  91.9 us
    pallas_call x1, Pallas kernels, front(): pl.pallas_call(front_kernel, in_specs=[vmem, hbm, vmem, vmem, vmem, hbm,...  46.7 us
    pallas_call x1, Pallas kernels, gather_weights(): pl.pallas_call(gather_kernel, in_specs=[pl.BlockSpec(memory_space=pltpu.V...  42.7 us

profile of v7, /device:TPU:1, one launch (start us, length us, event | category | flops | bytes accessed | tf_op | source)
XLA Modules:
  0.0 286.0 jit_solution(1389214998338776458)
XLA Ops:
  1.3 42.7 %gather_weights.1 = (bf16[2,8,8,16,1664]{4,3,2,1,0:T(8,128)(2,1)}, bf16[16,32,256]{2,1,0:T(8,128)(2,1)}, bf16[256,1024]{1,0:T(8,128)(2,1)}) custom-call(bf16[8,2048]{1,0:T(8,128)(2,1)} %qkv_ref.1, bf16[8,1024]{1,0:T(8,128)(2,1)} %wo_ref.1, bf16[8,32]{1,0:T(8,128)(2,1)} %router_ref.1, bf16[1,8]{1,0:T(2,128)(2,1)} %bitcast.21, bf16[1,8]{1,0:T(2,128)(2,1)} %bitcast.22, ...), custom_call_target="tpu_custom_call" | custom-call | tf_op jit(solution)/shard_map/gather_weights/pallas_call | solution.py:1093
  44.0 46.7 %front.1 = (bf16[8,256,256]{2,1,0:T(8,128)(2,1)}, bf16[16,256,1024]{2,1,0:T(8,128)(2,1)}, f32[2048,128]{1,0:T(8,128)}, f32[2048,128]{1,0:T(8,128)}, bf16[256,102...) custom-call(bf16[256,1024]{1,0:T(8,128)(2,1)} %bitcast.26, ...), custom_call_target="tpu_custom_call" | custom-call | flops 4000000000 | bytes 16777216 | tf_op jit(solution)/shard_map/front/pallas_call | solution.py:342
  90.7 91.9 %moe.1 = (f32[256,1024]{1,0:T(8,128)}, f32[256,128]{1,0:T(8,128)}, bf16[8,256,1024]{2,1,0:T(8,128)(2,1)}, bf16[8,256,1024]{2,1,0:T(8,128)(2,1)}, bf16[2,1024,153...) custom-call(bf16[256,1024]{1,0:T(8,128)(2,1)} %get-tuple-element.49.x_ref.normed_ref, bf16[256,1024]{1,0:T(8,128)(2,1)} %bitcast.17, ...), custom_call_target="tpu_custom_call" | custom-call | flops 32000000000 | bytes 41943040 | tf_op jit(solution)/shard_map/moe/pallas_call | solution.py:1441
  182.5 99.6 %back.1 = (bf16[256,1024]{1,0:T(8,128)(2,1)}, f32[256,1024]{1,0:T(8,128)}, f32[8,2048]{1,0:T(8,128)}, f32[8,1024]{1,0:T(8,128)}, f32[8,128]{1,0:T(8,128)}, /*ind...) custom-call(f32[256,128]{1,0:T(8,128)} %get-tuple-element.53.gate_sum_ref, f32[256,128]{1,0:T(8,128)} %get-tuple-element.54.gates_ref, ...), custom_call_target="tpu_custom_call" | custom-call | flops 8999999488 | bytes 33554432 | tf_op jit(solution)/shard_map/back/pallas_call | solution.py:889
  282.1 3.6 %finish.1 = (bf16[256,1024]{1,0:T(8,128)(2,1)}, f32[256,1024]{1,0:T(8,128)}, f32[2,128,1024]{2,1,0:T(8,128)}, f32[2,128,512]{2,1,0:T(8,128)}, f32[8,2048]{1,0:T(...) custom-call(bf16[256,1024]{1,0:T(8,128)(2,1)} %get-tuple-element.67.layer, ...), custom_call_target="tpu_custom_call" | custom-call | tf_op jit(solution)/shard_map/finish/pallas_call | solution.py:958
